TPU v7x, 32 devices: a whole 2x2x4 slice. The times are simulated.
32 devices in a mesh: ctx: 4 (over y, core), ep: 8 (over z, x).
Axes of the slice: x: 2, y: 2, z: 4, core: 2. Of those that a mesh axis runs over, the one named last changes fastest.
Arguments:
- queries: bfloat16 [1024, 1, 2048], P('ctx', None, 'ep'), may hold values from -6 to 6
- keys_in: bfloat16 [1024, 1, 2048], P('ctx', None, 'ep'), may hold values from -6 to 6
- values_in: bfloat16 [1024, 1, 2048], P('ctx', None, 'ep'), may hold values from -6 to 6
- log_decay: float32 [16, 1, 1024], P('ep', None, 'ctx'), may hold values from -1.5 to 0
- attn_gain: float32 [2048], P('ep'), may hold values from 0.1 to 1.9
- out_weight: bfloat16 [2048, 6144], P('ep', 'ctx'), may hold values from -0.125 to 0.125
- residual: bfloat16 [1024, 1, 6144], P(('ctx', 'ep')), may hold values from -42 to 42
- moe_gain: float32 [6144], replicated, may hold values from 0.1 to 1.9
- router: bfloat16 [6144, 8], replicated, may hold values from -0.078125 to 0.078125
- gate_weight: bfloat16 [8, 6144, 4608], P('ep', None, 'ctx'), may hold values from -0.078125 to 0.078125
- up_weight: bfloat16 [8, 6144, 4608], P('ep', None, 'ctx'), may hold values from -0.078125 to 0.078125
- down_weight: bfloat16 [8, 4608, 6144], P('ep', 'ctx'), may hold values from -0.09375 to 0.09375
- routes: int32 [1024, 1, 2], P(('ctx', 'ep')), may hold values from 0 to 7, all different within a row; in each aligned block of 32 rows (0 to 31, 32 to 63, ..., all dimensions but the last counted through in order) at most 12 rows name the same one
Outputs:
- mixed: bfloat16 [1024, 1, 6144], P(('ctx', 'ep'))
Inputs may be any that keep to these rules, and one draw needn't show every extreme that they name: `routes`: each row names two different experts. Among the tokens of one device (aligned blocks of 32 rows of the flattened positions and sequences) no expert is named more than 12 times.
All inputs are finite; a program needn't handle non-finite values.
Results may differ from a plain program's by a relative error of at most 0.017.
Values may be sent and summed in bfloat16 or wider, within the bound.
No kernel may reach another device: no remote copies, remote signals or barrier semaphores. Data moves between devices by JAX's collectives and lax.ppermute only.
A program may use at most 128 MiB of HBM per device.

v0:
```python
import jax
import jax.numpy as jnp
from jax import lax
from jax.sharding import PartitionSpec as P

highest = lax.Precision.HIGHEST


def entering(array, axis, join, neutral):
    place = lax.axis_index(axis)
    gathered = jax.tree.map(
        lambda a, kind: lax.all_gather(a.astype(kind), axis), array, (jnp.bfloat16, jnp.bfloat16)
    )
    state = jax.tree.map(lambda a, e: jnp.zeros_like(a) + jnp.asarray(e, a.dtype), array, neutral)

    def one(hop, state):
        return join(
            state,
            jax.tree.map(
                lambda a, own: lax.dynamic_index_in_dim(a, hop, 0, False).astype(own.dtype),
                gathered,
                array,
            ),
        )

    return lax.fori_loop(0, place, one, state)


def silu_float(values):
    return values * jax.nn.sigmoid(values)


def shards(
    queries,
    keys_in,
    values_in,
    log_decay,
    attn_gain,
    out_weight,
    residual,
    moe_gain,
    router,
    gate_weight,
    up_weight,
    down_weight,
    routes,
):
    length, sequences, width = queries.shape
    head_count = log_decay.shape[0]
    head_size = width // head_count
    q_local = silu_float(queries.astype(jnp.float32)).reshape(
        length, sequences, head_count, head_size
    )
    k_local = silu_float(keys_in.astype(jnp.float32)).reshape(
        length, sequences, head_count, head_size
    )
    v_local = values_in.astype(jnp.float32).reshape(length, sequences, head_count, head_size)
    cumulative = jnp.cumsum(jnp.transpose(log_decay, (1, 0, 2)), axis=-1)
    positions = jnp.arange(length, dtype=jnp.int32)
    causal = positions[:, None] >= positions[None, :]
    spacing = cumulative[..., :, None] - cumulative[..., None, :]
    damping = jnp.where(causal, jnp.exp(jnp.where(causal, spacing, 0.0)), 0.0)
    scores = jnp.einsum("tshd,ushd->shtu", q_local, k_local, precision=highest) * damping
    inside = jnp.einsum("shtu,ushe->tshe", scores, v_local, precision=highest)
    remaining = jnp.exp(cumulative[..., -1:] - cumulative)
    own_state = jnp.einsum(
        "ushd,ushe->shde",
        k_local * jnp.transpose(remaining, (2, 0, 1))[..., None],
        v_local,
        precision=highest,
    )
    block_log = cumulative[..., -1]

    def combine(earlier, later_part):
        return (
            earlier[0] * later_part[0],
            later_part[0][..., None, None] * earlier[1] + later_part[1],
        )

    identity = (jnp.ones_like(block_log), jnp.zeros_like(own_state))
    _, prefix_state = entering((jnp.exp(block_log), own_state), "ctx", combine, identity)
    carried = jnp.exp(jnp.transpose(cumulative, (2, 0, 1)))[..., None] * jnp.einsum(
        "tshd,shde->tshe", q_local, prefix_state, precision=highest
    )
    heads_out = inside + carried
    mean_square = jnp.mean(heads_out * heads_out, axis=-1, keepdims=True)
    normed_heads = (
        heads_out * lax.rsqrt(mean_square + 1e-06) * attn_gain.reshape(head_count, head_size)
    )
    normed_heads = normed_heads.astype(jnp.bfloat16).reshape(length * sequences, width)
    partial_out = jnp.dot(
        normed_heads,
        lax.all_gather(out_weight, "ctx", axis=1, tiled=True),
        preferred_element_type=jnp.float32,
    )
    attn = lax.psum_scatter(
        partial_out.reshape(length, sequences, -1).astype(jnp.bfloat16),
        "ep",
        scatter_dimension=0,
        tiled=True,
    ).astype(jnp.float32)
    hidden_state = residual.astype(jnp.float32) + attn
    token_count = hidden_state.shape[0] * sequences
    flat_state = hidden_state.reshape(token_count, -1)
    moe_scale = lax.rsqrt(jnp.mean(flat_state * flat_state, axis=-1, keepdims=True) + 1e-06)
    moe_in = (flat_state * moe_scale * moe_gain).astype(jnp.bfloat16)
    logits = jnp.dot(moe_in, router, preferred_element_type=jnp.float32)
    expert_count = router.shape[1]
    capacity = max(2, 3 * token_count // expert_count)
    expert_ids = routes.reshape(token_count, 2)
    route_hot = expert_ids[..., None] == jnp.arange(expert_count, dtype=jnp.int32)
    picked = jnp.sum(jnp.where(route_hot, logits[:, None, :], 0.0), axis=-1)
    weight_first = jax.nn.sigmoid(picked[:, 0] - picked[:, 1])
    weight_second = jax.nn.sigmoid(picked[:, 1] - picked[:, 0])
    hot_flat = route_hot.reshape(2 * token_count, expert_count).astype(jnp.int32)
    earlier = jnp.cumsum(hot_flat, axis=0) - hot_flat
    slots = jnp.sum(earlier * hot_flat, axis=-1).reshape(token_count, 2)
    target = expert_ids * capacity + slots
    placement = jnp.any(
        target[..., None] == jnp.arange(expert_count * capacity, dtype=jnp.int32), axis=1
    )
    outgoing = jnp.dot(placement.astype(jnp.bfloat16).T, moe_in, preferred_element_type=jnp.float32)
    outgoing = outgoing.astype(jnp.bfloat16).reshape(expert_count, capacity, -1)
    arrived = lax.all_to_all(outgoing, "ep", split_axis=0, concat_axis=0, tiled=True)
    piece = lax.all_gather(arrived[None], "ctx", axis=0, tiled=True)
    leading = piece.shape[:-1]
    flat_piece = piece.reshape(-1, piece.shape[-1])
    gate_out = jnp.dot(flat_piece, gate_weight[0], preferred_element_type=jnp.float32)
    up_out = jnp.dot(flat_piece, up_weight[0], preferred_element_type=jnp.float32)
    expert_hidden = (
        (silu_float(gate_out) * up_out)
        .astype(jnp.bfloat16)
        .reshape(leading + (gate_out.shape[-1],))
    )
    flat_hidden = expert_hidden.reshape(-1, expert_hidden.shape[-1])
    summed = lax.psum_scatter(
        jnp.dot(flat_hidden, down_weight[0], preferred_element_type=jnp.float32).astype(
            jnp.bfloat16
        ),
        "ctx",
        scatter_dimension=0,
        tiled=True,
    )
    expert_out = summed.reshape(expert_count, capacity, -1)
    returned = lax.all_to_all(expert_out, "ep", split_axis=0, concat_axis=0, tiled=True)
    returned = returned.reshape(expert_count * capacity, -1)
    fetched = returned[target].astype(jnp.float32)
    mixed = (
        flat_state + weight_first[:, None] * fetched[:, 0] + weight_second[:, None] * fetched[:, 1]
    )
    return mixed.astype(jnp.bfloat16).reshape(hidden_state.shape)


def solution(mesh):
    return jax.shard_map(
        shards,
        mesh=mesh,
        in_specs=(
            P("ctx", None, "ep"),
            P("ctx", None, "ep"),
            P("ctx", None, "ep"),
            P("ep", None, "ctx"),
            P("ep"),
            P("ep", "ctx"),
            P(("ctx", "ep"), None, None),
            P(),
            P(),
            P("ep", None, "ctx"),
            P("ep", None, "ctx"),
            P("ep", "ctx", None),
            P(("ctx", "ep"), None, None),
        ),
        out_specs=P(("ctx", "ep"), None, None),
        check_vma=False,
    )
```

profile of v0, /device:TPU:0, one launch (start us, length us, event | category | flops | bytes accessed | tf_op | source)
XLA Modules:
  0.0 359.3 jit_solution(11669898749633871269)
XLA Ops:
  6.5 0.7 all-gather.6.cloned.1.call-update
  7.3 1.3 reduce-window.6
  9.2 6.0 %all-gather = bf16[4,2,1]{2,1,0:T(2,128)(2,1)S(1)} all-gather(bf16[1,2,1]{2,1,0:T(2,128)(2,1)S(1)} %get-tuple-element.90), channel_id=2, replica_groups=mesh['ctx'=4,'ep'=8] {'ctx'}, dimensions={0}, use_global_device_ids=true | all-gather | bytes 20 | tf_op jit(solution)/shard_map/all_gather | solution.py:12
  15.3 0.9 reshape.321
  16.3 1.0 convert_multiply_fusion.1
  17.4 1.0 convert_multiply_fusion
  18.9 7.8 %all-gather.1 = bf16[8,128,128]{2,1,0:T(8,128)(2,1)S(1)} all-gather(bf16[2,128,128]{2,1,0:T(8,128)(2,1)S(1)} %convolution_convert_fusion.2), channel_id=3, replica_groups=mesh['ctx'=4,'ep'=8] {'ctx'}, dimensions={0}, use_global_device_ids=true | all-gather | bytes 327680 | tf_op jit(solution)/shard_map/all_gather | solution.py:12
  26.8 0.6 convolution_multiply_fusion
  27.9 0.5 multiply_reduce_fusion
  28.5 13.1 %all-gather.6.cloned.1.call-done = bf16[256,6144]{1,0:T(8,128)(2,1)} async-done(((bf16[256,1536]{1,0:T(8,128)(2,1)}), bf16[256,6144]{1,0:T(8,128)(2,1)}) %all-gather.6.cloned.1.call-update) | async-done | bytes 3145744 | tf_op jit(solution)/shard_map/all_gather | solution.py:93
  41.6 4.6 %fusion.9 = bf16[256,1,6144]{2,0,1:T(8,128)(2,1)} fusion(bf16[256,256]{0,1:T(8,128)(2,1)S(1)} %bitcast.115, bf16[256,6144]{1,0:T(8,128)(2,1)} %all-gather.6.cloned.1.call-done), kind=kOutput, calls=%fused_computation.12 | convolution fusion | flops 806879232 | bytes 6422528 | tf_op jit(solution)/shard_map/dot_general | solution.py:91
  46.3 0.6 copy-done.7
  47.8 73.1 %reduce-scatter.3.cloned.1.call-done = bf16[32,1,6144]{2,0,1:T(8,128)(2,1)} async-done(((bf16[256,1,6144]{2,0,1:T(8,128)(2,1)}), bf16[32,1,6144]{2,0,1:T(8,128)(2,1)}) %reduce-scatter.3.cloned.1.call-update) | async-done | bytes 393232 | tf_op jit(solution)/shard_map/reduce_scatter | solution.py:96
  120.8 1.2 fusion.29
  122.1 1.1 fusion.31
  123.3 0.7 copy-done.4
  124.0 0.5 convolution_convert_fusion.1
  124.9 40.4 %all_to_all.10 = bf16[8,12,6144]{2,1,0:T(8,128)(2,1)S(1)} all-to-all(bf16[8,12,6144]{2,1,0:T(8,128)(2,1)S(1)} %reshape.328), channel_id=1, replica_groups=mesh['ctx'=4,'ep'=8] {'ep'}, dimensions={0} | all-to-all | bytes 2359296 | tf_op jit(solution)/shard_map/all_to_all | solution.py:124
  165.3 1.7 copy.110
  167.2 36.4 %all-gather.8.cloned.1.call-done = bf16[32,12,6144]{2,0,1:T(8,128)(2,1)} async-done(((bf16[8,12,6144]{2,0,1:T(8,128)(2,1)}), bf16[32,12,6144]{2,0,1:T(8,128)(2,1)}) %all-gather.8.cloned.1.call-update) | async-done | bytes 4718608 | tf_op jit(solution)/shard_map/all_gather | solution.py:125
  203.5 7.7 %copy.111 = bf16[32,12,6144]{2,1,0:T(8,128)(2,1)} copy(bf16[32,12,6144]{2,0,1:T(8,128)(2,1)} %all-gather.8.cloned.1.call-done) | data formatting | bytes 9437184 | tf_op jit(solution)/shard_map/all_gather | solution.py:125
  211.3 7.6 %reshape.329 = bf16[384,6144]{1,0:T(8,128)(2,1)} reshape(bf16[32,12,6144]{2,1,0:T(8,128)(2,1)} %copy.111) | data formatting | bytes 9437184 | tf_op jit(solution)/shard_map/reshape | solution.py:127
  218.9 10.2 %fusion.4 = f32[384,1152]{1,0:T(8,128)S(1)} fusion(bf16[384,6144]{1,0:T(8,128)(2,1)} %reshape.329, bf16[1,6144,1152]{2,1,0:T(8,128)(2,1)} %param.24), kind=kOutput, calls=%fused_computation.8 | convolution fusion | flops 5435817984 | bytes 20643840 | tf_op jit(solution)/shard_map/dot_general | solution.py:128
  229.1 23.7 %fusion.6 = bf16[384,6144]{1,0:T(8,128)(2,1)} fusion(bf16[1,1152,6144]{2,1,0:T(8,128)(2,1)} %param.26, bf16[384,6144]{1,0:T(8,128)(2,1)} %reshape.329, bf16[1,6144,1152]{2,1,0:T(8,128)(2,1)} %param.25, f32[384,1152]{1,0:T(8,128)S(1)} %fusion.4), kind=kOutput, calls=%fused_computation.10 | convolution fusion | flops 10876649472 | bytes 39518208 | tf_op jit(solution)/shard_map/dot_general | solution.py:137
  252.9 48.0 %reduce-scatter.5.cloned.1.call-done = bf16[96,6144]{1,0:T(8,128)(2,1)} async-done(((bf16[384,6144]{1,0:T(8,128)(2,1)}), bf16[96,6144]{1,0:T(8,128)(2,1)}) %reduce-scatter.5.cloned.1.call-update) | async-done | bytes 1179664 | tf_op jit(solution)/shard_map/reduce_scatter | solution.py:136
  300.8 2.4 reshape.330
  303.2 5.5 %all-to-all-start.1 = ((bf16[8,12,6144]{2,1,0:T(8,128)(2,1)}), bf16[8,12,6144]{2,1,0:T(8,128)(2,1)S(1)}, u32[]{:S(2)}, u32[]{:S(2)}) async-start(bf16[8,12,6144]{2,1,0:T(8,128)(2,1)} %reshape.330), calls=%async_computation.3 | async-start | bytes 3145728 | tf_op jit(solution)/shard_map/all_to_all | solution.py:145
  309.4 36.3 %all-to-all-done.1 = bf16[8,12,6144]{2,1,0:T(8,128)(2,1)S(1)} async-done(((bf16[8,12,6144]{2,1,0:T(8,128)(2,1)}), bf16[8,12,6144]{2,1,0:T(8,128)(2,1)S(1)}, u32[]{:S(2)}, u32[]{:S(2)}) %all-to-all-start.1) | async-done | bytes 1179680 | tf_op jit(solution)/shard_map/all_to_all | solution.py:145
  346.0 1.9 gather_fusion
  347.9 2.2 reshape.348
  350.2 1.2 fusion.48
  351.4 1.3 fusion.27
  (71 shorter events, 4.5 us)
Async XLA Ops:
  6.5 302.6 %copy-start = (bf16[6144,8]{0,1:T(8,128)(2,1)S(1)}, bf16[6144,8]{0,1:T(8,128)(2,1)}, u32[]{:S(2)}) copy-start(bf16[6144,8]{0,1:T(8,128)(2,1)} %param.23) | copy-start | bytes 294916
  6.5 35.1 %all-gather.6.cloned.1.call-start = ((), (), s32[]{:S(2)}) async-start(), calls=%async_computation.4 | async-start | bytes 3932160 | tf_op jit(solution)/shard_map/all_gather | solution.py:93
  7.3 113.6 %reduce-scatter.3.cloned.1.call-start = ((), (), s32[]{:S(2)}) async-start(), calls=%async_computation.5 | async-start | bytes 3538944 | tf_op jit(solution)/shard_map/reduce_scatter | solution.py:96
  18.4 10.0 %copy-start.11 = (f32[256]{0:T(256)S(1)}, f32[256]{0:T(256)}, u32[]{:S(2)}) copy-start(f32[256]{0:T(256)} %param.19) | copy-start | bytes 3076
  46.2 0.7 copy-start.7
  46.2 74.6 %copy-start.1 = (bf16[32,1,6144]{2,0,1:T(8,128)(2,1)S(1)}, bf16[32,1,6144]{2,0,1:T(8,128)(2,1)}, u32[]{:S(2)}) copy-start(bf16[32,1,6144]{2,0,1:T(8,128)(2,1)} %param.21) | copy-start | bytes 1179652
  46.2 75.9 %copy-start.6 = (f32[6144]{0:T(1024)S(1)}, f32[6144]{0:T(1024)}, u32[]{:S(2)}) copy-start(f32[6144]{0:T(1024)} %param.22) | copy-start | bytes 73732
  46.3 157.3 %all-gather.8.cloned.1.call-start = ((), (), s32[]{:S(2)}) async-start(), calls=%async_computation.7 | async-start | bytes 5898240 | tf_op jit(solution)/shard_map/all_gather | solution.py:125
  47.5 74.6 %copy-start.9 = (s32[64]{0:T(128)}, s32[64]{0:T(128)S(1)}, u32[]{:S(2)}) copy-start(s32[64]{0:T(128)S(1)} %select_reduce_fusion) | copy-start | bytes 772
  123.3 0.7 copy-start.4
  166.9 133.9 %reduce-scatter.5.cloned.1.call-start = ((), (), s32[]{:S(2)}) async-start(), calls=%async_computation.6 | async-start | bytes 5898240 | tf_op jit(solution)/shard_map/reduce_scatter | solution.py:136
  252.8 55.9 %copy-start.10 = (s32[64]{0:T(128)S(1)}, s32[64]{0:T(128)}, u32[]{:S(2)}) copy-start(s32[64]{0:T(128)} %copy-done.9) | copy-start | bytes 772
  252.8 56.1 %copy-start.8 = (s32[32,1,2]{0,2,1:T(2,128)S(1)}, s32[32,1,2]{0,2,1:T(2,128)}, u32[]{:S(2)}) copy-start(s32[32,1,2]{0,2,1:T(2,128)} %param.27) | copy-start | bytes 772
  252.9 56.3 %copy-start.5 = (bf16[32,6144]{1,0:T(8,128)(2,1)S(1)}, bf16[32,6144]{1,0:T(8,128)(2,1)}, u32[]{:S(2)}) copy-start(bf16[32,6144]{1,0:T(8,128)(2,1)} %copy-done.4) | copy-start | bytes 1179652
  303.2 42.5 %all-to-all-start.1 = ((bf16[8,12,6144]{2,1,0:T(8,128)(2,1)}), bf16[8,12,6144]{2,1,0:T(8,128)(2,1)S(1)}, u32[]{:S(2)}, u32[]{:S(2)}) async-start(bf16[8,12,6144]{2,1,0:T(8,128)(2,1)} %reshape.330), calls=%async_computation.3 | async-start | bytes 3145728 | tf_op jit(solution)/shard_map/all_to_all | solution.py:145
  347.9 3.5 copy-start.2
  347.9 3.5 copy-start.3
Sparse Core Ops, SparseCore 0:
  8.9 32.6 all-gather.5
  46.4 74.4 reduce-scatter.2
  167.1 36.4 all-gather.7
  253.0 47.8 reduce-scatter.4
where the time goes:
time: 360 us; the launch traced here: 359 us
  waiting for transfers between devices  208 us (58%)
  blocking collectives  54.2 us (15%)
  matrix products  41 us (11%)
  local copies, waits for them, and re-layouts  29.1 us (8%)
  between operations  13.5 us (4%)
  other arithmetic  8.08 us (2%)
  starting transfers between devices  5.82 us (2%)
    reduce_scatter x1, waiting for transfers between devices, shards(): lax.psum_scatter(partial_out.reshape(length, sequences, -1).astype(jnp.bf...  73.1 us
    reduce_scatter x1, waiting for transfers between devices, shards(): lax.psum_scatter(jnp.dot(flat_hidden, down_weight[0], preferred_element_t...  48 us
    all_to_all x1, blocking collectives, shards(): lax.all_to_all(outgoing, 'ep', split_axis=0, concat_axis=0, tiled=True)  40.4 us
    all_gather x1, waiting for transfers between devices, shards(): piece = lax.all_gather(arrived[None], 'ctx', axis=0, tiled=True)  36.4 us
    all_to_all x1, waiting for transfers between devices, shards(): lax.all_to_all(expert_out, 'ep', split_axis=0, concat_axis=0, tiled=True)  36.3 us
    dot_general x1, matrix products, shards(): jnp.dot(flat_hidden, down_weight[0], preferred_element_type=jnp.float32)  23.7 us
    all_gather x2, blocking collectives, entering(): lax.all_gather(a.astype(kind), axis)  13.8 us
    all_gather x1, waiting for transfers between devices, shards(): lax.all_gather(out_weight, 'ctx', axis=1, tiled=True)  13.1 us
  transfers between devices with their start and end apart: 5, of which 5 were waited for; matrix products, arithmetic and copies ran while one was open for 2% of the time, Pallas kernels for 0%

commit v1 on v0

v1 whole, which is shorter than its diff:
```python
import jax
import jax.numpy as jnp
from jax import lax
from jax.sharding import PartitionSpec as P

highest = lax.Precision.HIGHEST
f32, bf16 = jnp.float32, jnp.bfloat16


def entering(array, axis, join, neutral):
    place = lax.axis_index(axis)
    gathered = jax.tree.map(
        lambda a, kind: lax.all_gather(a.astype(kind), axis), array, (bf16, bf16)
    )
    state = jax.tree.map(lambda a, e: jnp.zeros_like(a) + jnp.asarray(e, a.dtype), array, neutral)

    def one(hop, state):
        return join(
            state,
            jax.tree.map(
                lambda a, own: lax.dynamic_index_in_dim(a, hop, 0, False).astype(own.dtype),
                gathered,
                array,
            ),
        )

    return lax.fori_loop(0, place, one, state)


def silu_float(values):
    return values * jax.nn.sigmoid(values)


def swap(array, axis, mask):
    size = lax.axis_size(axis)
    return lax.ppermute(array, axis, [(i, i ^ mask) for i in range(size)])


def absolute(items, me):
    items, bit = list(items), 1
    while bit < len(items):
        flip = (me & bit) != 0
        items = [jnp.where(flip, items[i ^ bit], items[i]) for i in range(len(items))]
        bit *= 2
    return items


def attention(queries, keys_in, values_in, log_decay, attn_gain):
    length, sequences, width = queries.shape
    head_count = log_decay.shape[0]
    head_size = width // head_count
    split = (length, sequences, head_count, head_size)
    q_local = silu_float(queries.astype(f32)).reshape(split)
    k_local = silu_float(keys_in.astype(f32)).reshape(split)
    v_local = values_in.astype(f32).reshape(split)
    cumulative = jnp.cumsum(jnp.transpose(log_decay, (1, 0, 2)), axis=-1)
    positions = jnp.arange(length, dtype=jnp.int32)
    causal = positions[:, None] >= positions[None, :]
    spacing = cumulative[..., :, None] - cumulative[..., None, :]
    damping = jnp.where(causal, jnp.exp(jnp.where(causal, spacing, 0.0)), 0.0)
    scores = jnp.einsum("tshd,ushd->shtu", q_local, k_local, precision=highest) * damping
    inside = jnp.einsum("shtu,ushe->tshe", scores, v_local, precision=highest)
    remaining = jnp.exp(cumulative[..., -1:] - cumulative)
    own_state = jnp.einsum(
        "ushd,ushe->shde",
        k_local * jnp.transpose(remaining, (2, 0, 1))[..., None],
        v_local,
        precision=highest,
    )
    block_log = cumulative[..., -1]

    def combine(earlier, later_part):
        return (
            earlier[0] * later_part[0],
            later_part[0][..., None, None] * earlier[1] + later_part[1],
        )

    identity = (jnp.ones_like(block_log), jnp.zeros_like(own_state))
    _, prefix_state = entering((jnp.exp(block_log), own_state), "ctx", combine, identity)
    carried = jnp.exp(jnp.transpose(cumulative, (2, 0, 1)))[..., None] * jnp.einsum(
        "tshd,shde->tshe", q_local, prefix_state, precision=highest
    )
    heads_out = inside + carried
    mean_square = jnp.mean(heads_out * heads_out, axis=-1, keepdims=True)
    normed_heads = (
        heads_out * lax.rsqrt(mean_square + 1e-06) * attn_gain.reshape(head_count, head_size)
    )
    return normed_heads.astype(bf16).reshape(length * sequences, width)


def experts(rows, gate_weight, up_weight, down_weight):
    gate_out = jnp.dot(rows, gate_weight, preferred_element_type=f32)
    up_out = jnp.dot(rows, up_weight, preferred_element_type=f32)
    hidden = (silu_float(gate_out) * up_out).astype(bf16)
    return jnp.dot(hidden, down_weight, preferred_element_type=f32).astype(bf16)


def shards(
    queries,
    keys_in,
    values_in,
    log_decay,
    attn_gain,
    out_weight,
    residual,
    moe_gain,
    router,
    gate_weight,
    up_weight,
    down_weight,
    routes,
):
    n_ctx, n_ep = lax.axis_size("ctx"), lax.axis_size("ep")
    outer = 4
    fast = n_ep // outer
    high = n_ctx // fast
    place, member = lax.axis_index("ctx"), lax.axis_index("ep")
    far, near = member // fast, member % fast
    upper, lower = place // fast, place % fast
    model = residual.shape[-1]
    columns = out_weight.shape[1]

    def turned(a):
        pairs = []
        for h in range(high):
            for low in range(fast):
                for o in range(outer):
                    for n in range(fast):
                        source = (h * fast + low) * n_ep + o * fast + n
                        pairs.append((source, ((h ^ a) * fast + n) * n_ep + o * fast + low))
        return lax.ppermute(out_weight, ("ctx", "ep"), pairs)

    pieces = []
    for a in range(high):
        mine = turned(a)
        pieces.append(
            jnp.concatenate([mine] + [swap(mine, "ctx", j) for j in range(1, fast)], axis=0)
        )

    token_count = residual.shape[0] * residual.shape[1]
    own_residual = residual.reshape(token_count, model)
    own_routes = routes.reshape(token_count, 2)
    near_residual = absolute(
        [own_residual] + [swap(own_residual, "ep", k) for k in range(1, fast)], near
    )
    near_routes = absolute([own_routes] + [swap(own_routes, "ep", k) for k in range(1, fast)], near)

    normed_heads = attention(queries, keys_in, values_in, log_decay, attn_gain)
    heads = jnp.stack([normed_heads] + [swap(normed_heads, "ep", k) for k in range(1, fast)])
    heads = jnp.concatenate(
        [
            lax.dynamic_index_in_dim(heads, lower ^ j ^ near, 0, False)
            for j in range(fast)
        ],
        axis=1,
    ).reshape(outer, fast * token_count, -1)
    part = lambda k: lax.dynamic_index_in_dim(heads, far ^ k, 0, False)
    kept = jnp.concatenate([part(0), part(2)])
    given = jnp.concatenate([part(1), part(3)])
    block = fast * token_count
    attn = []
    for a in range(high):
        sent = jnp.dot(given, pieces[a], preferred_element_type=f32).astype(bf16)
        came = swap(sent, "ep", fast)
        total = jnp.dot(kept, pieces[a], preferred_element_type=f32) + came.astype(f32)
        came = swap(total[block:].astype(bf16), "ep", 2 * fast)
        total = total[:block] + came.astype(f32)
        narrow = total.astype(bf16)
        attn.extend([total] + [swap(narrow, "ep", k).astype(f32) for k in range(1, fast)])
    attn = absolute(attn, upper * fast + near)
    hidden_state = jnp.concatenate(near_residual).astype(f32) + jnp.concatenate(attn, axis=1)

    scale = lax.rsqrt(jnp.mean(hidden_state * hidden_state, axis=-1, keepdims=True) + 1e-06)
    moe_in = (hidden_state * scale * moe_gain).astype(bf16)
    logits = jnp.dot(moe_in, router, preferred_element_type=f32)
    expert_count = router.shape[1]
    capacity = max(2, 3 * token_count // expert_count)
    expert_ids = jnp.stack(near_routes)
    route_hot = expert_ids[..., None] == jnp.arange(expert_count, dtype=jnp.int32)
    picked = jnp.sum(
        jnp.where(route_hot, logits.reshape(fast, token_count, 1, expert_count), 0.0), axis=-1
    )
    weights = jax.nn.sigmoid(picked - picked[..., ::-1])
    hot_flat = route_hot.reshape(fast, 2 * token_count, expert_count).astype(jnp.int32)
    earlier = jnp.cumsum(hot_flat, axis=1) - hot_flat
    slots = jnp.sum(earlier * hot_flat, axis=-1).reshape(fast, token_count, 2)
    group = fast * capacity
    source = jnp.arange(fast, dtype=jnp.int32)[:, None, None]
    target = ((expert_ids // fast) ^ far) * group + source * capacity + slots
    target = jnp.where(expert_ids % fast == near, target, -1).reshape(block, 2)
    hit = target[..., None] == jnp.arange(outer * group, dtype=jnp.int32)
    placement = jnp.any(hit, axis=1).astype(bf16)
    mixing = jnp.sum(jnp.where(hit, weights.reshape(block, 2, 1), 0.0), axis=1)
    mixing_high = mixing.astype(bf16)
    mixing = jnp.concatenate([mixing_high, (mixing - mixing_high.astype(f32)).astype(bf16)])

    outgoing = jnp.dot(placement.T, moe_in, preferred_element_type=f32).astype(bf16)
    arrived = [outgoing[:group]] + [
        swap(outgoing[k * group : (k + 1) * group], "ep", k * fast) for k in range(1, outer)
    ]
    blocks = n_ctx // 2
    total = 0.0
    for first in (0, 2):
        own = jnp.concatenate(arrived[first : first + 2])
        size = own.shape[0]
        chip = jnp.concatenate([own] + [swap(own, "ctx", 2 * b) for b in range(1, blocks)])
        rows = jnp.concatenate([chip, swap(chip, "ctx", 1)])
        partial = experts(rows, gate_weight[0], up_weight[0], down_weight[0])
        half = blocks * size
        summed = partial[:half].astype(f32) + swap(partial[half:], "ctx", 1).astype(f32)
        result = summed[:size]
        for b in range(1, blocks):
            result = result + swap(
                summed[b * size : (b + 1) * size].astype(bf16), "ctx", 2 * b
            ).astype(f32)
        result = result.astype(bf16)
        returned = []
        for i, k in enumerate((first, first + 1)):
            piece = result[i * group : (i + 1) * group]
            returned.append(swap(piece, "ep", k * fast) if k else piece)
        returned = jnp.concatenate(returned)
        share = jnp.dot(
            mixing[:, first * group : (first + 2) * group], returned, preferred_element_type=f32
        )
        total = total + share[:block] + share[block:]
    total = total.reshape(fast, token_count, model)
    own_state = lax.dynamic_index_in_dim(
        hidden_state.reshape(fast, token_count, model), near, 0, False
    )
    result = own_state + lax.dynamic_index_in_dim(total, near, 0, False)
    for k in range(1, fast):
        other = lax.dynamic_index_in_dim(total, near ^ k, 0, False).astype(bf16)
        result = result + swap(other, "ep", k).astype(f32)
    return result.astype(bf16).reshape(residual.shape)


def solution(mesh):
    return jax.shard_map(
        shards,
        mesh=mesh,
        in_specs=(
            P("ctx", None, "ep"),
            P("ctx", None, "ep"),
            P("ctx", None, "ep"),
            P("ep", None, "ctx"),
            P("ep"),
            P("ep", "ctx"),
            P(("ctx", "ep"), None, None),
            P(),
            P(),
            P("ep", None, "ctx"),
            P("ep", None, "ctx"),
            P("ep", "ctx", None),
            P(("ctx", "ep"), None, None),
        ),
        out_specs=P(("ctx", "ep"), None, None),
        check_vma=False,
    )
```

time: 360 us -> 236 us (0.66)
  waiting for transfers between devices: 208 us -> 113 us
  starting transfers between devices: 5.82 us -> 45.4 us
  blocking collectives: 54.2 us -> 16.8 us
  local copies, waits for them, and re-layouts: 29.1 us -> 4.19 us
  between operations: 13.5 us -> 0.74 us
  matrix products: 41 us -> 47.5 us
    reduce_scatter x2 -> x0, waiting for transfers between devices: 121 us -> none  [the longest x1 73.1 us: shards(): lax.psum_scatter(partial_out.reshape(length, sequences, -1).astype(jnp.bf...]
    ppermute x0 -> x28, waiting for transfers between devices: none -> 113 us  [the longest x26 113 us: swap(): return lax.ppermute(array, axis, [(i, i ^ mask) for i in range(size)])]
    all_gather x2 -> x0, waiting for transfers between devices: 49.5 us -> none  [the longest x1 36.4 us: shards(): piece = lax.all_gather(arrived[None], 'ctx', axis=0, tiled=True)]
    ppermute x0 -> x28, starting transfers between devices: none -> 45.4 us  [the longest x26 40.7 us: swap(): return lax.ppermute(array, axis, [(i, i ^ mask) for i in range(size)])]
    all_to_all x1 -> x0, blocking collectives: 40.4 us -> none  [shards(): lax.all_to_all(outgoing, 'ep', split_axis=0, concat_axis=0, tiled=True)]
    all_to_all x1 -> x0, waiting for transfers between devices: 36.3 us -> none  [shards(): lax.all_to_all(expert_out, 'ep', split_axis=0, concat_axis=0, tiled=True)]
    reshape x8 -> x3, local copies, waits for them, and re-layouts: 11 us -> 0.28 us  [the longest x2 0.18 us: shards(): slots = jnp.sum(earlier * hot_flat, axis=-1).reshape(fast, token_count, 2)]
    all_gather x1 -> x0, local copies, waits for them, and re-layouts: 7.7 us -> none  [shards(): piece = lax.all_gather(arrived[None], 'ctx', axis=0, tiled=True)]
  transfers between devices with their start and end apart: 5 -> 28, of which waited for: 5 -> 14; matrix products, arithmetic and copies ran while one was open for 2% -> 23% of each run, Pallas kernels for 0% -> 0%
where the time goes in v1:
time: 236 us; the launch traced here: 235 us
  waiting for transfers between devices  113 us (48%)
  matrix products  47.5 us (20%)
  starting transfers between devices  45.4 us (19%)
  blocking collectives  16.8 us (7%)
  other arithmetic  7.9 us (3%)
  local copies, waits for them, and re-layouts  4.19 us (2%)
    ppermute x26, waiting for transfers between devices, swap(): return lax.ppermute(array, axis, [(i, i ^ mask) for i in range(size)])  113 us
    ppermute x26, starting transfers between devices, swap(): return lax.ppermute(array, axis, [(i, i ^ mask) for i in range(size)])  40.7 us
    all_gather x2, blocking collectives, entering(): lax.all_gather(a.astype(kind), axis)  16.8 us
    dot_general x2, matrix products, experts(): return jnp.dot(hidden, down_weight, preferred_element_type=f32).astype(bf16)  16.8 us
    dot_general x2, matrix products, experts(): gate_out = jnp.dot(rows, gate_weight, preferred_element_type=f32)  15.4 us
    dot_general x2, matrix products, experts(): up_out = jnp.dot(rows, up_weight, preferred_element_type=f32)  10 us
    ppermute x2, starting transfers between devices, turned(): return lax.ppermute(out_weight, ('ctx', 'ep'), pairs)  4.75 us
  transfers between devices with their start and end apart: 28, of which 14 were waited for; matrix products, arithmetic and copies ran while one was open for 23% of the time, Pallas kernels for 0%

profile of v1, /device:TPU:0, one launch (start us, length us, event | category | flops | bytes accessed | tf_op | source)
XLA Modules:
  0.0 235.1 jit_solution(14847843334668527967)
XLA Ops:
  0.0 3.0 %collective-permute-start.2 = (bf16[256,1536]{1,0:T(8,128)(2,1)}, bf16[256,1536]{1,0:T(8,128)(2,1)S(1)}, u32[]{:S(2)}, u32[]{:S(2)}) collective-permute-start(bf16[256,1536]{1,0:T(8,128)(2,1)} %param.20), channel_id=1, source_target_pairs={{0,16},{1,24},{2,18},{3,26},{4,20},{5,28},{6,22},{7,30},{8,17},{9,... | collective-permute-start | bytes 2359304 | tf_op jit(solution)/shard_map/ppermute | solution.py:131
  4.8 2.9 %collective-permute-start.12 = (s32[32,2]{0,1:T(2,128)}, s32[32,2]{0,1:T(2,128)S(1)}, u32[]{:S(2)}, u32[]{:S(2)}) collective-permute-start(s32[32,2]{0,1:T(2,128)} %bitcast.156), channel_id=1, source_target_pairs={{0,1},{1,0},{2,3},{3,2},{4,5},{5,4},{6,7},{7,6},{8,9},{9,8},{10,11... | collective-permute-start | bytes 776 | tf_op jit(solution)/shard_map/ppermute | solution.py:36
  11.9 10.5 %all-gather = bf16[4,2,1]{2,1,0:T(2,128)(2,1)S(1)} all-gather(bf16[1,2,1]{2,1,0:T(2,128)(2,1)S(1)} %get-tuple-element.110), channel_id=2, replica_groups=mesh['ctx'=4,'ep'=8] {'ctx'}, dimensions={0}, use_global_device_ids=true | all-gather | bytes 20 | tf_op jit(solution)/shard_map/all_gather | solution.py:13
  24.0 6.3 %all-gather.1 = bf16[8,128,128]{2,1,0:T(8,128)(2,1)S(1)} all-gather(bf16[2,128,128]{2,1,0:T(8,128)(2,1)S(1)} %convolution_convert_fusion.3), channel_id=3, replica_groups=mesh['ctx'=4,'ep'=8] {'ctx'}, dimensions={0}, use_global_device_ids=true | all-gather | bytes 327680 | tf_op jit(solution)/shard_map/all_gather | solution.py:13
  31.3 1.8 collective-permute-start
  34.7 2.8 %collective-permute-done.1 = bf16[256,256]{1,0:T(8,128)(2,1)S(1)} collective-permute-done((bf16[256,256]{1,0:T(8,128)(2,1)S(1)}, bf16[256,256]{1,0:T(8,128)(2,1)S(1)}, u32[]{:S(2)}, u32[]{:S(2)}) %collective-permute-start.1) | collective-permute-done | bytes 131104 | tf_op jit(solution)/shard_map/ppermute | solution.py:36
  42.2 8.1 %collective-permute-done.4 = bf16[128,1536]{1,0:T(8,128)(2,1)S(1)} collective-permute-done((bf16[128,1536]{1,0:T(8,128)(2,1)S(1)}, bf16[128,1536]{1,0:T(8,128)(2,1)S(1)}, u32[]{:S(2)}, u32[]{:S(2)}) %collective-permute-start.4) | collective-permute-done | bytes 393248 | tf_op jit(solution)/shard_map/ppermute | solution.py:36
  50.7 2.7 %collective-permute-start.5 = (bf16[64,1536]{1,0:T(8,128)(2,1)S(1)}, bf16[64,1536]{1,0:T(8,128)(2,1)S(1)}, u32[]{:S(2)}, u32[]{:S(2)}) collective-permute-start(bf16[64,1536]{1,0:T(8,128)(2,1)S(1)} %slice.206), channel_id=1, source_target_pairs={{0,4},{1,5},{2,6},{3,7},{4,0},{5,1},{6,2},{7,3},{8,12},{9,13},{10,... | collective-permute-start | bytes 589832 | tf_op jit(solution)/shard_map/ppermute | solution.py:36
  53.4 9.1 %collective-permute-done.9 = bf16[128,1536]{1,0:T(8,128)(2,1)S(1)} collective-permute-done((bf16[128,1536]{1,0:T(8,128)(2,1)S(1)}, bf16[128,1536]{1,0:T(8,128)(2,1)S(1)}, u32[]{:S(2)}, u32[]{:S(2)}) %collective-permute-start.9) | collective-permute-done | bytes 393248 | tf_op jit(solution)/shard_map/ppermute | solution.py:36
  62.9 1.8 collective-permute-start.10
  65.0 9.6 %collective-permute-done.10 = bf16[64,1536]{1,0:T(8,128)(2,1)S(1)} collective-permute-done((bf16[64,1536]{1,0:T(8,128)(2,1)S(1)}, bf16[64,1536]{1,0:T(8,128)(2,1)S(1)}, u32[]{:S(2)}, u32[]{:S(2)}) %collective-permute-start.10) | collective-permute-done | bytes 196640 | tf_op jit(solution)/shard_map/ppermute | solution.py:36
  75.0 5.5 %collective-permute-done.11 = bf16[64,1536]{1,0:T(8,128)(2,1)S(1)} collective-permute-done((bf16[64,1536]{1,0:T(8,128)(2,1)S(1)}, bf16[64,1536]{1,0:T(8,128)(2,1)S(1)}, u32[]{:S(2)}, u32[]{:S(2)}) %collective-permute-start.11) | collective-permute-done | bytes 196640 | tf_op jit(solution)/shard_map/ppermute | solution.py:36
  83.2 3.7 %collective-permute-start.20 = (bf16[24,6144]{1,0:T(8,128)(2,1)}, bf16[24,6144]{1,0:T(8,128)(2,1)S(1)}, u32[]{:S(2)}, u32[]{:S(2)}) collective-permute-start(bf16[24,6144]{1,0:T(8,128)(2,1)} %get-tuple-element.94), channel_id=1, source_target_pairs={{0,6},{1,7},{2,4},{3,5},{4,2},{5,3},{6,0},{7,1},{8,14},{9,15},{10,... | collective-permute-start | bytes 884744 | tf_op jit(solution)/shard_map/ppermute | solution.py:36
  88.1 18.2 %collective-permute-done.19 = bf16[24,6144]{1,0:T(8,128)(2,1)S(1)} collective-permute-done((bf16[24,6144]{1,0:T(8,128)(2,1)}, bf16[24,6144]{1,0:T(8,128)(2,1)S(1)}, u32[]{:S(2)}, u32[]{:S(2)}) %collective-permute-start.19) | collective-permute-done | bytes 294944 | tf_op jit(solution)/shard_map/ppermute | solution.py:36
  106.3 2.2 collective-permute-start.21
  108.7 14.0 %collective-permute-done.21 = bf16[48,6144]{1,0:T(8,128)(2,1)S(1)} collective-permute-done((bf16[48,6144]{1,0:T(8,128)(2,1)S(1)}, bf16[48,6144]{1,0:T(8,128)(2,1)S(1)}, u32[]{:S(2)}, u32[]{:S(2)}) %collective-permute-start.21) | collective-permute-done | bytes 589856 | tf_op jit(solution)/shard_map/ppermute | solution.py:36
  122.9 7.5 %collective-permute-done.14 = bf16[48,6144]{1,0:T(8,128)(2,1)S(1)} collective-permute-done((bf16[48,6144]{1,0:T(8,128)(2,1)S(1)}, bf16[48,6144]{1,0:T(8,128)(2,1)S(1)}, u32[]{:S(2)}, u32[]{:S(2)}) %collective-permute-start.14) | collective-permute-done | bytes 589856 | tf_op jit(solution)/shard_map/ppermute | solution.py:36
  130.7 6.8 %fusion.4 = f32[192,1152]{1,0:T(8,128)S(1)} fusion(bf16[192,6144]{1,0:T(8,128)(2,1)S(1)} %constant_dynamic-update-slice_fusion.4, bf16[1,6144,1152]{2,1,0:T(8,128)(2,1)} %param.25), kind=kOutput, calls=%fused_computation.7 | convolution fusion | flops 2717908992 | bytes 17399808 | tf_op jit(solution)/shard_map/dot_general | solution.py:93
  137.6 7.1 %fusion.8 = f32[192,1152]{1,0:T(8,128)S(1)} fusion(bf16[192,6144]{1,0:T(8,128)(2,1)S(1)} %constant_dynamic-update-slice_fusion.4, bf16[1,6144,1152]{2,1,0:T(8,128)(2,1)} %param.24), kind=kOutput, calls=%fused_computation.11 | convolution fusion | flops 2717908992 | bytes 17399808 | tf_op jit(solution)/shard_map/dot_general | solution.py:92
  144.7 8.5 %fusion.15 = bf16[192,6144]{1,0:T(8,128)(2,1)S(1)} fusion(bf16[1,1152,6144]{2,1,0:T(8,128)(2,1)} %param.26, f32[192,1152]{1,0:T(8,128)S(1)} %fusion.4, f32[192,1152]{1,0:T(8,128)S(1)} %fusion.8), kind=kOutput, calls=%fused_computation.16 | convolution fusion | flops 2720415744 | bytes 18284544 | tf_op jit(solution)/shard_map/dot_general | solution.py:95
  153.9 3.2 %fusion.6 = f32[192,1152]{1,0:T(8,128)S(1)} fusion(bf16[1,6144,1152]{2,1,0:T(8,128)(2,1)S(1)} %bitcast.159, bf16[96,6144]{1,0:T(8,128)(2,1)S(1)} %collective-permute-done.15, bf16[48,6144]{1,0:T(8,128)(2,1)S(1)} %collective-permute-done.14, bf16[24,6144]{1,0:T(8,128)(2,1)S(1)} %collective-permute-done.13, bf16[24,6144]{1,0:T(8,128)(2,1)S(1)} %get-tuple-element.93), kind=kOutput, calls=%fused_computation.9 | convolution fusion | flops 2727346176 | bytes 17399808 | tf_op jit(solution)/shard_map/dot_general | solution.py:93
  157.1 8.3 %fusion.10 = f32[192,1152]{1,0:T(8,128)S(1)} fusion(bf16[1,6144,1152]{2,1,0:T(8,128)(2,1)} %param.24, bf16[96,6144]{1,0:T(8,128)(2,1)S(1)} %collective-permute-done.15, bf16[48,6144]{1,0:T(8,128)(2,1)S(1)} %collective-permute-done.14, bf16[24,6144]{1,0:T(8,128)(2,1)S(1)} %collective-permute-done.13, bf16[24,6144]{1,0:T(8,128)(2,1)S(1)} %get-tuple-element.93), kind=kOutput, calls=%fused_computation.13 | convolution fusion | flops 2727346176 | bytes 17399808 | tf_op jit(solution)/shard_map/dot_general | solution.py:92
  165.5 8.3 %fusion.12 = bf16[192,6144]{1,0:T(8,128)(2,1)S(1)} fusion(bf16[1,1152,6144]{2,1,0:T(8,128)(2,1)} %param.26, f32[192,1152]{1,0:T(8,128)S(1)} %fusion.6, f32[192,1152]{1,0:T(8,128)S(1)} %fusion.10), kind=kOutput, calls=%fused_computation.15 | convolution fusion | flops 2720415744 | bytes 18284544 | tf_op jit(solution)/shard_map/dot_general | solution.py:95
  177.1 1.8 collective-permute-start.17
  178.9 11.6 %collective-permute-done.24 = bf16[48,6144]{1,0:T(8,128)(2,1)S(1)} collective-permute-done((bf16[48,6144]{1,0:T(8,128)(2,1)S(1)}, bf16[48,6144]{1,0:T(8,128)(2,1)S(1)}, u32[]{:S(2)}, u32[]{:S(2)}) %collective-permute-start.24) | collective-permute-done | bytes 589856 | tf_op jit(solution)/shard_map/ppermute | solution.py:36
  190.7 3.3 %collective-permute-start.26 = (bf16[24,6144]{1,0:T(8,128)(2,1)S(1)}, bf16[24,6144]{1,0:T(8,128)(2,1)S(1)}, u32[]{:S(2)}, u32[]{:S(2)}) collective-permute-start(bf16[24,6144]{1,0:T(8,128)(2,1)S(1)} %get-tuple-element.102), channel_id=1, source_target_pairs={{0,6},{1,7},{2,4},{3,5},{4,2},{5,3},{6,0},{7,1},{8,14},{9,15},{10,... | collective-permute-start | bytes 884744 | tf_op jit(solution)/shard_map/ppermute | solution.py:36
  194.0 5.5 %collective-permute-start.25 = (bf16[24,6144]{1,0:T(8,128)(2,1)S(1)}, bf16[24,6144]{1,0:T(8,128)(2,1)S(1)}, u32[]{:S(2)}, u32[]{:S(2)}) collective-permute-start(bf16[24,6144]{1,0:T(8,128)(2,1)S(1)} %get-tuple-element.101), channel_id=1, source_target_pairs={{0,4},{1,5},{2,6},{3,7},{4,0},{5,1},{6,2},{7,3},{8,12},{9,13},{10,... | collective-permute-start | bytes 884744 | tf_op jit(solution)/shard_map/ppermute | solution.py:36
  199.5 3.3 %collective-permute-done.17 = bf16[48,6144]{1,0:T(8,128)(2,1)S(1)} collective-permute-done((bf16[48,6144]{1,0:T(8,128)(2,1)S(1)}, bf16[48,6144]{1,0:T(8,128)(2,1)S(1)}, u32[]{:S(2)}, u32[]{:S(2)}) %collective-permute-start.17) | collective-permute-done | bytes 589856 | tf_op jit(solution)/shard_map/ppermute | solution.py:36
  202.9 6.9 %collective-permute-start.18 = (bf16[24,6144]{1,0:T(8,128)(2,1)S(1)}, bf16[24,6144]{1,0:T(8,128)(2,1)S(1)}, u32[]{:S(2)}, u32[]{:S(2)}) collective-permute-start(bf16[24,6144]{1,0:T(8,128)(2,1)S(1)} %get-tuple-element.100), channel_id=1, source_target_pairs={{0,2},{1,3},{2,0},{3,1},{4,6},{5,7},{6,4},{7,5},{8,10},{9,11},{10,... | collective-permute-start | bytes 884744 | tf_op jit(solution)/shard_map/ppermute | solution.py:36
  209.9 9.9 %collective-permute-done.25 = bf16[24,6144]{1,0:T(8,128)(2,1)S(1)} collective-permute-done((bf16[24,6144]{1,0:T(8,128)(2,1)S(1)}, bf16[24,6144]{1,0:T(8,128)(2,1)S(1)}, u32[]{:S(2)}, u32[]{:S(2)}) %collective-permute-start.25) | collective-permute-done | bytes 294944 | tf_op jit(solution)/shard_map/ppermute | solution.py:36
  220.4 2.6 %collective-permute-done.18 = bf16[24,6144]{1,0:T(8,128)(2,1)S(1)} collective-permute-done((bf16[24,6144]{1,0:T(8,128)(2,1)S(1)}, bf16[24,6144]{1,0:T(8,128)(2,1)S(1)}, u32[]{:S(2)}, u32[]{:S(2)}) %collective-permute-start.18) | collective-permute-done | bytes 294944 | tf_op jit(solution)/shard_map/ppermute | solution.py:36
  224.5 9.6 %collective-permute-done.27 = bf16[32,6144]{1,0:T(8,128)(2,1)S(1)} collective-permute-done((bf16[32,6144]{1,0:T(8,128)(2,1)S(1)}, bf16[32,6144]{1,0:T(8,128)(2,1)S(1)}, u32[]{:S(2)}, u32[]{:S(2)}) %collective-permute-start.27) | collective-permute-done | bytes 393248 | tf_op jit(solution)/shard_map/ppermute | solution.py:36
  (158 shorter events, 27.9 us)
Async XLA Ops:
  0.0 86.9 %copy-start = (bf16[6144,8]{0,1:T(8,128)(2,1)S(1)}, bf16[6144,8]{0,1:T(8,128)(2,1)}, u32[]{:S(2)}) copy-start(bf16[6144,8]{0,1:T(8,128)(2,1)} %param.23) | copy-start | bytes 294916
  0.0 11.6 %copy-start.3 = (bf16[256,1,256]{2,0,1:T(8,128)(2,1)S(1)}, bf16[256,1,256]{2,0,1:T(8,128)(2,1)}, u32[]{:S(2)}) copy-start(bf16[256,1,256]{2,0,1:T(8,128)(2,1)} %param.17) | copy-start | bytes 393220
  0.0 34.6 %collective-permute-start.2 = (bf16[256,1536]{1,0:T(8,128)(2,1)}, bf16[256,1536]{1,0:T(8,128)(2,1)S(1)}, u32[]{:S(2)}, u32[]{:S(2)}) collective-permute-start(bf16[256,1536]{1,0:T(8,128)(2,1)} %param.20), channel_id=1, source_target_pairs={{0,16},{1,24},{2,18},{3,26},{4,20},{5,28},{6,22},{7,30},{8,17},{9,... | collective-permute-start | bytes 2359304 | tf_op jit(solution)/shard_map/ppermute | solution.py:131
  3.0 34.7 %collective-permute-start.7 = (bf16[256,1536]{1,0:T(8,128)(2,1)}, bf16[256,1536]{1,0:T(8,128)(2,1)S(1)}, u32[]{:S(2)}, u32[]{:S(2)}) collective-permute-start(bf16[256,1536]{1,0:T(8,128)(2,1)} %param.20), channel_id=1, source_target_pairs={{0,0},{1,8},{2,2},{3,10},{4,4},{5,12},{6,6},{7,14},{8,1},{9,9},{10... | collective-permute-start | bytes 2359304 | tf_op jit(solution)/shard_map/ppermute | solution.py:131
  4.8 28.7 %collective-permute-start.12 = (s32[32,2]{0,1:T(2,128)}, s32[32,2]{0,1:T(2,128)S(1)}, u32[]{:S(2)}, u32[]{:S(2)}) collective-permute-start(s32[32,2]{0,1:T(2,128)} %bitcast.156), channel_id=1, source_target_pairs={{0,1},{1,0},{2,3},{3,2},{4,5},{5,4},{6,7},{7,6},{8,9},{9,8},{10,11... | collective-permute-start | bytes 776 | tf_op jit(solution)/shard_map/ppermute | solution.py:36
  31.0 6.4 %collective-permute-start.1 = (bf16[256,256]{1,0:T(8,128)(2,1)S(1)}, bf16[256,256]{1,0:T(8,128)(2,1)S(1)}, u32[]{:S(2)}, u32[]{:S(2)}) collective-permute-start(bf16[256,256]{1,0:T(8,128)(2,1)S(1)} %copy.108), channel_id=1, source_target_pairs={{0,1},{1,0},{2,3},{3,2},{4,5},{5,4},{6,7},{7,6},{8,9},{9,8},{10,11... | collective-permute-start | bytes 393224 | tf_op jit(solution)/shard_map/ppermute | solution.py:36
  31.3 43.6 %collective-permute-start = (bf16[32,6144]{1,0:T(8,128)(2,1)S(1)}, bf16[32,6144]{1,0:T(8,128)(2,1)S(1)}, u32[]{:S(2)}, u32[]{:S(2)}) collective-permute-start(bf16[32,6144]{1,0:T(8,128)(2,1)S(1)} %bitcast.149), channel_id=1, source_target_pairs={{0,1},{1,0},{2,3},{3,2},{4,5},{5,4},{6,7},{7,6},{8,9},{9,8},{10,11... | collective-permute-start | bytes 1179656 | tf_op jit(solution)/shard_map/ppermute | solution.py:36
  34.6 3.3 %collective-permute-start.3 = (bf16[256,1536]{1,0:T(8,128)(2,1)S(1)}, bf16[256,1536]{1,0:T(8,128)(2,1)S(1)}, u32[]{:S(2)}, u32[]{:S(2)}) collective-permute-start(bf16[256,1536]{1,0:T(8,128)(2,1)S(1)} %collective-permute-done.2), channel_id=1, source_target_pairs={{0,8},{8,0},{16,24},{24,16},{1,9},{9,1},{17,25},{25,17},{2,10},{10... | collective-permute-start | bytes 2359304 | tf_op jit(solution)/shard_map/ppermute | solution.py:36
  37.6 2.4 collective-permute-start.8
  38.3 12.0 %collective-permute-start.4 = (bf16[128,1536]{1,0:T(8,128)(2,1)S(1)}, bf16[128,1536]{1,0:T(8,128)(2,1)S(1)}, u32[]{:S(2)}, u32[]{:S(2)}) collective-permute-start(bf16[128,1536]{1,0:T(8,128)(2,1)S(1)} %convolution_convert_fusion.2), channel_id=1, source_target_pairs={{0,2},{1,3},{2,0},{3,1},{4,6},{5,7},{6,4},{7,5},{8,10},{9,11},{10,... | collective-permute-start | bytes 1179656 | tf_op jit(solution)/shard_map/ppermute | solution.py:36
  40.4 22.1 %collective-permute-start.9 = (bf16[128,1536]{1,0:T(8,128)(2,1)S(1)}, bf16[128,1536]{1,0:T(8,128)(2,1)S(1)}, u32[]{:S(2)}, u32[]{:S(2)}) collective-permute-start(bf16[128,1536]{1,0:T(8,128)(2,1)S(1)} %convolution_convert_fusion.1), channel_id=1, source_target_pairs={{0,2},{1,3},{2,0},{3,1},{4,6},{5,7},{6,4},{7,5},{8,10},{9,11},{10,... | collective-permute-start | bytes 1179656 | tf_op jit(solution)/shard_map/ppermute | solution.py:36
  50.7 14.0 %collective-permute-start.5 = (bf16[64,1536]{1,0:T(8,128)(2,1)S(1)}, bf16[64,1536]{1,0:T(8,128)(2,1)S(1)}, u32[]{:S(2)}, u32[]{:S(2)}) collective-permute-start(bf16[64,1536]{1,0:T(8,128)(2,1)S(1)} %slice.206), channel_id=1, source_target_pairs={{0,4},{1,5},{2,6},{3,7},{4,0},{5,1},{6,2},{7,3},{8,12},{9,13},{10,... | collective-permute-start | bytes 589832 | tf_op jit(solution)/shard_map/ppermute | solution.py:36
  62.9 11.7 %collective-permute-start.10 = (bf16[64,1536]{1,0:T(8,128)(2,1)S(1)}, bf16[64,1536]{1,0:T(8,128)(2,1)S(1)}, u32[]{:S(2)}, u32[]{:S(2)}) collective-permute-start(bf16[64,1536]{1,0:T(8,128)(2,1)S(1)} %slice.205), channel_id=1, source_target_pairs={{0,4},{1,5},{2,6},{3,7},{4,0},{5,1},{6,2},{7,3},{8,12},{9,13},{10,... | collective-permute-start | bytes 589832 | tf_op jit(solution)/shard_map/ppermute | solution.py:36
  64.8 10.3 %collective-permute-start.6 = (bf16[64,1536]{1,0:T(8,128)(2,1)S(1)}, bf16[64,1536]{1,0:T(8,128)(2,1)S(1)}, u32[]{:S(2)}, u32[]{:S(2)}) collective-permute-start(bf16[64,1536]{1,0:T(8,128)(2,1)S(1)} %fusion.87), channel_id=1, source_target_pairs={{0,1},{1,0},{2,3},{3,2},{4,5},{5,4},{6,7},{7,6},{8,9},{9,8},{10,11... | collective-permute-start | bytes 589832 | tf_op jit(solution)/shard_map/ppermute | solution.py:36
  74.6 5.9 %collective-permute-start.11 = (bf16[64,1536]{1,0:T(8,128)(2,1)S(1)}, bf16[64,1536]{1,0:T(8,128)(2,1)S(1)}, u32[]{:S(2)}, u32[]{:S(2)}) collective-permute-start(bf16[64,1536]{1,0:T(8,128)(2,1)S(1)} %fusion.88), channel_id=1, source_target_pairs={{0,1},{1,0},{2,3},{3,2},{4,5},{5,4},{6,7},{7,6},{8,9},{9,8},{10,11... | collective-permute-start | bytes 589832 | tf_op jit(solution)/shard_map/ppermute | solution.py:36
  83.2 23.1 %collective-permute-start.19 = (bf16[24,6144]{1,0:T(8,128)(2,1)}, bf16[24,6144]{1,0:T(8,128)(2,1)S(1)}, u32[]{:S(2)}, u32[]{:S(2)}) collective-permute-start(bf16[24,6144]{1,0:T(8,128)(2,1)} %get-tuple-element.95), channel_id=1, source_target_pairs={{0,4},{1,5},{2,6},{3,7},{4,0},{5,1},{6,2},{7,3},{8,12},{9,13},{10,... | collective-permute-start | bytes 884744 | tf_op jit(solution)/shard_map/ppermute | solution.py:36
  83.2 23.1 %collective-permute-start.20 = (bf16[24,6144]{1,0:T(8,128)(2,1)}, bf16[24,6144]{1,0:T(8,128)(2,1)S(1)}, u32[]{:S(2)}, u32[]{:S(2)}) collective-permute-start(bf16[24,6144]{1,0:T(8,128)(2,1)} %get-tuple-element.94), channel_id=1, source_target_pairs={{0,6},{1,7},{2,4},{3,5},{4,2},{5,3},{6,0},{7,1},{8,14},{9,15},{10,... | collective-permute-start | bytes 884744 | tf_op jit(solution)/shard_map/ppermute | solution.py:36
  87.4 21.1 %collective-permute-start.13 = (bf16[24,6144]{1,0:T(8,128)(2,1)}, bf16[24,6144]{1,0:T(8,128)(2,1)S(1)}, u32[]{:S(2)}, u32[]{:S(2)}) collective-permute-start(bf16[24,6144]{1,0:T(8,128)(2,1)} %get-tuple-element.96), channel_id=1, source_target_pairs={{0,2},{1,3},{2,0},{3,1},{4,6},{5,7},{6,4},{7,5},{8,10},{9,11},{10,... | collective-permute-start | bytes 884744 | tf_op jit(solution)/shard_map/ppermute | solution.py:36
  106.3 16.5 %collective-permute-start.21 = (bf16[48,6144]{1,0:T(8,128)(2,1)S(1)}, bf16[48,6144]{1,0:T(8,128)(2,1)S(1)}, u32[]{:S(2)}, u32[]{:S(2)}) collective-permute-start(bf16[48,6144]{1,0:T(8,128)(2,1)S(1)} %pad_maximum_fusion.4), channel_id=1, source_target_pairs={{0,16},{8,24},{16,0},{24,8},{1,17},{9,25},{17,1},{25,9},{2,18},{10... | collective-permute-start | bytes 1769480 | tf_op jit(solution)/shard_map/ppermute | solution.py:36
  108.6 21.9 %collective-permute-start.14 = (bf16[48,6144]{1,0:T(8,128)(2,1)S(1)}, bf16[48,6144]{1,0:T(8,128)(2,1)S(1)}, u32[]{:S(2)}, u32[]{:S(2)}) collective-permute-start(bf16[48,6144]{1,0:T(8,128)(2,1)S(1)} %pad_maximum_fusion.3), channel_id=1, source_target_pairs={{0,16},{8,24},{16,0},{24,8},{1,17},{9,25},{17,1},{25,9},{2,18},{10... | collective-permute-start | bytes 1769480 | tf_op jit(solution)/shard_map/ppermute | solution.py:36
  122.8 7.8 %collective-permute-start.22 = (bf16[96,6144]{1,0:T(8,128)(2,1)S(1)}, bf16[96,6144]{1,0:T(8,128)(2,1)S(1)}, u32[]{:S(2)}, u32[]{:S(2)}) collective-permute-start(bf16[96,6144]{1,0:T(8,128)(2,1)S(1)} %pad_maximum_fusion.2), channel_id=1, source_target_pairs={{0,8},{8,0},{16,24},{24,16},{1,9},{9,1},{17,25},{25,17},{2,10},{10... | collective-permute-start | bytes 3538952 | tf_op jit(solution)/shard_map/ppermute | solution.py:36
  130.5 23.4 %collective-permute-start.15 = (bf16[96,6144]{1,0:T(8,128)(2,1)S(1)}, bf16[96,6144]{1,0:T(8,128)(2,1)S(1)}, u32[]{:S(2)}, u32[]{:S(2)}) collective-permute-start(bf16[96,6144]{1,0:T(8,128)(2,1)S(1)} %pad_maximum_fusion.1), channel_id=1, source_target_pairs={{0,8},{8,0},{16,24},{24,16},{1,9},{9,1},{17,25},{25,17},{2,10},{10... | collective-permute-start | bytes 3538952 | tf_op jit(solution)/shard_map/ppermute | solution.py:36
  137.5 16.3 %slice-start = ((s8[14155776]{0:T(1024)(128)(4,1)}), s8[4194304]{0:T(1024)(128)(4,1)S(1)}, s32[]{:S(2)}) async-start(s8[14155776]{0:T(1024)(128)(4,1)} %bitcast.158), calls=%async_computation | async-start | bytes 8388608
  137.6 16.3 %slice-start.1 = ((s8[14155776]{0:T(1024)(128)(4,1)}), s8[4194304]{0:T(1024)(128)(4,1)S(1)}, s32[]{:S(2)}) async-start(s8[14155776]{0:T(1024)(128)(4,1)} %bitcast.158), calls=%async_computation.1 | async-start | bytes 8388608
  153.3 20.7 %collective-permute-start.23 = (bf16[96,6144]{1,0:T(8,128)(2,1)S(1)}, bf16[96,6144]{1,0:T(8,128)(2,1)S(1)}, u32[]{:S(2)}, u32[]{:S(2)}) collective-permute-start(bf16[96,6144]{1,0:T(8,128)(2,1)S(1)} %slice.142), channel_id=1, source_target_pairs={{0,8},{8,0},{16,24},{24,16},{1,9},{9,1},{17,25},{25,17},{2,10},{10... | collective-permute-start | bytes 3538952 | tf_op jit(solution)/shard_map/ppermute | solution.py:36
  173.9 2.9 %collective-permute-start.16 = (bf16[96,6144]{1,0:T(8,128)(2,1)S(1)}, bf16[96,6144]{1,0:T(8,128)(2,1)S(1)}, u32[]{:S(2)}, u32[]{:S(2)}) collective-permute-start(bf16[96,6144]{1,0:T(8,128)(2,1)S(1)} %slice.132), channel_id=1, source_target_pairs={{0,8},{8,0},{16,24},{24,16},{1,9},{9,1},{17,25},{25,17},{2,10},{10... | collective-permute-start | bytes 3538952 | tf_op jit(solution)/shard_map/ppermute | solution.py:36
  174.3 16.2 %collective-permute-start.24 = (bf16[48,6144]{1,0:T(8,128)(2,1)S(1)}, bf16[48,6144]{1,0:T(8,128)(2,1)S(1)}, u32[]{:S(2)}, u32[]{:S(2)}) collective-permute-start(bf16[48,6144]{1,0:T(8,128)(2,1)S(1)} %slice.203), channel_id=1, source_target_pairs={{0,16},{8,24},{16,0},{24,8},{1,17},{9,25},{17,1},{25,9},{2,18},{10... | collective-permute-start | bytes 1769480 | tf_op jit(solution)/shard_map/ppermute | solution.py:36
  177.1 25.6 %collective-permute-start.17 = (bf16[48,6144]{1,0:T(8,128)(2,1)S(1)}, bf16[48,6144]{1,0:T(8,128)(2,1)S(1)}, u32[]{:S(2)}, u32[]{:S(2)}) collective-permute-start(bf16[48,6144]{1,0:T(8,128)(2,1)S(1)} %slice.204), channel_id=1, source_target_pairs={{0,16},{8,24},{16,0},{24,8},{1,17},{9,25},{17,1},{25,9},{2,18},{10... | collective-permute-start | bytes 1769480 | tf_op jit(solution)/shard_map/ppermute | solution.py:36
  190.7 19.2 %collective-permute-start.26 = (bf16[24,6144]{1,0:T(8,128)(2,1)S(1)}, bf16[24,6144]{1,0:T(8,128)(2,1)S(1)}, u32[]{:S(2)}, u32[]{:S(2)}) collective-permute-start(bf16[24,6144]{1,0:T(8,128)(2,1)S(1)} %get-tuple-element.102), channel_id=1, source_target_pairs={{0,6},{1,7},{2,4},{3,5},{4,2},{5,3},{6,0},{7,1},{8,14},{9,15},{10,... | collective-permute-start | bytes 884744 | tf_op jit(solution)/shard_map/ppermute | solution.py:36
  194.0 25.8 %collective-permute-start.25 = (bf16[24,6144]{1,0:T(8,128)(2,1)S(1)}, bf16[24,6144]{1,0:T(8,128)(2,1)S(1)}, u32[]{:S(2)}, u32[]{:S(2)}) collective-permute-start(bf16[24,6144]{1,0:T(8,128)(2,1)S(1)} %get-tuple-element.101), channel_id=1, source_target_pairs={{0,4},{1,5},{2,6},{3,7},{4,0},{5,1},{6,2},{7,3},{8,12},{9,13},{10,... | collective-permute-start | bytes 884744 | tf_op jit(solution)/shard_map/ppermute | solution.py:36
  202.9 20.1 %collective-permute-start.18 = (bf16[24,6144]{1,0:T(8,128)(2,1)S(1)}, bf16[24,6144]{1,0:T(8,128)(2,1)S(1)}, u32[]{:S(2)}, u32[]{:S(2)}) collective-permute-start(bf16[24,6144]{1,0:T(8,128)(2,1)S(1)} %get-tuple-element.100), channel_id=1, source_target_pairs={{0,2},{1,3},{2,0},{3,1},{4,6},{5,7},{6,4},{7,5},{8,10},{9,11},{10,... | collective-permute-start | bytes 884744 | tf_op jit(solution)/shard_map/ppermute | solution.py:36
  223.9 10.2 %collective-permute-start.27 = (bf16[32,6144]{1,0:T(8,128)(2,1)S(1)}, bf16[32,6144]{1,0:T(8,128)(2,1)S(1)}, u32[]{:S(2)}, u32[]{:S(2)}) collective-permute-start(bf16[32,6144]{1,0:T(8,128)(2,1)S(1)} %fusion.40), channel_id=1, source_target_pairs={{0,1},{1,0},{2,3},{3,2},{4,5},{5,4},{6,7},{7,6},{8,9},{9,8},{10,11... | collective-permute-start | bytes 1179656 | tf_op jit(solution)/shard_map/ppermute | solution.py:36
  (7 other events, 31.0 us)

commit v2 on v1

v2 whole, which is shorter than its diff:
```python
import functools
import jax
import jax.numpy as jnp
from jax import lax
from jax.experimental import pallas as pl
from jax.experimental.pallas import tpu as pltpu
from jax.sharding import PartitionSpec as P

highest = lax.Precision.HIGHEST
f32, bf16 = jnp.float32, jnp.bfloat16


def silu_float(values):
    return values * jax.nn.sigmoid(values)


def swap(array, axis, mask):
    size = lax.axis_size(axis)
    return lax.ppermute(array, axis, [(i, i ^ mask) for i in range(size)])


def absolute(items, me):
    items, bit = list(items), 1
    while bit < len(items):
        flip = (me & bit) != 0
        items = [jnp.where(flip, items[i ^ bit], items[i]) for i in range(len(items))]
        bit *= 2
    return items


TAIL = 16


def dot_highest(left, right, contract):
    return lax.dot_general(
        left, right, ((contract[:1], contract[1:]), ((), ())),
        precision=highest, preferred_element_type=f32,
    )


def within_kernel(heads, size, q_ref, k_ref, v_ref, decay_ref, inside_ref, query_ref, state_ref):
    length = q_ref.shape[0]
    row = lax.broadcasted_iota(jnp.int32, (length, length), 0)
    column = lax.broadcasted_iota(jnp.int32, (length, length), 1)
    causal = row >= column
    upto = jnp.where(causal, 1.0, 0.0).astype(f32)
    decay = decay_ref[...]
    along = dot_highest(decay, upto, (1, 1))
    down = dot_highest(upto, decay, (1, 1))
    for h in range(heads):
        span = slice(h * size, (h + 1) * size)
        query = silu_float(q_ref[:, span].astype(f32))
        key = silu_float(k_ref[:, span].astype(f32))
        value = v_ref[:, span].astype(f32)
        passed = down[:, h : h + 1]
        spacing = passed - along[h : h + 1, :]
        damping = jnp.where(causal, jnp.exp(jnp.where(causal, spacing, 0.0)), 0.0)
        scores = dot_highest(query, key, (1, 1)) * damping
        inside_ref[:, span] = dot_highest(scores, value, (1, 0))
        query_ref[:, span] = query * jnp.exp(passed)
        whole = passed[length - 1 : length, :]
        state = dot_highest(key * jnp.exp(whole - passed), value, (0, 0))
        base = h * (size + TAIL)
        state_ref[base : base + size, :] = state.astype(bf16)
        state_ref[base + size : base + size + TAIL, :] = jnp.broadcast_to(
            jnp.exp(whole), (TAIL, size)
        ).astype(bf16)


def across_kernel(heads, size, place_ref, states_ref, inside_ref, query_ref, gain_ref, out_ref):
    place = place_ref[0]
    for h in range(heads):
        span = slice(h * size, (h + 1) * size)
        base = h * (size + TAIL)
        state = jnp.zeros((size, size), f32)
        for hop in range(states_ref.shape[0]):
            own = states_ref[hop, base : base + size, :].astype(f32)
            decay = states_ref[hop, base + size : base + size + TAIL, :].astype(f32)[:1]
            state = jnp.where(hop < place, decay * state + own, state)
        total = inside_ref[:, span] + dot_highest(query_ref[:, span], state, (1, 0))
        mean_square = jnp.mean(total * total, axis=-1, keepdims=True)
        out_ref[:, span] = (
            total * lax.rsqrt(mean_square + 1e-06) * gain_ref[:, span]
        ).astype(bf16)


def attention(queries, keys_in, values_in, log_decay, attn_gain):
    length, sequences, width = queries.shape
    heads = log_decay.shape[0]
    size = width // heads
    flat = lambda a: a.reshape(length * sequences, width)
    inside, query, state = pl.pallas_call(
        functools.partial(within_kernel, heads, size),
        out_shape=(
            jax.ShapeDtypeStruct((length, width), f32),
            jax.ShapeDtypeStruct((length, width), f32),
            jax.ShapeDtypeStruct((heads * (size + TAIL), size), bf16),
        ),
        name="within_block",
    )(flat(queries), flat(keys_in), flat(values_in), log_decay.reshape(heads, length))
    states = lax.all_gather(state, "ctx")
    place = lax.axis_index("ctx").astype(jnp.int32).reshape(1)
    vmem = pl.BlockSpec(memory_space=pltpu.VMEM)
    return pl.pallas_call(
        functools.partial(across_kernel, heads, size),
        in_specs=[pl.BlockSpec(memory_space=pltpu.SMEM)] + [vmem] * 4,
        out_specs=vmem,
        out_shape=jax.ShapeDtypeStruct((length, width), bf16),
        name="across_blocks",
    )(place, states, inside, query, attn_gain.reshape(1, width))


def experts(rows, gate_weight, up_weight, down_weight):
    gate_out = jnp.dot(rows, gate_weight, preferred_element_type=f32)
    up_out = jnp.dot(rows, up_weight, preferred_element_type=f32)
    hidden = (silu_float(gate_out) * up_out).astype(bf16)
    return jnp.dot(hidden, down_weight, preferred_element_type=f32).astype(bf16)


def shards(
    queries,
    keys_in,
    values_in,
    log_decay,
    attn_gain,
    out_weight,
    residual,
    moe_gain,
    router,
    gate_weight,
    up_weight,
    down_weight,
    routes,
):
    n_ctx, n_ep = lax.axis_size("ctx"), lax.axis_size("ep")
    outer = 4
    fast = n_ep // outer
    high = n_ctx // fast
    place, member = lax.axis_index("ctx"), lax.axis_index("ep")
    far, near = member // fast, member % fast
    upper, lower = place // fast, place % fast
    model = residual.shape[-1]
    columns = out_weight.shape[1]

    def turned(a):
        pairs = []
        for h in range(high):
            for low in range(fast):
                for o in range(outer):
                    for n in range(fast):
                        source = (h * fast + low) * n_ep + o * fast + n
                        pairs.append((source, ((h ^ a) * fast + n) * n_ep + o * fast + low))
        return lax.ppermute(out_weight, ("ctx", "ep"), pairs)

    pieces = []
    for a in range(high):
        mine = turned(a)
        pieces.append(
            jnp.concatenate([mine] + [swap(mine, "ctx", j) for j in range(1, fast)], axis=0)
        )

    token_count = residual.shape[0] * residual.shape[1]
    own_residual = residual.reshape(token_count, model)
    own_routes = routes.reshape(token_count, 2)
    normed_heads = attention(queries, keys_in, values_in, log_decay, attn_gain)
    heads = jnp.stack([normed_heads] + [swap(normed_heads, "ep", k) for k in range(1, fast)])
    own_residual, own_routes, _ = lax.optimization_barrier((own_residual, own_routes, heads))
    near_residual = [own_residual] + [swap(own_residual, "ep", k) for k in range(1, fast)]
    near_routes = [own_routes] + [swap(own_routes, "ep", k) for k in range(1, fast)]
    heads = jnp.concatenate(
        [
            lax.dynamic_index_in_dim(heads, lower ^ j ^ near, 0, False)
            for j in range(fast)
        ],
        axis=1,
    ).reshape(outer, fast * token_count, -1)
    part = lambda k: lax.dynamic_index_in_dim(heads, far ^ k, 0, False)
    kept = jnp.concatenate([part(0), part(2)])
    given = jnp.concatenate([part(1), part(3)])
    block = fast * token_count
    attn = []
    for a in range(high):
        sent = jnp.dot(given, pieces[a], preferred_element_type=f32).astype(bf16)
        came = swap(sent, "ep", fast)
        if a == 0:
            near_routes, near_residual, came = lax.optimization_barrier(
                (near_routes, near_residual, came)
            )
            near_routes = absolute(near_routes, near)
            near_residual = absolute(near_residual, near)
        total = jnp.dot(kept, pieces[a], preferred_element_type=f32) + came.astype(f32)
        came = swap(total[block:].astype(bf16), "ep", 2 * fast)
        total = total[:block] + came.astype(f32)
        narrow = total.astype(bf16)
        attn.extend([total] + [swap(narrow, "ep", k).astype(f32) for k in range(1, fast)])
    attn = absolute(attn, upper * fast + near)
    hidden_state = jnp.concatenate(near_residual).astype(f32) + jnp.concatenate(attn, axis=1)

    scale = lax.rsqrt(jnp.mean(hidden_state * hidden_state, axis=-1, keepdims=True) + 1e-06)
    moe_in = (hidden_state * scale * moe_gain).astype(bf16)
    logits = jnp.dot(moe_in, router, preferred_element_type=f32)
    expert_count = router.shape[1]
    capacity = max(2, 3 * token_count // expert_count)
    expert_ids = jnp.stack(near_routes)
    route_hot = expert_ids[..., None] == jnp.arange(expert_count, dtype=jnp.int32)
    picked = jnp.sum(
        jnp.where(route_hot, logits.reshape(fast, token_count, 1, expert_count), 0.0), axis=-1
    )
    weights = jax.nn.sigmoid(picked - picked[..., ::-1])
    hot_flat = route_hot.reshape(fast, 2 * token_count, expert_count).astype(jnp.int32)
    earlier = jnp.cumsum(hot_flat, axis=1) - hot_flat
    slots = jnp.sum(earlier * hot_flat, axis=-1).reshape(fast, token_count, 2)
    group = fast * capacity
    source = jnp.arange(fast, dtype=jnp.int32)[:, None, None]
    target = ((expert_ids // fast) ^ far) * group + source * capacity + slots
    target = jnp.where(expert_ids % fast == near, target, -1).reshape(block, 2)
    hit = target[..., None] == jnp.arange(outer * group, dtype=jnp.int32)
    placement = jnp.any(hit, axis=1).astype(bf16)
    mixing = jnp.sum(jnp.where(hit, weights.reshape(block, 2, 1), 0.0), axis=1)

    outgoing = jnp.dot(placement.T, moe_in, preferred_element_type=f32).astype(bf16)
    arrived = [outgoing[k * group : (k + 1) * group] for k in range(outer)]
    for k in (2, 1):
        arrived[k] = swap(arrived[k], "ep", k * fast)
    arrived[3], _ = lax.optimization_barrier((arrived[3], arrived[1]))
    arrived[3] = swap(arrived[3], "ep", 3 * fast)
    blocks = n_ctx // 2
    over = [[swap(rows, "ctx", 2 * b) for b in range(1, blocks)] for rows in arrived]

    def visit(members, sooner, latest):
        chip = [arrived[k] for k in members]
        chip += [over[k][b] for b in range(blocks - 1) for k in members]
        chip, _ = lax.optimization_barrier((chip, sooner))
        chip = jnp.concatenate(chip)
        rows = jnp.concatenate([chip, swap(chip, "ctx", 1)])
        rows, _ = lax.optimization_barrier((rows, latest))
        partial = experts(rows, gate_weight[0], up_weight[0], down_weight[0])
        half = chip.shape[0]
        return partial[:half].astype(f32) + swap(partial[half:], "ctx", 1).astype(f32), partial

    def collect(summed, first, last):
        size = summed.shape[0] // blocks
        result = summed[first:last]
        for b in range(1, blocks):
            other = summed[b * size + first : b * size + last].astype(bf16)
            result = result + swap(other, "ctx", 2 * b).astype(f32)
        return result.astype(bf16)

    summed, partial = visit((0, 1), (), (arrived[2], arrived[3]))
    both = collect(summed, 0, 2 * group)
    summed, _ = visit((2, 3), partial, ())
    summed, both = lax.optimization_barrier((summed, both))
    returned = [both[:group], swap(both[group:], "ep", fast), None, None]
    third = collect(summed, group, 2 * group)
    summed, third = lax.optimization_barrier((summed, third))
    returned[3] = swap(third, "ep", 3 * fast)
    returned[2] = swap(collect(summed, 0, group), "ep", 2 * fast)

    def weighted(shares, rows):
        high = shares.astype(bf16)
        low = (shares - high.astype(f32)).astype(bf16)
        out = jnp.dot(jnp.concatenate([high, low]), rows, preferred_element_type=f32)
        return out[: shares.shape[0]] + out[shares.shape[0] :]

    cut = lambda k: mixing[:, k * group : (k + 1) * group]
    total = weighted(
        jnp.concatenate([cut(0), cut(1), cut(3)], axis=1),
        jnp.concatenate([returned[0], returned[1], returned[3]]),
    )
    mine = lambda a: lax.dynamic_index_in_dim(
        a.reshape((fast, token_count) + a.shape[1:]), near, 0, False
    )
    result = mine(hidden_state) + mine(total)
    shares, rows = [mine(cut(2))], [returned[2]]
    own_ids, own_slots, own_weights = mine(expert_ids.reshape(block, 2)), mine(slots.reshape(block, 2)), mine(weights.reshape(block, 2))
    for k in range(1, fast):
        other = lax.dynamic_index_in_dim(
            total.reshape(fast, token_count, model), near ^ k, 0, False
        )
        result = result + swap(other.astype(bf16), "ep", k).astype(f32)
        theirs = lax.dynamic_slice_in_dim(returned[2], (near ^ k) * capacity, capacity, 0)
        rows.append(swap(theirs, "ep", k))
        named = own_ids == (far ^ 2) * fast + (near ^ k)
        there = named[..., None] & (
            own_slots[..., None] == jnp.arange(capacity, dtype=jnp.int32)
        )
        shares.append(jnp.sum(jnp.where(there, own_weights[..., None], 0.0), axis=1))
    result = result + weighted(jnp.concatenate(shares, axis=1), jnp.concatenate(rows))
    return result.astype(bf16).reshape(residual.shape)


def solution(mesh):
    return jax.shard_map(
        shards,
        mesh=mesh,
        in_specs=(
            P("ctx", None, "ep"),
            P("ctx", None, "ep"),
            P("ctx", None, "ep"),
            P("ep", None, "ctx"),
            P("ep"),
            P("ep", "ctx"),
            P(("ctx", "ep"), None, None),
            P(),
            P(),
            P("ep", None, "ctx"),
            P("ep", None, "ctx"),
            P("ep", "ctx", None),
            P(("ctx", "ep"), None, None),
        ),
        out_specs=P(("ctx", "ep"), None, None),
        check_vma=False,
    )
```

time: 236 us -> 221 us (0.936)
  waiting for transfers between devices: 113 us -> 84.1 us
  local copies, waits for them, and re-layouts: 4.19 us -> 11.6 us
  Pallas kernels: 0 us -> 6.07 us
  starting transfers between devices: 45.4 us -> 50.7 us
  matrix products: 47.5 us -> 43.3 us
    ppermute x26 -> x30, waiting for transfers between devices: 113 us -> 84.1 us  [swap(): return lax.ppermute(array, axis, [(i, i ^ mask) for i in range(size)])]
    unnamed x28 -> x37, local copies, waits for them, and re-layouts: 0.73 us -> 6.84 us
    pallas_call x0 -> x2, Pallas kernels: none -> 6.07 us  [the longest x1 3.75 us: attention(): pl.pallas_call(functools.partial(within_kernel, heads, size), out_shape=(...]
    ppermute x2, starting transfers between devices: 4.75 us -> 10.5 us  [turned(): return lax.ppermute(out_weight, ('ctx', 'ep'), pairs)]
    dot_general x2, matrix products: 10 us -> 6.51 us  [experts(): up_out = jnp.dot(rows, up_weight, preferred_element_type=f32)]
    ppermute x26 -> x30, starting transfers between devices: 40.7 us -> 40.2 us  [swap(): return lax.ppermute(array, axis, [(i, i ^ mask) for i in range(size)])]
    all_gather x2 -> x1, blocking collectives: 16.8 us -> 16.4 us  [attention(): states = lax.all_gather(state, 'ctx')]
  transfers between devices with their start and end apart: 28 -> 32, of which waited for: 14 -> 16; matrix products, arithmetic and copies ran while one was open for 23% -> 25% of each run, Pallas kernels for 0% -> 3%
where the time goes in v2:
time: 221 us; the launch traced here: 220 us
  waiting for transfers between devices  84.1 us (38%)
  starting transfers between devices  50.7 us (23%)
  matrix products  43.3 us (20%)
  blocking collectives  16.4 us (7%)
  local copies, waits for them, and re-layouts  11.6 us (5%)
  other arithmetic  7.49 us (3%)
  Pallas kernels  6.07 us (3%)
    ppermute x30, waiting for transfers between devices, swap(): return lax.ppermute(array, axis, [(i, i ^ mask) for i in range(size)])  84.1 us
    ppermute x30, starting transfers between devices, swap(): return lax.ppermute(array, axis, [(i, i ^ mask) for i in range(size)])  40.2 us
    dot_general x2, matrix products, experts(): return jnp.dot(hidden, down_weight, preferred_element_type=f32).astype(bf16)  16.6 us
    all_gather x1, blocking collectives, attention(): states = lax.all_gather(state, 'ctx')  16.4 us
    dot_general x2, matrix products, experts(): gate_out = jnp.dot(rows, gate_weight, preferred_element_type=f32)  14.1 us
    ppermute x2, starting transfers between devices, turned(): return lax.ppermute(out_weight, ('ctx', 'ep'), pairs)  10.5 us
    unnamed x37, local copies, waits for them, and re-layouts  6.84 us
    dot_general x2, matrix products, experts(): up_out = jnp.dot(rows, up_weight, preferred_element_type=f32)  6.51 us
  transfers between devices with their start and end apart: 32, of which 16 were waited for; matrix products, arithmetic and copies ran while one was open for 25% of the time, Pallas kernels for 3%

profile of v2, /device:TPU:0, one launch (start us, length us, event | category | flops | bytes accessed | tf_op | source)
XLA Modules:
  0.0 220.4 jit_solution(4921813134968017443)
XLA Ops:
  0.0 7.5 %collective-permute-start.3 = (bf16[256,1536]{1,0:T(8,128)(2,1)}, bf16[256,1536]{1,0:T(8,128)(2,1)}, u32[]{:S(2)}, u32[]{:S(2)}) collective-permute-start(bf16[256,1536]{1,0:T(8,128)(2,1)} %param.18), channel_id=1, source_target_pairs={{0,0},{1,8},{2,2},{3,10},{4,4},{5,12},{6,6},{7,14},{8,1},{9,9},{10... | collective-permute-start | bytes 2359304 | tf_op jit(solution)/shard_map/ppermute | solution.py:153
  7.5 3.0 %collective-permute-start.6 = (bf16[256,1536]{1,0:T(8,128)(2,1)}, bf16[256,1536]{1,0:T(8,128)(2,1)}, u32[]{:S(2)}, u32[]{:S(2)}) collective-permute-start(bf16[256,1536]{1,0:T(8,128)(2,1)} %param.18), channel_id=1, source_target_pairs={{0,16},{1,24},{2,18},{3,26},{4,20},{5,28},{6,22},{7,30},{8,17},{9,... | collective-permute-start | bytes 2359304 | tf_op jit(solution)/shard_map/ppermute | solution.py:153
  11.8 3.7 %within_block.1 = (f32[256,256]{1,0:T(8,128)}, f32[256,256]{1,0:T(8,128)}, bf16[288,128]{1,0:T(8,128)(2,1)}) custom-call(bf16[256,256]{1,0:T(8,128)(2,1)} %bitcast.106, bf16[256,256]{1,0:T(8,128)(2,1)} %bitcast.107, bf16[256,256]{1,0:T(8,128)(2,1)} %bitcast.108, f32[2,256]{1,0:T(2,128)} %bitcast.115), custom_call_target="tpu_custom_call" | custom-call | tf_op jit(solution)/shard_map/within_block/pallas_call | solution.py:92
  15.5 16.4 %all-gather = bf16[1152,128]{1,0:T(8,128)(2,1)} all-gather(bf16[288,128]{1,0:T(8,128)(2,1)} %get-tuple-element.29), channel_id=2, replica_groups=mesh['ctx'=4,'ep'=8] {'ctx'}, dimensions={0}, use_global_device_ids=true | all-gather | bytes 368640 | tf_op jit(solution)/shard_map/all_gather | solution.py:101
  32.0 2.3 %across_blocks.1 = bf16[256,256]{1,0:T(8,128)(2,1)} custom-call(s32[1]{0:T(128)} %bitcast.2.place_ref, bf16[4,288,128]{2,1,0:T(8,128)(2,1)} %bitcast.98, f32[256,256]{1,0:T(8,128)} %get-tuple-element.30.inside_ref, f32[256,256]{1,0:T(8,128)} %get-tuple-element.31.query_ref, f32[1,256]{1,0:T(1,128)} %bitcast.119), custom_call_target="tpu_custom_call" | custom-call | tf_op jit(solution)/shard_map/across_blocks/pallas_call | solution.py:104
  37.1 3.7 %collective-permute-done = bf16[256,256]{1,0:T(8,128)(2,1)S(1)} collective-permute-done((bf16[256,256]{1,0:T(8,128)(2,1)}, bf16[256,256]{1,0:T(8,128)(2,1)S(1)}, u32[]{:S(2)}, u32[]{:S(2)}) %collective-permute-start) | collective-permute-done | bytes 131104 | tf_op jit(solution)/shard_map/ppermute | solution.py:19
  49.3 8.7 %collective-permute-done.5 = bf16[128,1536]{1,0:T(8,128)(2,1)S(1)} collective-permute-done((bf16[128,1536]{1,0:T(8,128)(2,1)S(1)}, bf16[128,1536]{1,0:T(8,128)(2,1)S(1)}, u32[]{:S(2)}, u32[]{:S(2)}) %collective-permute-start.5) | collective-permute-done | bytes 393248 | tf_op jit(solution)/shard_map/ppermute | solution.py:19
  62.0 3.0 %collective-permute-start.11 = (bf16[64,1536]{1,0:T(8,128)(2,1)}, bf16[64,1536]{1,0:T(8,128)(2,1)S(1)}, u32[]{:S(2)}, u32[]{:S(2)}) collective-permute-start(bf16[64,1536]{1,0:T(8,128)(2,1)} %slice.185), channel_id=1, source_target_pairs={{0,4},{1,5},{2,6},{3,7},{4,0},{5,1},{6,2},{7,3},{8,12},{9,13},{10,... | collective-permute-start | bytes 589832 | tf_op jit(solution)/shard_map/ppermute | solution.py:19
  64.9 4.6 %collective-permute-done.8 = bf16[128,1536]{1,0:T(8,128)(2,1)} collective-permute-done((bf16[128,1536]{1,0:T(8,128)(2,1)}, bf16[128,1536]{1,0:T(8,128)(2,1)}, u32[]{:S(2)}, u32[]{:S(2)}) %collective-permute-start.8) | collective-permute-done | bytes 393248 | tf_op jit(solution)/shard_map/ppermute | solution.py:19
  73.8 4.9 %collective-permute-done.11 = bf16[64,1536]{1,0:T(8,128)(2,1)S(1)} collective-permute-done((bf16[64,1536]{1,0:T(8,128)(2,1)}, bf16[64,1536]{1,0:T(8,128)(2,1)S(1)}, u32[]{:S(2)}, u32[]{:S(2)}) %collective-permute-start.11) | collective-permute-done | bytes 196640 | tf_op jit(solution)/shard_map/ppermute | solution.py:19
  78.8 3.5 %collective-permute-done.9 = bf16[64,1536]{1,0:T(8,128)(2,1)S(1)} collective-permute-done((bf16[64,1536]{1,0:T(8,128)(2,1)S(1)}, bf16[64,1536]{1,0:T(8,128)(2,1)S(1)}, u32[]{:S(2)}, u32[]{:S(2)}) %collective-permute-start.9) | collective-permute-done | bytes 196640 | tf_op jit(solution)/shard_map/ppermute | solution.py:19
  84.5 4.2 %collective-permute-done.10 = bf16[64,1536]{1,0:T(8,128)(2,1)S(1)} collective-permute-done((bf16[64,1536]{1,0:T(8,128)(2,1)S(1)}, bf16[64,1536]{1,0:T(8,128)(2,1)S(1)}, u32[]{:S(2)}, u32[]{:S(2)}) %collective-permute-start.10) | collective-permute-done | bytes 196640 | tf_op jit(solution)/shard_map/ppermute | solution.py:19
  94.6 3.3 %collective-permute-start.13 = (bf16[24,6144]{1,0:T(8,128)(2,1)S(1)}, bf16[24,6144]{1,0:T(8,128)(2,1)S(1)}, u32[]{:S(2)}, u32[]{:S(2)}) collective-permute-start(bf16[24,6144]{1,0:T(8,128)(2,1)S(1)} %get-tuple-element.60), channel_id=1, source_target_pairs={{0,4},{1,5},{2,6},{3,7},{4,0},{5,1},{6,2},{7,3},{8,12},{9,13},{10,... | collective-permute-start | bytes 884744 | tf_op jit(solution)/shard_map/ppermute | solution.py:19
  98.0 6.4 %collective-permute-done.14 = bf16[24,6144]{1,0:T(8,128)(2,1)S(1)} collective-permute-done((bf16[24,6144]{1,0:T(8,128)(2,1)}, bf16[24,6144]{1,0:T(8,128)(2,1)S(1)}, u32[]{:S(2)}, u32[]{:S(2)}) %collective-permute-start.14) | collective-permute-done | bytes 294944 | tf_op jit(solution)/shard_map/ppermute | solution.py:19
  104.4 2.6 %collective-permute-start.19 = (bf16[24,6144]{1,0:T(8,128)(2,1)S(1)}, bf16[24,6144]{1,0:T(8,128)(2,1)S(1)}, u32[]{:S(2)}, u32[]{:S(2)}) collective-permute-start(bf16[24,6144]{1,0:T(8,128)(2,1)S(1)} %collective-permute-done.14), channel_id=1, source_target_pairs={{0,16},{8,24},{16,0},{24,8},{1,17},{9,25},{17,1},{25,9},{2,18},{10... | collective-permute-start | bytes 884744 | tf_op jit(solution)/shard_map/ppermute | solution.py:19
  107.2 2.9 %collective-permute-start.15 = (bf16[24,6144]{1,0:T(8,128)(2,1)S(1)}, bf16[24,6144]{1,0:T(8,128)(2,1)S(1)}, u32[]{:S(2)}, u32[]{:S(2)}) collective-permute-start(bf16[24,6144]{1,0:T(8,128)(2,1)S(1)} %get-tuple-element.39), channel_id=1, source_target_pairs={{0,6},{1,7},{2,4},{3,5},{4,2},{5,3},{6,0},{7,1},{8,14},{9,15},{10,... | collective-permute-start | bytes 884744 | tf_op jit(solution)/shard_map/ppermute | solution.py:19
  110.1 7.4 %collective-permute-done.13 = bf16[24,6144]{1,0:T(8,128)(2,1)S(1)} collective-permute-done((bf16[24,6144]{1,0:T(8,128)(2,1)S(1)}, bf16[24,6144]{1,0:T(8,128)(2,1)S(1)}, u32[]{:S(2)}, u32[]{:S(2)}) %collective-permute-start.13) | collective-permute-done | bytes 294944 | tf_op jit(solution)/shard_map/ppermute | solution.py:19
  120.6 7.1 %fusion.10 = f32[192,1152]{1,0:T(8,128)S(1)} fusion(bf16[192,6144]{1,0:T(8,128)(2,1)S(1)} %constant_dynamic-update-slice_fusion.4, bf16[1,6144,1152]{2,1,0:T(8,128)(2,1)} %param.22), kind=kOutput, calls=%fused_computation.10 | convolution fusion | flops 2717908992 | bytes 17399808 | tf_op jit(solution)/shard_map/dot_general | solution.py:114
  129.6 3.3 %fusion.6 = f32[192,1152]{1,0:T(8,128)S(1)} fusion(bf16[192,6144]{1,0:T(8,128)(2,1)S(1)} %constant_dynamic-update-slice_fusion.4, bf16[1,6144,1152]{2,1,0:T(8,128)(2,1)S(1)} %bitcast.121), kind=kOutput, calls=%fused_computation.6 | convolution fusion | flops 2717908992 | bytes 17399808 | tf_op jit(solution)/shard_map/dot_general | solution.py:115
  132.9 8.3 %fusion.12 = bf16[192,6144]{1,0:T(8,128)(2,1)S(1)} fusion(bf16[1,1152,6144]{2,1,0:T(8,128)(2,1)} %param.24, f32[192,1152]{1,0:T(8,128)S(1)} %fusion.6, f32[192,1152]{1,0:T(8,128)S(1)} %fusion.10), kind=kOutput, calls=%fused_computation.12 | convolution fusion | flops 2720415744 | bytes 18284544 | tf_op jit(solution)/shard_map/dot_general | solution.py:117
  142.2 3.8 %collective-permute-done.21 = bf16[96,6144]{1,0:T(8,128)(2,1)S(1)} collective-permute-done((bf16[96,6144]{1,0:T(8,128)(2,1)S(1)}, bf16[96,6144]{1,0:T(8,128)(2,1)S(1)}, u32[]{:S(2)}, u32[]{:S(2)}) %collective-permute-start.21) | collective-permute-done | bytes 1179680 | tf_op jit(solution)/shard_map/ppermute | solution.py:19
  146.0 3.2 %fusion.4 = f32[192,1152]{1,0:T(8,128)S(1)} fusion(bf16[192,6144]{1,0:T(8,128)(2,1)S(1)} %constant_dynamic-update-slice_fusion.9, bf16[1,6144,1152]{2,1,0:T(8,128)(2,1)S(1)} %bitcast.121), kind=kOutput, calls=%fused_computation.4 | convolution fusion | flops 2717908992 | bytes 17399808 | tf_op jit(solution)/shard_map/dot_general | solution.py:115
  149.3 7.0 %fusion.8 = f32[192,1152]{1,0:T(8,128)S(1)} fusion(bf16[192,6144]{1,0:T(8,128)(2,1)S(1)} %constant_dynamic-update-slice_fusion.9, bf16[1,6144,1152]{2,1,0:T(8,128)(2,1)} %param.22), kind=kOutput, calls=%fused_computation.8 | convolution fusion | flops 2717908992 | bytes 17399808 | tf_op jit(solution)/shard_map/dot_general | solution.py:114
  158.7 8.3 %fusion.15 = bf16[192,6144]{1,0:T(8,128)(2,1)S(1)} fusion(bf16[1,1152,6144]{2,1,0:T(8,128)(2,1)} %param.24, f32[192,1152]{1,0:T(8,128)S(1)} %fusion.4, f32[192,1152]{1,0:T(8,128)S(1)} %fusion.8), kind=kOutput, calls=%fused_computation.13 | convolution fusion | flops 2720415744 | bytes 18284544 | tf_op jit(solution)/shard_map/dot_general | solution.py:117
  167.2 5.1 %collective-permute-done.24 = bf16[48,6144]{1,0:T(8,128)(2,1)S(1)} collective-permute-done((bf16[48,6144]{1,0:T(8,128)(2,1)S(1)}, bf16[48,6144]{1,0:T(8,128)(2,1)S(1)}, u32[]{:S(2)}, u32[]{:S(2)}) %collective-permute-start.24) | collective-permute-done | bytes 589856 | tf_op jit(solution)/shard_map/ppermute | solution.py:19
  174.6 2.7 %collective-permute-start.25 = (bf16[24,6144]{1,0:T(8,128)(2,1)S(1)}, bf16[24,6144]{1,0:T(8,128)(2,1)S(1)}, u32[]{:S(2)}, u32[]{:S(2)}) collective-permute-start(bf16[24,6144]{1,0:T(8,128)(2,1)S(1)} %get-tuple-element.64), channel_id=1, source_target_pairs={{0,2},{1,3},{2,0},{3,1},{4,6},{5,7},{6,4},{7,5},{8,10},{9,11},{10,... | collective-permute-start | bytes 884744 | tf_op jit(solution)/shard_map/ppermute | solution.py:19
  177.3 4.1 %collective-permute-done.26 = bf16[24,6144]{1,0:T(8,128)(2,1)S(1)} collective-permute-done((bf16[24,6144]{1,0:T(8,128)(2,1)S(1)}, bf16[24,6144]{1,0:T(8,128)(2,1)S(1)}, u32[]{:S(2)}, u32[]{:S(2)}) %collective-permute-start.26) | collective-permute-done | bytes 294944 | tf_op jit(solution)/shard_map/ppermute | solution.py:19
  181.5 2.7 %collective-permute-start.27 = (bf16[24,6144]{1,0:T(8,128)(2,1)S(1)}, bf16[24,6144]{1,0:T(8,128)(2,1)S(1)}, u32[]{:S(2)}, u32[]{:S(2)}) collective-permute-start(bf16[24,6144]{1,0:T(8,128)(2,1)S(1)} %add_convert_fusion.1), channel_id=1, source_target_pairs={{0,6},{1,7},{2,4},{3,5},{4,2},{5,3},{6,0},{7,1},{8,14},{9,15},{10,... | collective-permute-start | bytes 884744 | tf_op jit(solution)/shard_map/ppermute | solution.py:19
  186.1 5.9 %collective-permute-done.27 = bf16[24,6144]{1,0:T(8,128)(2,1)S(1)} collective-permute-done((bf16[24,6144]{1,0:T(8,128)(2,1)S(1)}, bf16[24,6144]{1,0:T(8,128)(2,1)S(1)}, u32[]{:S(2)}, u32[]{:S(2)}) %collective-permute-start.27) | collective-permute-done | bytes 294944 | tf_op jit(solution)/shard_map/ppermute | solution.py:19
  192.8 6.6 %collective-permute-start.30 = (bf16[24,6144]{1,0:T(8,128)(2,1)S(1)}, bf16[24,6144]{1,0:T(8,128)(2,1)S(1)}, u32[]{:S(2)}, u32[]{:S(2)}) collective-permute-start(bf16[24,6144]{1,0:T(8,128)(2,1)S(1)} %add_convert_fusion), channel_id=1, source_target_pairs={{0,4},{1,5},{2,6},{3,7},{4,0},{5,1},{6,2},{7,3},{8,12},{9,13},{10,... | collective-permute-start | bytes 884744 | tf_op jit(solution)/shard_map/ppermute | solution.py:19
  199.6 13.0 %collective-permute-done.30 = bf16[24,6144]{1,0:T(8,128)(2,1)S(1)} collective-permute-done((bf16[24,6144]{1,0:T(8,128)(2,1)S(1)}, bf16[24,6144]{1,0:T(8,128)(2,1)S(1)}, u32[]{:S(2)}, u32[]{:S(2)}) %collective-permute-start.30) | collective-permute-done | bytes 294944 | tf_op jit(solution)/shard_map/ppermute | solution.py:19
  213.0 6.0 %collective-permute-done.31 = bf16[12,6144]{1,0:T(8,128)(2,1)S(1)} collective-permute-done((bf16[12,6144]{1,0:T(8,128)(2,1)S(1)}, bf16[12,6144]{1,0:T(8,128)(2,1)S(1)}, u32[]{:S(2)}, u32[]{:S(2)}) %collective-permute-start.31) | collective-permute-done | bytes 147488 | tf_op jit(solution)/shard_map/ppermute | solution.py:19
  (161 shorter events, 44.2 us)
Async XLA Ops:
  0.0 36.8 %collective-permute-start.3 = (bf16[256,1536]{1,0:T(8,128)(2,1)}, bf16[256,1536]{1,0:T(8,128)(2,1)}, u32[]{:S(2)}, u32[]{:S(2)}) collective-permute-start(bf16[256,1536]{1,0:T(8,128)(2,1)} %param.18), channel_id=1, source_target_pairs={{0,0},{1,8},{2,2},{3,10},{4,4},{5,12},{6,6},{7,14},{8,1},{9,9},{10... | collective-permute-start | bytes 2359304 | tf_op jit(solution)/shard_map/ppermute | solution.py:153
  7.5 34.3 %collective-permute-start.6 = (bf16[256,1536]{1,0:T(8,128)(2,1)}, bf16[256,1536]{1,0:T(8,128)(2,1)}, u32[]{:S(2)}, u32[]{:S(2)}) collective-permute-start(bf16[256,1536]{1,0:T(8,128)(2,1)} %param.18), channel_id=1, source_target_pairs={{0,16},{1,24},{2,18},{3,26},{4,20},{5,28},{6,22},{7,30},{8,17},{9,... | collective-permute-start | bytes 2359304 | tf_op jit(solution)/shard_map/ppermute | solution.py:153
  34.3 6.5 %collective-permute-start = (bf16[256,256]{1,0:T(8,128)(2,1)}, bf16[256,256]{1,0:T(8,128)(2,1)S(1)}, u32[]{:S(2)}, u32[]{:S(2)}) collective-permute-start(bf16[256,256]{1,0:T(8,128)(2,1)} %across_blocks.1), channel_id=1, source_target_pairs={{0,1},{1,0},{2,3},{3,2},{4,5},{5,4},{6,7},{7,6},{8,9},{9,8},{10,11... | collective-permute-start | bytes 393224 | tf_op jit(solution)/shard_map/ppermute | solution.py:19
  34.8 14.5 %collective-permute-start.2 = (bf16[32,6144]{1,0:T(8,128)(2,1)}, bf16[32,6144]{1,0:T(8,128)(2,1)}, u32[]{:S(2)}, u32[]{:S(2)}) collective-permute-start(bf16[32,6144]{1,0:T(8,128)(2,1)} %bitcast.104), channel_id=1, source_target_pairs={{0,1},{1,0},{2,3},{3,2},{4,5},{5,4},{6,7},{7,6},{8,9},{9,8},{10,11... | collective-permute-start | bytes 1179656 | tf_op jit(solution)/shard_map/ppermute | solution.py:19
  36.3 13.0 %collective-permute-start.1 = (s32[32,2]{0,1:T(2,128)}, s32[32,2]{0,1:T(2,128)S(1)}, u32[]{:S(2)}, u32[]{:S(2)}) collective-permute-start(s32[32,2]{0,1:T(2,128)} %bitcast.117), channel_id=1, source_target_pairs={{0,1},{1,0},{2,3},{3,2},{4,5},{5,4},{6,7},{7,6},{8,9},{9,8},{10,11... | collective-permute-start | bytes 776 | tf_op jit(solution)/shard_map/ppermute | solution.py:19
  36.9 7.5 %collective-permute-start.4 = (bf16[256,1536]{1,0:T(8,128)(2,1)}, bf16[256,1536]{1,0:T(8,128)(2,1)}, u32[]{:S(2)}, u32[]{:S(2)}) collective-permute-start(bf16[256,1536]{1,0:T(8,128)(2,1)} %collective-permute-done.3), channel_id=1, source_target_pairs={{0,8},{8,0},{16,24},{24,16},{1,9},{9,1},{17,25},{25,17},{2,10},{10... | collective-permute-start | bytes 2359304 | tf_op jit(solution)/shard_map/ppermute | solution.py:19
  41.9 6.2 %collective-permute-start.7 = (bf16[256,1536]{1,0:T(8,128)(2,1)}, bf16[256,1536]{1,0:T(8,128)(2,1)S(1)}, u32[]{:S(2)}, u32[]{:S(2)}) collective-permute-start(bf16[256,1536]{1,0:T(8,128)(2,1)} %collective-permute-done.6), channel_id=1, source_target_pairs={{0,8},{8,0},{16,24},{24,16},{1,9},{9,1},{17,25},{25,17},{2,10},{10... | collective-permute-start | bytes 2359304 | tf_op jit(solution)/shard_map/ppermute | solution.py:19
  45.9 12.1 %collective-permute-start.5 = (bf16[128,1536]{1,0:T(8,128)(2,1)S(1)}, bf16[128,1536]{1,0:T(8,128)(2,1)S(1)}, u32[]{:S(2)}, u32[]{:S(2)}) collective-permute-start(bf16[128,1536]{1,0:T(8,128)(2,1)S(1)} %convolution_convert_fusion.2), channel_id=1, source_target_pairs={{0,2},{1,3},{2,0},{3,1},{4,6},{5,7},{6,4},{7,5},{8,10},{9,11},{10,... | collective-permute-start | bytes 1179656 | tf_op jit(solution)/shard_map/ppermute | solution.py:19
  49.3 20.3 %collective-permute-start.8 = (bf16[128,1536]{1,0:T(8,128)(2,1)}, bf16[128,1536]{1,0:T(8,128)(2,1)}, u32[]{:S(2)}, u32[]{:S(2)}) collective-permute-start(bf16[128,1536]{1,0:T(8,128)(2,1)} %convolution_convert_fusion.1), channel_id=1, source_target_pairs={{0,2},{1,3},{2,0},{3,1},{4,6},{5,7},{6,4},{7,5},{8,10},{9,11},{10,... | collective-permute-start | bytes 1179656 | tf_op jit(solution)/shard_map/ppermute | solution.py:19
  62.0 16.7 %collective-permute-start.11 = (bf16[64,1536]{1,0:T(8,128)(2,1)}, bf16[64,1536]{1,0:T(8,128)(2,1)S(1)}, u32[]{:S(2)}, u32[]{:S(2)}) collective-permute-start(bf16[64,1536]{1,0:T(8,128)(2,1)} %slice.185), channel_id=1, source_target_pairs={{0,4},{1,5},{2,6},{3,7},{4,0},{5,1},{6,2},{7,3},{8,12},{9,13},{10,... | collective-permute-start | bytes 589832 | tf_op jit(solution)/shard_map/ppermute | solution.py:19
  71.0 11.3 %collective-permute-start.9 = (bf16[64,1536]{1,0:T(8,128)(2,1)S(1)}, bf16[64,1536]{1,0:T(8,128)(2,1)S(1)}, u32[]{:S(2)}, u32[]{:S(2)}) collective-permute-start(bf16[64,1536]{1,0:T(8,128)(2,1)S(1)} %slice.186), channel_id=1, source_target_pairs={{0,4},{1,5},{2,6},{3,7},{4,0},{5,1},{6,2},{7,3},{8,12},{9,13},{10,... | collective-permute-start | bytes 589832 | tf_op jit(solution)/shard_map/ppermute | solution.py:19
  78.7 5.7 %collective-permute-start.12 = (bf16[64,1536]{1,0:T(8,128)(2,1)S(1)}, bf16[64,1536]{1,0:T(8,128)(2,1)S(1)}, u32[]{:S(2)}, u32[]{:S(2)}) collective-permute-start(bf16[64,1536]{1,0:T(8,128)(2,1)S(1)} %fusion.78), channel_id=1, source_target_pairs={{0,1},{1,0},{2,3},{3,2},{4,5},{5,4},{6,7},{7,6},{8,9},{9,8},{10,11... | collective-permute-start | bytes 589832 | tf_op jit(solution)/shard_map/ppermute | solution.py:19
  82.3 6.4 %collective-permute-start.10 = (bf16[64,1536]{1,0:T(8,128)(2,1)S(1)}, bf16[64,1536]{1,0:T(8,128)(2,1)S(1)}, u32[]{:S(2)}, u32[]{:S(2)}) collective-permute-start(bf16[64,1536]{1,0:T(8,128)(2,1)S(1)} %fusion.77), channel_id=1, source_target_pairs={{0,1},{1,0},{2,3},{3,2},{4,5},{5,4},{6,7},{7,6},{8,9},{9,8},{10,11... | collective-permute-start | bytes 589832 | tf_op jit(solution)/shard_map/ppermute | solution.py:19
  91.8 12.7 %collective-permute-start.14 = (bf16[24,6144]{1,0:T(8,128)(2,1)}, bf16[24,6144]{1,0:T(8,128)(2,1)S(1)}, u32[]{:S(2)}, u32[]{:S(2)}) collective-permute-start(bf16[24,6144]{1,0:T(8,128)(2,1)} %get-tuple-element.58), channel_id=1, source_target_pairs={{0,2},{1,3},{2,0},{3,1},{4,6},{5,7},{6,4},{7,5},{8,10},{9,11},{10,... | collective-permute-start | bytes 884744 | tf_op jit(solution)/shard_map/ppermute | solution.py:19
  93.1 24.4 %collective-permute-start.18 = (bf16[24,6144]{1,0:T(8,128)(2,1)S(1)}, bf16[24,6144]{1,0:T(8,128)(2,1)S(1)}, u32[]{:S(2)}, u32[]{:S(2)}) collective-permute-start(bf16[24,6144]{1,0:T(8,128)(2,1)S(1)} %get-tuple-element.40), channel_id=1, source_target_pairs={{0,16},{8,24},{16,0},{24,8},{1,17},{9,25},{17,1},{25,9},{2,18},{10... | collective-permute-start | bytes 884744 | tf_op jit(solution)/shard_map/ppermute | solution.py:19
  94.6 22.9 %collective-permute-start.13 = (bf16[24,6144]{1,0:T(8,128)(2,1)S(1)}, bf16[24,6144]{1,0:T(8,128)(2,1)S(1)}, u32[]{:S(2)}, u32[]{:S(2)}) collective-permute-start(bf16[24,6144]{1,0:T(8,128)(2,1)S(1)} %get-tuple-element.60), channel_id=1, source_target_pairs={{0,4},{1,5},{2,6},{3,7},{4,0},{5,1},{6,2},{7,3},{8,12},{9,13},{10,... | collective-permute-start | bytes 884744 | tf_op jit(solution)/shard_map/ppermute | solution.py:19
  104.4 13.0 %collective-permute-start.19 = (bf16[24,6144]{1,0:T(8,128)(2,1)S(1)}, bf16[24,6144]{1,0:T(8,128)(2,1)S(1)}, u32[]{:S(2)}, u32[]{:S(2)}) collective-permute-start(bf16[24,6144]{1,0:T(8,128)(2,1)S(1)} %collective-permute-done.14), channel_id=1, source_target_pairs={{0,16},{8,24},{16,0},{24,8},{1,17},{9,25},{17,1},{25,9},{2,18},{10... | collective-permute-start | bytes 884744 | tf_op jit(solution)/shard_map/ppermute | solution.py:19
  107.2 10.5 %collective-permute-start.15 = (bf16[24,6144]{1,0:T(8,128)(2,1)S(1)}, bf16[24,6144]{1,0:T(8,128)(2,1)S(1)}, u32[]{:S(2)}, u32[]{:S(2)}) collective-permute-start(bf16[24,6144]{1,0:T(8,128)(2,1)S(1)} %get-tuple-element.39), channel_id=1, source_target_pairs={{0,6},{1,7},{2,4},{3,5},{4,2},{5,3},{6,0},{7,1},{8,14},{9,15},{10,... | collective-permute-start | bytes 884744 | tf_op jit(solution)/shard_map/ppermute | solution.py:19
  117.5 24.1 %collective-permute-start.16 = (bf16[24,6144]{1,0:T(8,128)(2,1)S(1)}, bf16[24,6144]{1,0:T(8,128)(2,1)S(1)}, u32[]{:S(2)}, u32[]{:S(2)}) collective-permute-start(bf16[24,6144]{1,0:T(8,128)(2,1)S(1)} %collective-permute-done.13), channel_id=1, source_target_pairs={{0,16},{8,24},{16,0},{24,8},{1,17},{9,25},{17,1},{25,9},{2,18},{10... | collective-permute-start | bytes 884744 | tf_op jit(solution)/shard_map/ppermute | solution.py:19
  117.6 2.9 %collective-permute-start.20 = (bf16[96,6144]{1,0:T(8,128)(2,1)S(1)}, bf16[96,6144]{1,0:T(8,128)(2,1)S(1)}, u32[]{:S(2)}, u32[]{:S(2)}) collective-permute-start(bf16[96,6144]{1,0:T(8,128)(2,1)S(1)} %pad_maximum_fusion), channel_id=1, source_target_pairs={{0,8},{8,0},{16,24},{24,16},{1,9},{9,1},{17,25},{25,17},{2,10},{10... | collective-permute-start | bytes 3538952 | tf_op jit(solution)/shard_map/ppermute | solution.py:19
  117.7 23.8 %collective-permute-start.17 = (bf16[24,6144]{1,0:T(8,128)(2,1)S(1)}, bf16[24,6144]{1,0:T(8,128)(2,1)S(1)}, u32[]{:S(2)}, u32[]{:S(2)}) collective-permute-start(bf16[24,6144]{1,0:T(8,128)(2,1)S(1)} %collective-permute-done.15), channel_id=1, source_target_pairs={{0,16},{8,24},{16,0},{24,8},{1,17},{9,25},{17,1},{25,9},{2,18},{10... | collective-permute-start | bytes 884744 | tf_op jit(solution)/shard_map/ppermute | solution.py:19
  141.3 14.9 %collective-permute-start.23 = (bf16[96,6144]{1,0:T(8,128)(2,1)S(1)}, bf16[96,6144]{1,0:T(8,128)(2,1)S(1)}, u32[]{:S(2)}, u32[]{:S(2)}) collective-permute-start(bf16[96,6144]{1,0:T(8,128)(2,1)S(1)} %slice.128), channel_id=1, source_target_pairs={{0,8},{8,0},{16,24},{24,16},{1,9},{9,1},{17,25},{25,17},{2,10},{10... | collective-permute-start | bytes 3538952 | tf_op jit(solution)/shard_map/ppermute | solution.py:19
  141.7 4.3 %collective-permute-start.21 = (bf16[96,6144]{1,0:T(8,128)(2,1)S(1)}, bf16[96,6144]{1,0:T(8,128)(2,1)S(1)}, u32[]{:S(2)}, u32[]{:S(2)}) collective-permute-start(bf16[96,6144]{1,0:T(8,128)(2,1)S(1)} %pad_maximum_fusion.1), channel_id=1, source_target_pairs={{0,8},{8,0},{16,24},{24,16},{1,9},{9,1},{17,25},{25,17},{2,10},{10... | collective-permute-start | bytes 3538952 | tf_op jit(solution)/shard_map/ppermute | solution.py:19
  156.6 15.7 %collective-permute-start.24 = (bf16[48,6144]{1,0:T(8,128)(2,1)S(1)}, bf16[48,6144]{1,0:T(8,128)(2,1)S(1)}, u32[]{:S(2)}, u32[]{:S(2)}) collective-permute-start(bf16[48,6144]{1,0:T(8,128)(2,1)S(1)} %slice.182), channel_id=1, source_target_pairs={{0,16},{8,24},{16,0},{24,8},{1,17},{9,25},{17,1},{25,9},{2,18},{10... | collective-permute-start | bytes 1769480 | tf_op jit(solution)/shard_map/ppermute | solution.py:19
  167.1 5.3 %collective-permute-start.22 = (bf16[96,6144]{1,0:T(8,128)(2,1)S(1)}, bf16[96,6144]{1,0:T(8,128)(2,1)S(1)}, u32[]{:S(2)}, u32[]{:S(2)}) collective-permute-start(bf16[96,6144]{1,0:T(8,128)(2,1)S(1)} %slice.126), channel_id=1, source_target_pairs={{0,8},{8,0},{16,24},{24,16},{1,9},{9,1},{17,25},{25,17},{2,10},{10... | collective-permute-start | bytes 3538952 | tf_op jit(solution)/shard_map/ppermute | solution.py:19
  172.8 8.6 %collective-permute-start.26 = (bf16[24,6144]{1,0:T(8,128)(2,1)S(1)}, bf16[24,6144]{1,0:T(8,128)(2,1)S(1)}, u32[]{:S(2)}, u32[]{:S(2)}) collective-permute-start(bf16[24,6144]{1,0:T(8,128)(2,1)S(1)} %slice.184), channel_id=1, source_target_pairs={{0,16},{8,24},{16,0},{24,8},{1,17},{9,25},{17,1},{25,9},{2,18},{10... | collective-permute-start | bytes 884744 | tf_op jit(solution)/shard_map/ppermute | solution.py:19
  174.6 11.4 %collective-permute-start.25 = (bf16[24,6144]{1,0:T(8,128)(2,1)S(1)}, bf16[24,6144]{1,0:T(8,128)(2,1)S(1)}, u32[]{:S(2)}, u32[]{:S(2)}) collective-permute-start(bf16[24,6144]{1,0:T(8,128)(2,1)S(1)} %get-tuple-element.64), channel_id=1, source_target_pairs={{0,2},{1,3},{2,0},{3,1},{4,6},{5,7},{6,4},{7,5},{8,10},{9,11},{10,... | collective-permute-start | bytes 884744 | tf_op jit(solution)/shard_map/ppermute | solution.py:19
  181.5 10.5 %collective-permute-start.27 = (bf16[24,6144]{1,0:T(8,128)(2,1)S(1)}, bf16[24,6144]{1,0:T(8,128)(2,1)S(1)}, u32[]{:S(2)}, u32[]{:S(2)}) collective-permute-start(bf16[24,6144]{1,0:T(8,128)(2,1)S(1)} %add_convert_fusion.1), channel_id=1, source_target_pairs={{0,6},{1,7},{2,4},{3,5},{4,2},{5,3},{6,0},{7,1},{8,14},{9,15},{10,... | collective-permute-start | bytes 884744 | tf_op jit(solution)/shard_map/ppermute | solution.py:19
  184.4 8.3 %collective-permute-start.29 = (bf16[24,6144]{1,0:T(8,128)(2,1)S(1)}, bf16[24,6144]{1,0:T(8,128)(2,1)S(1)}, u32[]{:S(2)}, u32[]{:S(2)}) collective-permute-start(bf16[24,6144]{1,0:T(8,128)(2,1)S(1)} %slice.183), channel_id=1, source_target_pairs={{0,16},{8,24},{16,0},{24,8},{1,17},{9,25},{17,1},{25,9},{2,18},{10... | collective-permute-start | bytes 884744 | tf_op jit(solution)/shard_map/ppermute | solution.py:19
  192.8 19.7 %collective-permute-start.30 = (bf16[24,6144]{1,0:T(8,128)(2,1)S(1)}, bf16[24,6144]{1,0:T(8,128)(2,1)S(1)}, u32[]{:S(2)}, u32[]{:S(2)}) collective-permute-start(bf16[24,6144]{1,0:T(8,128)(2,1)S(1)} %add_convert_fusion), channel_id=1, source_target_pairs={{0,4},{1,5},{2,6},{3,7},{4,0},{5,1},{6,2},{7,3},{8,12},{9,13},{10,... | collective-permute-start | bytes 884744 | tf_op jit(solution)/shard_map/ppermute | solution.py:19
  199.4 20.0 %collective-permute-start.28 = (bf16[32,6144]{1,0:T(8,128)(2,1)S(1)}, bf16[32,6144]{1,0:T(8,128)(2,1)S(1)}, u32[]{:S(2)}, u32[]{:S(2)}) collective-permute-start(bf16[32,6144]{1,0:T(8,128)(2,1)S(1)} %fusion.40), channel_id=1, source_target_pairs={{0,1},{1,0},{2,3},{3,2},{4,5},{5,4},{6,7},{7,6},{8,9},{9,8},{10,11... | collective-permute-start | bytes 1179656 | tf_op jit(solution)/shard_map/ppermute | solution.py:19
  212.6 6.4 %collective-permute-start.31 = (bf16[12,6144]{1,0:T(8,128)(2,1)S(1)}, bf16[12,6144]{1,0:T(8,128)(2,1)S(1)}, u32[]{:S(2)}, u32[]{:S(2)}) collective-permute-start(bf16[12,6144]{1,0:T(8,128)(2,1)S(1)} %constant_dynamic-slice_fusion), channel_id=1, source_target_pairs={{0,1},{1,0},{2,3},{3,2},{4,5},{5,4},{6,7},{7,6},{8,9},{9,8},{10,11... | collective-permute-start | bytes 442376 | tf_op jit(solution)/shard_map/ppermute | solution.py:19
  (13 other events, 190.8 us)

commit v3 on v2

--- a/solution.py
+++ b/solution.py
@@ -84,7 +84,7 @@
         ).astype(bf16)
 
 
-def attention(queries, keys_in, values_in, log_decay, attn_gain):
+def attention(queries, keys_in, values_in, log_decay, attn_gain, beside):
     length, sequences, width = queries.shape
     heads = log_decay.shape[0]
     size = width // heads
@@ -98,7 +98,7 @@
         ),
         name="within_block",
     )(flat(queries), flat(keys_in), flat(values_in), log_decay.reshape(heads, length))
-    states = lax.all_gather(state, "ctx")
+    states, beside = lax.optimization_barrier((lax.all_gather(state, "ctx"), beside))
     place = lax.axis_index("ctx").astype(jnp.int32).reshape(1)
     vmem = pl.BlockSpec(memory_space=pltpu.VMEM)
     return pl.pallas_call(
@@ -107,7 +107,7 @@
         out_specs=vmem,
         out_shape=jax.ShapeDtypeStruct((length, width), bf16),
         name="across_blocks",
-    )(place, states, inside, query, attn_gain.reshape(1, width))
+    )(place, states, inside, query, attn_gain.reshape(1, width)), beside
 
 
 def experts(rows, gate_weight, up_weight, down_weight):
@@ -142,29 +142,31 @@
     model = residual.shape[-1]
     columns = out_weight.shape[1]
 
-    def turned(a):
+    def turned(rows, a):
         pairs = []
         for h in range(high):
             for low in range(fast):
                 for o in range(outer):
                     for n in range(fast):
                         source = (h * fast + low) * n_ep + o * fast + n
-                        pairs.append((source, ((h ^ a) * fast + n) * n_ep + o * fast + low))
-        return lax.ppermute(out_weight, ("ctx", "ep"), pairs)
-
-    pieces = []
-    for a in range(high):
-        mine = turned(a)
-        pieces.append(
-            jnp.concatenate([mine] + [swap(mine, "ctx", j) for j in range(1, fast)], axis=0)
-        )
+                        goal = ((h ^ a) * fast + n) * n_ep + o * fast + low
+                        if source != goal:
+                            pairs.append((source, goal))
+        return lax.ppermute(rows, ("ctx", "ep"), pairs)
+
+    soon = [turned(out_weight, a) for a in range(high)]
 
     token_count = residual.shape[0] * residual.shape[1]
     own_residual = residual.reshape(token_count, model)
     own_routes = routes.reshape(token_count, 2)
-    normed_heads = attention(queries, keys_in, values_in, log_decay, attn_gain)
+    normed_heads, soon = attention(queries, keys_in, values_in, log_decay, attn_gain, soon)
+    soon[0] = jnp.where(lower == near, out_weight, soon[0])
+    pieces = [
+        jnp.concatenate([mine] + [swap(mine, "ctx", j) for j in range(1, fast)], axis=0)
+        for mine in soon
+    ]
     heads = jnp.stack([normed_heads] + [swap(normed_heads, "ep", k) for k in range(1, fast)])
-    own_residual, own_routes, _ = lax.optimization_barrier((own_residual, own_routes, heads))
+    own_residual, own_routes, heads = lax.optimization_barrier((own_residual, own_routes, heads))
     near_residual = [own_residual] + [swap(own_residual, "ep", k) for k in range(1, fast)]
     near_routes = [own_routes] + [swap(own_routes, "ep", k) for k in range(1, fast)]
     heads = jnp.concatenate(
@@ -188,8 +190,11 @@
             )
             near_routes = absolute(near_routes, near)
             near_residual = absolute(near_residual, near)
+        else:
+            came, earlier = lax.optimization_barrier((came, earlier))
         total = jnp.dot(kept, pieces[a], preferred_element_type=f32) + came.astype(f32)
         came = swap(total[block:].astype(bf16), "ep", 2 * fast)
+        earlier = came
         total = total[:block] + came.astype(f32)
         narrow = total.astype(bf16)
         attn.extend([total] + [swap(narrow, "ep", k).astype(f32) for k in range(1, fast)])

time: 221 us -> 211 us (0.955)
  starting transfers between devices: 50.7 us -> 42.1 us
    ppermute x2, starting transfers between devices: 10.5 us -> 3.86 us  [turned(): return lax.ppermute(rows, ('ctx', 'ep'), pairs)]
    unnamed x37 -> x32, local copies, waits for them, and re-layouts: 6.84 us -> 4.14 us
    ppermute x30, waiting for transfers between devices: 84.1 us -> 81.9 us  [swap(): return lax.ppermute(array, axis, [(i, i ^ mask) for i in range(size)])]
    all_gather x1, blocking collectives: 16.4 us -> 14.2 us  [attention(): lax.all_gather(state, 'ctx')]
  transfers between devices with their start and end apart: 32 -> 32, of which waited for: 16 -> 15; matrix products, arithmetic and copies ran while one was open for 25% -> 26% of each run, Pallas kernels for 3% -> 3%
where the time goes in v3:
time: 211 us; the launch traced here: 210 us
  waiting for transfers between devices  81.9 us (39%)
  matrix products  44.6 us (21%)
  starting transfers between devices  42.1 us (20%)
  blocking collectives  14.2 us (7%)
  local copies, waits for them, and re-layouts  11.3 us (5%)
  other arithmetic  9.29 us (4%)
  Pallas kernels  6.06 us (3%)
    ppermute x30, waiting for transfers between devices, swap(): return lax.ppermute(array, axis, [(i, i ^ mask) for i in range(size)])  81.9 us
    ppermute x30, starting transfers between devices, swap(): return lax.ppermute(array, axis, [(i, i ^ mask) for i in range(size)])  38.2 us
    dot_general x2, matrix products, experts(): return jnp.dot(hidden, down_weight, preferred_element_type=f32).astype(bf16)  16.6 us
    all_gather x1, blocking collectives, attention(): lax.all_gather(state, 'ctx')  14.2 us
    dot_general x2, matrix products, experts(): gate_out = jnp.dot(rows, gate_weight, preferred_element_type=f32)  14.1 us
    dot_general x2, matrix products, experts(): up_out = jnp.dot(rows, up_weight, preferred_element_type=f32)  6.46 us
  transfers between devices with their start and end apart: 32, of which 15 were waited for; matrix products, arithmetic and copies ran while one was open for 26% of the time, Pallas kernels for 3%

profile of v3, /device:TPU:0, one launch (start us, length us, event | category | flops | bytes accessed | tf_op | source)
XLA Modules:
  0.0 210.0 jit_solution(9172688709987964058)
XLA Ops:
  0.8 3.0 %collective-permute-start.1 = (bf16[256,1536]{1,0:T(8,128)(2,1)}, bf16[256,1536]{1,0:T(8,128)(2,1)S(1)}, u32[]{:S(2)}, u32[]{:S(2)}) collective-permute-start(bf16[256,1536]{1,0:T(8,128)(2,1)} %param.18), channel_id=1, source_target_pairs={{0,16},{1,24},{2,18},{3,26},{4,20},{5,28},{6,22},{7,30},{8,17},{9,... | collective-permute-start | bytes 2359304 | tf_op jit(solution)/shard_map/ppermute | solution.py:155
  5.1 3.7 %within_block.1 = (f32[256,256]{1,0:T(8,128)}, f32[256,256]{1,0:T(8,128)}, bf16[288,128]{1,0:T(8,128)(2,1)}) custom-call(bf16[256,256]{1,0:T(8,128)(2,1)} %bitcast.104, bf16[256,256]{1,0:T(8,128)(2,1)} %bitcast.105, bf16[256,256]{1,0:T(8,128)(2,1)} %bitcast.106, f32[2,256]{1,0:T(2,128)} %bitcast.113), custom_call_target="tpu_custom_call" | custom-call | tf_op jit(solution)/shard_map/within_block/pallas_call | solution.py:92
  8.9 14.2 %all-gather = bf16[1152,128]{1,0:T(8,128)(2,1)} all-gather(bf16[288,128]{1,0:T(8,128)(2,1)} %get-tuple-element.34), channel_id=2, replica_groups=mesh['ctx'=4,'ep'=8] {'ctx'}, dimensions={0}, use_global_device_ids=true | all-gather | bytes 368640 | tf_op jit(solution)/shard_map/all_gather | solution.py:101
  25.7 2.3 %across_blocks.1 = bf16[256,256]{1,0:T(8,128)(2,1)} custom-call(s32[1]{0:T(128)} %bitcast.2.place_ref, bf16[4,288,128]{2,1,0:T(8,128)(2,1)} %bitcast.96, f32[256,256]{1,0:T(8,128)} %get-tuple-element.36.inside_ref, f32[256,256]{1,0:T(8,128)} %get-tuple-element.37.query_ref, f32[1,256]{1,0:T(1,128)} %bitcast.117), custom_call_target="tpu_custom_call" | custom-call | tf_op jit(solution)/shard_map/across_blocks/pallas_call | solution.py:104
  28.0 4.5 %collective-permute-start.2 = (bf16[256,256]{1,0:T(8,128)(2,1)}, bf16[256,256]{1,0:T(8,128)(2,1)S(1)}, u32[]{:S(2)}, u32[]{:S(2)}) collective-permute-start(bf16[256,256]{1,0:T(8,128)(2,1)} %across_blocks.1), channel_id=1, source_target_pairs={{0,1},{1,0},{2,3},{3,2},{4,5},{5,4},{6,7},{7,6},{8,9},{9,8},{10,11... | collective-permute-start | bytes 393224 | tf_op jit(solution)/shard_map/ppermute | solution.py:19
  32.5 4.2 %collective-permute-done.2 = bf16[256,256]{1,0:T(8,128)(2,1)S(1)} collective-permute-done((bf16[256,256]{1,0:T(8,128)(2,1)}, bf16[256,256]{1,0:T(8,128)(2,1)S(1)}, u32[]{:S(2)}, u32[]{:S(2)}) %collective-permute-start.2) | collective-permute-done | bytes 131104 | tf_op jit(solution)/shard_map/ppermute | solution.py:19
  37.7 1.8 collective-permute-start.4
  45.8 3.1 %collective-permute-done.3 = s32[32,2]{0,1:T(2,128)S(1)} collective-permute-done((s32[32,2]{0,1:T(2,128)S(1)}, s32[32,2]{0,1:T(2,128)S(1)}, u32[]{:S(2)}, u32[]{:S(2)}) %collective-permute-start.3) | collective-permute-done | bytes 288 | tf_op jit(solution)/shard_map/ppermute | solution.py:19
  49.0 4.6 %collective-permute-done.6 = bf16[128,1536]{1,0:T(8,128)(2,1)S(1)} collective-permute-done((bf16[128,1536]{1,0:T(8,128)(2,1)S(1)}, bf16[128,1536]{1,0:T(8,128)(2,1)S(1)}, u32[]{:S(2)}, u32[]{:S(2)}) %collective-permute-start.6) | collective-permute-done | bytes 393248 | tf_op jit(solution)/shard_map/ppermute | solution.py:19
  58.3 2.6 %collective-permute-start.9 = (bf16[64,1536]{1,0:T(8,128)(2,1)}, bf16[64,1536]{1,0:T(8,128)(2,1)S(1)}, u32[]{:S(2)}, u32[]{:S(2)}) collective-permute-start(bf16[64,1536]{1,0:T(8,128)(2,1)} %slice.186), channel_id=1, source_target_pairs={{0,4},{1,5},{2,6},{3,7},{4,0},{5,1},{6,2},{7,3},{8,12},{9,13},{10,... | collective-permute-start | bytes 589832 | tf_op jit(solution)/shard_map/ppermute | solution.py:19
  65.5 3.4 %collective-permute-done.9 = bf16[64,1536]{1,0:T(8,128)(2,1)S(1)} collective-permute-done((bf16[64,1536]{1,0:T(8,128)(2,1)}, bf16[64,1536]{1,0:T(8,128)(2,1)S(1)}, u32[]{:S(2)}, u32[]{:S(2)}) %collective-permute-start.9) | collective-permute-done | bytes 196640 | tf_op jit(solution)/shard_map/ppermute | solution.py:19
  72.1 5.8 %collective-permute-done.10 = bf16[64,1536]{1,0:T(8,128)(2,1)S(1)} collective-permute-done((bf16[64,1536]{1,0:T(8,128)(2,1)S(1)}, bf16[64,1536]{1,0:T(8,128)(2,1)S(1)}, u32[]{:S(2)}, u32[]{:S(2)}) %collective-permute-start.10) | collective-permute-done | bytes 196640 | tf_op jit(solution)/shard_map/ppermute | solution.py:19
  77.9 2.8 %collective-permute-start.11 = (bf16[64,1536]{1,0:T(8,128)(2,1)S(1)}, bf16[64,1536]{1,0:T(8,128)(2,1)S(1)}, u32[]{:S(2)}, u32[]{:S(2)}) collective-permute-start(bf16[64,1536]{1,0:T(8,128)(2,1)S(1)} %fusion.75), channel_id=1, source_target_pairs={{0,1},{1,0},{2,3},{3,2},{4,5},{5,4},{6,7},{7,6},{8,9},{9,8},{10,11... | collective-permute-start | bytes 589832 | tf_op jit(solution)/shard_map/ppermute | solution.py:19
  80.9 3.5 %collective-permute-done.11 = bf16[64,1536]{1,0:T(8,128)(2,1)S(1)} collective-permute-done((bf16[64,1536]{1,0:T(8,128)(2,1)S(1)}, bf16[64,1536]{1,0:T(8,128)(2,1)S(1)}, u32[]{:S(2)}, u32[]{:S(2)}) %collective-permute-start.11) | collective-permute-done | bytes 196640 | tf_op jit(solution)/shard_map/ppermute | solution.py:19
  88.0 2.5 %collective-permute-start.13 = (bf16[24,6144]{1,0:T(8,128)(2,1)S(1)}, bf16[24,6144]{1,0:T(8,128)(2,1)S(1)}, u32[]{:S(2)}, u32[]{:S(2)}) collective-permute-start(bf16[24,6144]{1,0:T(8,128)(2,1)S(1)} %get-tuple-element.70), channel_id=1, source_target_pairs={{0,4},{1,5},{2,6},{3,7},{4,0},{5,1},{6,2},{7,3},{8,12},{9,13},{10,... | collective-permute-start | bytes 884744 | tf_op jit(solution)/shard_map/ppermute | solution.py:19
  90.6 6.9 %collective-permute-done.14 = bf16[24,6144]{1,0:T(8,128)(2,1)S(1)} collective-permute-done((bf16[24,6144]{1,0:T(8,128)(2,1)}, bf16[24,6144]{1,0:T(8,128)(2,1)S(1)}, u32[]{:S(2)}, u32[]{:S(2)}) %collective-permute-start.14) | collective-permute-done | bytes 294944 | tf_op jit(solution)/shard_map/ppermute | solution.py:19
  98.2 3.5 %collective-permute-start.15 = (bf16[24,6144]{1,0:T(8,128)(2,1)S(1)}, bf16[24,6144]{1,0:T(8,128)(2,1)S(1)}, u32[]{:S(2)}, u32[]{:S(2)}) collective-permute-start(bf16[24,6144]{1,0:T(8,128)(2,1)S(1)} %get-tuple-element.49), channel_id=1, source_target_pairs={{0,6},{1,7},{2,4},{3,5},{4,2},{5,3},{6,0},{7,1},{8,14},{9,15},{10,... | collective-permute-start | bytes 884744 | tf_op jit(solution)/shard_map/ppermute | solution.py:19
  101.7 6.3 %collective-permute-done.13 = bf16[24,6144]{1,0:T(8,128)(2,1)S(1)} collective-permute-done((bf16[24,6144]{1,0:T(8,128)(2,1)S(1)}, bf16[24,6144]{1,0:T(8,128)(2,1)S(1)}, u32[]{:S(2)}, u32[]{:S(2)}) %collective-permute-start.13) | collective-permute-done | bytes 294944 | tf_op jit(solution)/shard_map/ppermute | solution.py:19
  112.3 7.1 %fusion.10 = f32[192,1152]{1,0:T(8,128)S(1)} fusion(bf16[192,6144]{1,0:T(8,128)(2,1)S(1)} %constant_dynamic-update-slice_fusion.2, bf16[1,6144,1152]{2,1,0:T(8,128)(2,1)} %param.22), kind=kOutput, calls=%fused_computation.10 | convolution fusion | flops 2717908992 | bytes 17399808 | tf_op jit(solution)/shard_map/dot_general | solution.py:114
  121.3 3.2 %fusion.6 = f32[192,1152]{1,0:T(8,128)S(1)} fusion(bf16[192,6144]{1,0:T(8,128)(2,1)S(1)} %constant_dynamic-update-slice_fusion.2, bf16[1,6144,1152]{2,1,0:T(8,128)(2,1)S(1)} %bitcast.119), kind=kOutput, calls=%fused_computation.6 | convolution fusion | flops 2717908992 | bytes 17399808 | tf_op jit(solution)/shard_map/dot_general | solution.py:115
  124.6 8.3 %fusion.12 = bf16[192,6144]{1,0:T(8,128)(2,1)S(1)} fusion(bf16[1,1152,6144]{2,1,0:T(8,128)(2,1)} %param.24, f32[192,1152]{1,0:T(8,128)S(1)} %fusion.6, f32[192,1152]{1,0:T(8,128)S(1)} %fusion.10), kind=kOutput, calls=%fused_computation.12 | convolution fusion | flops 2720415744 | bytes 18284544 | tf_op jit(solution)/shard_map/dot_general | solution.py:117
  133.8 3.8 %collective-permute-done.21 = bf16[96,6144]{1,0:T(8,128)(2,1)S(1)} collective-permute-done((bf16[96,6144]{1,0:T(8,128)(2,1)S(1)}, bf16[96,6144]{1,0:T(8,128)(2,1)S(1)}, u32[]{:S(2)}, u32[]{:S(2)}) %collective-permute-start.21) | collective-permute-done | bytes 1179680 | tf_op jit(solution)/shard_map/ppermute | solution.py:19
  137.7 3.2 %fusion.4 = f32[192,1152]{1,0:T(8,128)S(1)} fusion(bf16[192,6144]{1,0:T(8,128)(2,1)S(1)} %constant_dynamic-update-slice_fusion.7, bf16[1,6144,1152]{2,1,0:T(8,128)(2,1)S(1)} %bitcast.119), kind=kOutput, calls=%fused_computation.4 | convolution fusion | flops 2717908992 | bytes 17399808 | tf_op jit(solution)/shard_map/dot_general | solution.py:115
  140.9 7.0 %fusion.8 = f32[192,1152]{1,0:T(8,128)S(1)} fusion(bf16[192,6144]{1,0:T(8,128)(2,1)S(1)} %constant_dynamic-update-slice_fusion.7, bf16[1,6144,1152]{2,1,0:T(8,128)(2,1)} %param.22), kind=kOutput, calls=%fused_computation.8 | convolution fusion | flops 2717908992 | bytes 17399808 | tf_op jit(solution)/shard_map/dot_general | solution.py:114
  149.2 8.3 %fusion.15 = bf16[192,6144]{1,0:T(8,128)(2,1)S(1)} fusion(bf16[1,1152,6144]{2,1,0:T(8,128)(2,1)} %param.24, f32[192,1152]{1,0:T(8,128)S(1)} %fusion.4, f32[192,1152]{1,0:T(8,128)S(1)} %fusion.8), kind=kOutput, calls=%fused_computation.13 | convolution fusion | flops 2720415744 | bytes 18284544 | tf_op jit(solution)/shard_map/dot_general | solution.py:117
  157.7 6.0 %collective-permute-done.24 = bf16[48,6144]{1,0:T(8,128)(2,1)S(1)} collective-permute-done((bf16[48,6144]{1,0:T(8,128)(2,1)S(1)}, bf16[48,6144]{1,0:T(8,128)(2,1)S(1)}, u32[]{:S(2)}, u32[]{:S(2)}) %collective-permute-start.24) | collective-permute-done | bytes 589856 | tf_op jit(solution)/shard_map/ppermute | solution.py:19
  165.9 6.5 %collective-permute-done.26 = bf16[24,6144]{1,0:T(8,128)(2,1)S(1)} collective-permute-done((bf16[24,6144]{1,0:T(8,128)(2,1)S(1)}, bf16[24,6144]{1,0:T(8,128)(2,1)S(1)}, u32[]{:S(2)}, u32[]{:S(2)}) %collective-permute-start.26) | collective-permute-done | bytes 294944 | tf_op jit(solution)/shard_map/ppermute | solution.py:19
  173.8 8.1 %collective-permute-done.27 = bf16[24,6144]{1,0:T(8,128)(2,1)S(1)} collective-permute-done((bf16[24,6144]{1,0:T(8,128)(2,1)S(1)}, bf16[24,6144]{1,0:T(8,128)(2,1)S(1)}, u32[]{:S(2)}, u32[]{:S(2)}) %collective-permute-start.27) | collective-permute-done | bytes 294944 | tf_op jit(solution)/shard_map/ppermute | solution.py:19
  182.6 5.7 %collective-permute-start.30 = (bf16[24,6144]{1,0:T(8,128)(2,1)S(1)}, bf16[24,6144]{1,0:T(8,128)(2,1)S(1)}, u32[]{:S(2)}, u32[]{:S(2)}) collective-permute-start(bf16[24,6144]{1,0:T(8,128)(2,1)S(1)} %add_convert_fusion), channel_id=1, source_target_pairs={{0,4},{1,5},{2,6},{3,7},{4,0},{5,1},{6,2},{7,3},{8,12},{9,13},{10,... | collective-permute-start | bytes 884744 | tf_op jit(solution)/shard_map/ppermute | solution.py:19
  188.4 2.0 collective-permute-start.28
  190.3 11.5 %collective-permute-done.30 = bf16[24,6144]{1,0:T(8,128)(2,1)S(1)} collective-permute-done((bf16[24,6144]{1,0:T(8,128)(2,1)S(1)}, bf16[24,6144]{1,0:T(8,128)(2,1)S(1)}, u32[]{:S(2)}, u32[]{:S(2)}) %collective-permute-start.30) | collective-permute-done | bytes 294944 | tf_op jit(solution)/shard_map/ppermute | solution.py:19
  202.3 6.3 %collective-permute-done.31 = bf16[12,6144]{1,0:T(8,128)(2,1)S(1)} collective-permute-done((bf16[12,6144]{1,0:T(8,128)(2,1)S(1)}, bf16[12,6144]{1,0:T(8,128)(2,1)S(1)}, u32[]{:S(2)}, u32[]{:S(2)}) %collective-permute-start.31) | collective-permute-done | bytes 147488 | tf_op jit(solution)/shard_map/ppermute | solution.py:19
  (157 shorter events, 43.4 us)
Async XLA Ops:
  0.0 23.1 %collective-permute-start = (bf16[256,1536]{1,0:T(8,128)(2,1)}, bf16[256,1536]{1,0:T(8,128)(2,1)S(1)}, u32[]{:S(2)}, u32[]{:S(2)}) collective-permute-start(bf16[256,1536]{1,0:T(8,128)(2,1)} %param.18), channel_id=1, source_target_pairs={{1,8},{3,10},{5,12},{7,14},{8,1},{10,3},{12,5},{14,7},{17,24},{19,... | collective-permute-start | bytes 2359304 | tf_op jit(solution)/shard_map/ppermute | solution.py:155
  0.8 22.3 %collective-permute-start.1 = (bf16[256,1536]{1,0:T(8,128)(2,1)}, bf16[256,1536]{1,0:T(8,128)(2,1)S(1)}, u32[]{:S(2)}, u32[]{:S(2)}) collective-permute-start(bf16[256,1536]{1,0:T(8,128)(2,1)} %param.18), channel_id=1, source_target_pairs={{0,16},{1,24},{2,18},{3,26},{4,20},{5,28},{6,22},{7,30},{8,17},{9,... | collective-permute-start | bytes 2359304 | tf_op jit(solution)/shard_map/ppermute | solution.py:155
  24.3 15.6 %collective-permute-start.5 = (bf16[256,1536]{1,0:T(8,128)(2,1)S(1)}, bf16[256,1536]{1,0:T(8,128)(2,1)}, u32[]{:S(2)}, u32[]{:S(2)}) collective-permute-start(bf16[256,1536]{1,0:T(8,128)(2,1)S(1)} %broadcast_select_fusion), channel_id=1, source_target_pairs={{0,8},{8,0},{16,24},{24,16},{1,9},{9,1},{17,25},{25,17},{2,10},{10... | collective-permute-start | bytes 2359304 | tf_op jit(solution)/shard_map/ppermute | solution.py:19
  24.5 18.6 %collective-permute-start.7 = (bf16[256,1536]{1,0:T(8,128)(2,1)S(1)}, bf16[256,1536]{1,0:T(8,128)(2,1)}, u32[]{:S(2)}, u32[]{:S(2)}) collective-permute-start(bf16[256,1536]{1,0:T(8,128)(2,1)S(1)} %collective-permute-done.1), channel_id=1, source_target_pairs={{0,8},{8,0},{16,24},{24,16},{1,9},{9,1},{17,25},{25,17},{2,10},{10... | collective-permute-start | bytes 2359304 | tf_op jit(solution)/shard_map/ppermute | solution.py:19
  28.0 8.8 %collective-permute-start.2 = (bf16[256,256]{1,0:T(8,128)(2,1)}, bf16[256,256]{1,0:T(8,128)(2,1)S(1)}, u32[]{:S(2)}, u32[]{:S(2)}) collective-permute-start(bf16[256,256]{1,0:T(8,128)(2,1)} %across_blocks.1), channel_id=1, source_target_pairs={{0,1},{1,0},{2,3},{3,2},{4,5},{5,4},{6,7},{7,6},{8,9},{9,8},{10,11... | collective-permute-start | bytes 393224 | tf_op jit(solution)/shard_map/ppermute | solution.py:19
  37.7 11.3 %collective-permute-start.4 = (bf16[32,6144]{1,0:T(8,128)(2,1)}, bf16[32,6144]{1,0:T(8,128)(2,1)}, u32[]{:S(2)}, u32[]{:S(2)}) collective-permute-start(bf16[32,6144]{1,0:T(8,128)(2,1)} %bitcast.102), channel_id=1, source_target_pairs={{0,1},{1,0},{2,3},{3,2},{4,5},{5,4},{6,7},{7,6},{8,9},{9,8},{10,11... | collective-permute-start | bytes 1179656 | tf_op jit(solution)/shard_map/ppermute | solution.py:19
  39.5 9.4 %collective-permute-start.3 = (s32[32,2]{0,1:T(2,128)S(1)}, s32[32,2]{0,1:T(2,128)S(1)}, u32[]{:S(2)}, u32[]{:S(2)}) collective-permute-start(s32[32,2]{0,1:T(2,128)S(1)} %bitcast.115), channel_id=1, source_target_pairs={{0,1},{1,0},{2,3},{3,2},{4,5},{5,4},{6,7},{7,6},{8,9},{9,8},{10,11... | collective-permute-start | bytes 776 | tf_op jit(solution)/shard_map/ppermute | solution.py:19
  41.4 12.1 %collective-permute-start.6 = (bf16[128,1536]{1,0:T(8,128)(2,1)S(1)}, bf16[128,1536]{1,0:T(8,128)(2,1)S(1)}, u32[]{:S(2)}, u32[]{:S(2)}) collective-permute-start(bf16[128,1536]{1,0:T(8,128)(2,1)S(1)} %convolution_convert_fusion.2), channel_id=1, source_target_pairs={{0,2},{1,3},{2,0},{3,1},{4,6},{5,7},{6,4},{7,5},{8,10},{9,11},{10,... | collective-permute-start | bytes 1179656 | tf_op jit(solution)/shard_map/ppermute | solution.py:19
  45.4 20.1 %collective-permute-start.8 = (bf16[128,1536]{1,0:T(8,128)(2,1)}, bf16[128,1536]{1,0:T(8,128)(2,1)}, u32[]{:S(2)}, u32[]{:S(2)}) collective-permute-start(bf16[128,1536]{1,0:T(8,128)(2,1)} %convolution_convert_fusion.1), channel_id=1, source_target_pairs={{0,2},{1,3},{2,0},{3,1},{4,6},{5,7},{6,4},{7,5},{8,10},{9,11},{10,... | collective-permute-start | bytes 1179656 | tf_op jit(solution)/shard_map/ppermute | solution.py:19
  58.3 10.7 %collective-permute-start.9 = (bf16[64,1536]{1,0:T(8,128)(2,1)}, bf16[64,1536]{1,0:T(8,128)(2,1)S(1)}, u32[]{:S(2)}, u32[]{:S(2)}) collective-permute-start(bf16[64,1536]{1,0:T(8,128)(2,1)} %slice.186), channel_id=1, source_target_pairs={{0,4},{1,5},{2,6},{3,7},{4,0},{5,1},{6,2},{7,3},{8,12},{9,13},{10,... | collective-permute-start | bytes 589832 | tf_op jit(solution)/shard_map/ppermute | solution.py:19
  70.4 7.5 %collective-permute-start.10 = (bf16[64,1536]{1,0:T(8,128)(2,1)S(1)}, bf16[64,1536]{1,0:T(8,128)(2,1)S(1)}, u32[]{:S(2)}, u32[]{:S(2)}) collective-permute-start(bf16[64,1536]{1,0:T(8,128)(2,1)S(1)} %slice.185), channel_id=1, source_target_pairs={{0,4},{1,5},{2,6},{3,7},{4,0},{5,1},{6,2},{7,3},{8,12},{9,13},{10,... | collective-permute-start | bytes 589832 | tf_op jit(solution)/shard_map/ppermute | solution.py:19
  70.5 10.4 %collective-permute-start.12 = (bf16[64,1536]{1,0:T(8,128)(2,1)S(1)}, bf16[64,1536]{1,0:T(8,128)(2,1)S(1)}, u32[]{:S(2)}, u32[]{:S(2)}) collective-permute-start(bf16[64,1536]{1,0:T(8,128)(2,1)S(1)} %fusion.76), channel_id=1, source_target_pairs={{0,1},{1,0},{2,3},{3,2},{4,5},{5,4},{6,7},{7,6},{8,9},{9,8},{10,11... | collective-permute-start | bytes 589832 | tf_op jit(solution)/shard_map/ppermute | solution.py:19
  77.9 6.5 %collective-permute-start.11 = (bf16[64,1536]{1,0:T(8,128)(2,1)S(1)}, bf16[64,1536]{1,0:T(8,128)(2,1)S(1)}, u32[]{:S(2)}, u32[]{:S(2)}) collective-permute-start(bf16[64,1536]{1,0:T(8,128)(2,1)S(1)} %fusion.75), channel_id=1, source_target_pairs={{0,1},{1,0},{2,3},{3,2},{4,5},{5,4},{6,7},{7,6},{8,9},{9,8},{10,11... | collective-permute-start | bytes 589832 | tf_op jit(solution)/shard_map/ppermute | solution.py:19
  87.0 10.5 %collective-permute-start.14 = (bf16[24,6144]{1,0:T(8,128)(2,1)}, bf16[24,6144]{1,0:T(8,128)(2,1)S(1)}, u32[]{:S(2)}, u32[]{:S(2)}) collective-permute-start(bf16[24,6144]{1,0:T(8,128)(2,1)} %get-tuple-element.68), channel_id=1, source_target_pairs={{0,2},{1,3},{2,0},{3,1},{4,6},{5,7},{6,4},{7,5},{8,10},{9,11},{10,... | collective-permute-start | bytes 884744 | tf_op jit(solution)/shard_map/ppermute | solution.py:19
  87.2 22.0 %collective-permute-start.18 = (bf16[24,6144]{1,0:T(8,128)(2,1)S(1)}, bf16[24,6144]{1,0:T(8,128)(2,1)S(1)}, u32[]{:S(2)}, u32[]{:S(2)}) collective-permute-start(bf16[24,6144]{1,0:T(8,128)(2,1)S(1)} %get-tuple-element.50), channel_id=1, source_target_pairs={{0,16},{8,24},{16,0},{24,8},{1,17},{9,25},{17,1},{25,9},{2,18},{10... | collective-permute-start | bytes 884744 | tf_op jit(solution)/shard_map/ppermute | solution.py:19
  88.0 20.0 %collective-permute-start.13 = (bf16[24,6144]{1,0:T(8,128)(2,1)S(1)}, bf16[24,6144]{1,0:T(8,128)(2,1)S(1)}, u32[]{:S(2)}, u32[]{:S(2)}) collective-permute-start(bf16[24,6144]{1,0:T(8,128)(2,1)S(1)} %get-tuple-element.70), channel_id=1, source_target_pairs={{0,4},{1,5},{2,6},{3,7},{4,0},{5,1},{6,2},{7,3},{8,12},{9,13},{10,... | collective-permute-start | bytes 884744 | tf_op jit(solution)/shard_map/ppermute | solution.py:19
  97.6 11.6 %collective-permute-start.19 = (bf16[24,6144]{1,0:T(8,128)(2,1)S(1)}, bf16[24,6144]{1,0:T(8,128)(2,1)S(1)}, u32[]{:S(2)}, u32[]{:S(2)}) collective-permute-start(bf16[24,6144]{1,0:T(8,128)(2,1)S(1)} %collective-permute-done.14), channel_id=1, source_target_pairs={{0,16},{8,24},{16,0},{24,8},{1,17},{9,25},{17,1},{25,9},{2,18},{10... | collective-permute-start | bytes 884744 | tf_op jit(solution)/shard_map/ppermute | solution.py:19
  98.2 11.2 %collective-permute-start.15 = (bf16[24,6144]{1,0:T(8,128)(2,1)S(1)}, bf16[24,6144]{1,0:T(8,128)(2,1)S(1)}, u32[]{:S(2)}, u32[]{:S(2)}) collective-permute-start(bf16[24,6144]{1,0:T(8,128)(2,1)S(1)} %get-tuple-element.49), channel_id=1, source_target_pairs={{0,6},{1,7},{2,4},{3,5},{4,2},{5,3},{6,0},{7,1},{8,14},{9,15},{10,... | collective-permute-start | bytes 884744 | tf_op jit(solution)/shard_map/ppermute | solution.py:19
  108.0 25.2 %collective-permute-start.16 = (bf16[24,6144]{1,0:T(8,128)(2,1)S(1)}, bf16[24,6144]{1,0:T(8,128)(2,1)S(1)}, u32[]{:S(2)}, u32[]{:S(2)}) collective-permute-start(bf16[24,6144]{1,0:T(8,128)(2,1)S(1)} %collective-permute-done.13), channel_id=1, source_target_pairs={{0,16},{8,24},{16,0},{24,8},{1,17},{9,25},{17,1},{25,9},{2,18},{10... | collective-permute-start | bytes 884744 | tf_op jit(solution)/shard_map/ppermute | solution.py:19
  109.3 2.9 %collective-permute-start.20 = (bf16[96,6144]{1,0:T(8,128)(2,1)S(1)}, bf16[96,6144]{1,0:T(8,128)(2,1)S(1)}, u32[]{:S(2)}, u32[]{:S(2)}) collective-permute-start(bf16[96,6144]{1,0:T(8,128)(2,1)S(1)} %pad_maximum_fusion.1), channel_id=1, source_target_pairs={{0,8},{8,0},{16,24},{24,16},{1,9},{9,1},{17,25},{25,17},{2,10},{10... | collective-permute-start | bytes 3538952 | tf_op jit(solution)/shard_map/ppermute | solution.py:19
  109.4 23.8 %collective-permute-start.17 = (bf16[24,6144]{1,0:T(8,128)(2,1)S(1)}, bf16[24,6144]{1,0:T(8,128)(2,1)S(1)}, u32[]{:S(2)}, u32[]{:S(2)}) collective-permute-start(bf16[24,6144]{1,0:T(8,128)(2,1)S(1)} %collective-permute-done.15), channel_id=1, source_target_pairs={{0,16},{8,24},{16,0},{24,8},{1,17},{9,25},{17,1},{25,9},{2,18},{10... | collective-permute-start | bytes 884744 | tf_op jit(solution)/shard_map/ppermute | solution.py:19
  133.0 14.9 %collective-permute-start.23 = (bf16[96,6144]{1,0:T(8,128)(2,1)S(1)}, bf16[96,6144]{1,0:T(8,128)(2,1)S(1)}, u32[]{:S(2)}, u32[]{:S(2)}) collective-permute-start(bf16[96,6144]{1,0:T(8,128)(2,1)S(1)} %slice.128), channel_id=1, source_target_pairs={{0,8},{8,0},{16,24},{24,16},{1,9},{9,1},{17,25},{25,17},{2,10},{10... | collective-permute-start | bytes 3538952 | tf_op jit(solution)/shard_map/ppermute | solution.py:19
  133.3 4.3 %collective-permute-start.21 = (bf16[96,6144]{1,0:T(8,128)(2,1)S(1)}, bf16[96,6144]{1,0:T(8,128)(2,1)S(1)}, u32[]{:S(2)}, u32[]{:S(2)}) collective-permute-start(bf16[96,6144]{1,0:T(8,128)(2,1)S(1)} %pad_maximum_fusion.2), channel_id=1, source_target_pairs={{0,8},{8,0},{16,24},{24,16},{1,9},{9,1},{17,25},{25,17},{2,10},{10... | collective-permute-start | bytes 3538952 | tf_op jit(solution)/shard_map/ppermute | solution.py:19
  148.3 15.4 %collective-permute-start.24 = (bf16[48,6144]{1,0:T(8,128)(2,1)S(1)}, bf16[48,6144]{1,0:T(8,128)(2,1)S(1)}, u32[]{:S(2)}, u32[]{:S(2)}) collective-permute-start(bf16[48,6144]{1,0:T(8,128)(2,1)S(1)} %slice.182), channel_id=1, source_target_pairs={{0,16},{8,24},{16,0},{24,8},{1,17},{9,25},{17,1},{25,9},{2,18},{10... | collective-permute-start | bytes 1769480 | tf_op jit(solution)/shard_map/ppermute | solution.py:19
  157.6 6.2 %collective-permute-start.22 = (bf16[96,6144]{1,0:T(8,128)(2,1)S(1)}, bf16[96,6144]{1,0:T(8,128)(2,1)S(1)}, u32[]{:S(2)}, u32[]{:S(2)}) collective-permute-start(bf16[96,6144]{1,0:T(8,128)(2,1)S(1)} %slice.126), channel_id=1, source_target_pairs={{0,8},{8,0},{16,24},{24,16},{1,9},{9,1},{17,25},{25,17},{2,10},{10... | collective-permute-start | bytes 3538952 | tf_op jit(solution)/shard_map/ppermute | solution.py:19
  164.2 8.3 %collective-permute-start.26 = (bf16[24,6144]{1,0:T(8,128)(2,1)S(1)}, bf16[24,6144]{1,0:T(8,128)(2,1)S(1)}, u32[]{:S(2)}, u32[]{:S(2)}) collective-permute-start(bf16[24,6144]{1,0:T(8,128)(2,1)S(1)} %slice.184), channel_id=1, source_target_pairs={{0,16},{8,24},{16,0},{24,8},{1,17},{9,25},{17,1},{25,9},{2,18},{10... | collective-permute-start | bytes 884744 | tf_op jit(solution)/shard_map/ppermute | solution.py:19
  165.1 8.6 %collective-permute-start.25 = (bf16[24,6144]{1,0:T(8,128)(2,1)S(1)}, bf16[24,6144]{1,0:T(8,128)(2,1)S(1)}, u32[]{:S(2)}, u32[]{:S(2)}) collective-permute-start(bf16[24,6144]{1,0:T(8,128)(2,1)S(1)} %get-tuple-element.74), channel_id=1, source_target_pairs={{0,2},{1,3},{2,0},{3,1},{4,6},{5,7},{6,4},{7,5},{8,10},{9,11},{10,... | collective-permute-start | bytes 884744 | tf_op jit(solution)/shard_map/ppermute | solution.py:19
  172.5 9.3 %collective-permute-start.27 = (bf16[24,6144]{1,0:T(8,128)(2,1)S(1)}, bf16[24,6144]{1,0:T(8,128)(2,1)S(1)}, u32[]{:S(2)}, u32[]{:S(2)}) collective-permute-start(bf16[24,6144]{1,0:T(8,128)(2,1)S(1)} %add_convert_fusion.1), channel_id=1, source_target_pairs={{0,6},{1,7},{2,4},{3,5},{4,2},{5,3},{6,0},{7,1},{8,14},{9,15},{10,... | collective-permute-start | bytes 884744 | tf_op jit(solution)/shard_map/ppermute | solution.py:19
  172.8 9.7 %collective-permute-start.29 = (bf16[24,6144]{1,0:T(8,128)(2,1)S(1)}, bf16[24,6144]{1,0:T(8,128)(2,1)S(1)}, u32[]{:S(2)}, u32[]{:S(2)}) collective-permute-start(bf16[24,6144]{1,0:T(8,128)(2,1)S(1)} %slice.183), channel_id=1, source_target_pairs={{0,16},{8,24},{16,0},{24,8},{1,17},{9,25},{17,1},{25,9},{2,18},{10... | collective-permute-start | bytes 884744 | tf_op jit(solution)/shard_map/ppermute | solution.py:19
  182.6 19.2 %collective-permute-start.30 = (bf16[24,6144]{1,0:T(8,128)(2,1)S(1)}, bf16[24,6144]{1,0:T(8,128)(2,1)S(1)}, u32[]{:S(2)}, u32[]{:S(2)}) collective-permute-start(bf16[24,6144]{1,0:T(8,128)(2,1)S(1)} %add_convert_fusion), channel_id=1, source_target_pairs={{0,4},{1,5},{2,6},{3,7},{4,0},{5,1},{6,2},{7,3},{8,12},{9,13},{10,... | collective-permute-start | bytes 884744 | tf_op jit(solution)/shard_map/ppermute | solution.py:19
  188.4 20.6 %collective-permute-start.28 = (bf16[32,6144]{1,0:T(8,128)(2,1)S(1)}, bf16[32,6144]{1,0:T(8,128)(2,1)S(1)}, u32[]{:S(2)}, u32[]{:S(2)}) collective-permute-start(bf16[32,6144]{1,0:T(8,128)(2,1)S(1)} %fusion.40), channel_id=1, source_target_pairs={{0,1},{1,0},{2,3},{3,2},{4,5},{5,4},{6,7},{7,6},{8,9},{9,8},{10,11... | collective-permute-start | bytes 1179656 | tf_op jit(solution)/shard_map/ppermute | solution.py:19
  201.9 6.7 %collective-permute-start.31 = (bf16[12,6144]{1,0:T(8,128)(2,1)S(1)}, bf16[12,6144]{1,0:T(8,128)(2,1)S(1)}, u32[]{:S(2)}, u32[]{:S(2)}) collective-permute-start(bf16[12,6144]{1,0:T(8,128)(2,1)S(1)} %constant_dynamic-slice_fusion), channel_id=1, source_target_pairs={{0,1},{1,0},{2,3},{3,2},{4,5},{5,4},{6,7},{7,6},{8,9},{9,8},{10,11... | collective-permute-start | bytes 442376 | tf_op jit(solution)/shard_map/ppermute | solution.py:19
  (11 other events, 184.0 us)

commit v4 on v3

--- a/solution.py
+++ b/solution.py
@@ -251,15 +251,18 @@
             result = result + swap(other, "ctx", 2 * b).astype(f32)
         return result.astype(bf16)
 
-    summed, partial = visit((0, 1), (), (arrived[2], arrived[3]))
-    both = collect(summed, 0, 2 * group)
+    early, partial = visit((0, 1), (), (arrived[2], arrived[3]))
+    second = collect(early, group, 2 * group)
     summed, _ = visit((2, 3), partial, ())
-    summed, both = lax.optimization_barrier((summed, both))
-    returned = [both[:group], swap(both[group:], "ep", fast), None, None]
+    summed, second = lax.optimization_barrier((summed, second))
     third = collect(summed, group, 2 * group)
-    summed, third = lax.optimization_barrier((summed, third))
-    returned[3] = swap(third, "ep", 3 * fast)
-    returned[2] = swap(collect(summed, 0, group), "ep", 2 * fast)
+    summed, early, third = lax.optimization_barrier((summed, early, third))
+    returned = [
+        collect(early, 0, group),
+        swap(second, "ep", fast),
+        swap(collect(summed, 0, group), "ep", 2 * fast),
+        swap(third, "ep", 3 * fast),
+    ]
 
     def weighted(shares, rows):
         high = shares.astype(bf16)

time: 211 us -> 201 us (0.953)
  waiting for transfers between devices: 81.9 us -> 67.8 us
  starting transfers between devices: 42.1 us -> 49.4 us
    ppermute x30 -> x31, waiting for transfers between devices: 81.9 us -> 67.8 us  [swap(): return lax.ppermute(array, axis, [(i, i ^ mask) for i in range(size)])]
    ppermute x30 -> x31, starting transfers between devices: 38.2 us -> 45.6 us  [swap(): return lax.ppermute(array, axis, [(i, i ^ mask) for i in range(size)])]
    dot_general x2, matrix products: 16.6 us -> 12.3 us  [experts(): return jnp.dot(hidden, down_weight, preferred_element_type=f32).astype(bf16)]
    dot_general x2, matrix products: 6.46 us -> 10.3 us  [experts(): up_out = jnp.dot(rows, up_weight, preferred_element_type=f32)]
  transfers between devices with their start and end apart: 32 -> 33, of which waited for: 15 -> 17; matrix products, arithmetic and copies ran while one was open for 26% -> 27% of each run, Pallas kernels for 3% -> 3%
where the time goes in v4:
time: 201 us
  waiting for transfers between devices  67.8 us (34%)
  starting transfers between devices  49.4 us (25%)
  matrix products  43.8 us (22%)
  blocking collectives  14.2 us (7%)
  local copies, waits for them, and re-layouts  9.32 us (5%)
  other arithmetic  9.3 us (5%)
  Pallas kernels  6.08 us (3%)
    ppermute x31, waiting for transfers between devices, swap(): return lax.ppermute(array, axis, [(i, i ^ mask) for i in range(size)])  67.8 us
    ppermute x31, starting transfers between devices, swap(): return lax.ppermute(array, axis, [(i, i ^ mask) for i in range(size)])  45.6 us
    all_gather x1, blocking collectives, attention(): lax.all_gather(state, 'ctx')  14.2 us
    dot_general x2, matrix products, experts(): gate_out = jnp.dot(rows, gate_weight, preferred_element_type=f32)  13.9 us
    dot_general x2, matrix products, experts(): return jnp.dot(hidden, down_weight, preferred_element_type=f32).astype(bf16)  12.3 us
    dot_general x2, matrix products, experts(): up_out = jnp.dot(rows, up_weight, preferred_element_type=f32)  10.3 us
  transfers between devices with their start and end apart: 33, of which 17 were waited for; matrix products, arithmetic and copies ran while one was open for 27% of the time, Pallas kernels for 3%

profile of v4, /device:TPU:0, one launch (start us, length us, event | category | flops | bytes accessed | tf_op | source)
XLA Modules:
  0.0 200.7 jit_solution(6226270939478786965)
XLA Ops:
  0.8 3.0 %collective-permute-start.1 = (bf16[256,1536]{1,0:T(8,128)(2,1)}, bf16[256,1536]{1,0:T(8,128)(2,1)S(1)}, u32[]{:S(2)}, u32[]{:S(2)}) collective-permute-start(bf16[256,1536]{1,0:T(8,128)(2,1)} %param.18), channel_id=1, source_target_pairs={{0,16},{1,24},{2,18},{3,26},{4,20},{5,28},{6,22},{7,30},{8,17},{9,... | collective-permute-start | bytes 2359304 | tf_op jit(solution)/shard_map/ppermute | solution.py:155
  5.1 3.8 %within_block.1 = (f32[256,256]{1,0:T(8,128)}, f32[256,256]{1,0:T(8,128)}, bf16[288,128]{1,0:T(8,128)(2,1)}) custom-call(bf16[256,256]{1,0:T(8,128)(2,1)} %bitcast.104, bf16[256,256]{1,0:T(8,128)(2,1)} %bitcast.105, bf16[256,256]{1,0:T(8,128)(2,1)} %bitcast.106, f32[2,256]{1,0:T(2,128)} %bitcast.113), custom_call_target="tpu_custom_call" | custom-call | tf_op jit(solution)/shard_map/within_block/pallas_call | solution.py:92
  8.9 14.2 %all-gather = bf16[1152,128]{1,0:T(8,128)(2,1)} all-gather(bf16[288,128]{1,0:T(8,128)(2,1)} %get-tuple-element.35), channel_id=2, replica_groups=mesh['ctx'=4,'ep'=8] {'ctx'}, dimensions={0}, use_global_device_ids=true | all-gather | bytes 368640 | tf_op jit(solution)/shard_map/all_gather | solution.py:101
  25.6 2.3 %across_blocks.1 = bf16[256,256]{1,0:T(8,128)(2,1)} custom-call(s32[1]{0:T(128)} %bitcast.2.place_ref, bf16[4,288,128]{2,1,0:T(8,128)(2,1)} %bitcast.96, f32[256,256]{1,0:T(8,128)} %get-tuple-element.37.inside_ref, f32[256,256]{1,0:T(8,128)} %get-tuple-element.38.query_ref, f32[1,256]{1,0:T(1,128)} %bitcast.117), custom_call_target="tpu_custom_call" | custom-call | tf_op jit(solution)/shard_map/across_blocks/pallas_call | solution.py:104
  28.0 4.6 %collective-permute-start.2 = (bf16[256,256]{1,0:T(8,128)(2,1)}, bf16[256,256]{1,0:T(8,128)(2,1)S(1)}, u32[]{:S(2)}, u32[]{:S(2)}) collective-permute-start(bf16[256,256]{1,0:T(8,128)(2,1)} %across_blocks.1), channel_id=1, source_target_pairs={{0,1},{1,0},{2,3},{3,2},{4,5},{5,4},{6,7},{7,6},{8,9},{9,8},{10,11... | collective-permute-start | bytes 393224 | tf_op jit(solution)/shard_map/ppermute | solution.py:19
  32.6 4.2 %collective-permute-done.2 = bf16[256,256]{1,0:T(8,128)(2,1)S(1)} collective-permute-done((bf16[256,256]{1,0:T(8,128)(2,1)}, bf16[256,256]{1,0:T(8,128)(2,1)S(1)}, u32[]{:S(2)}, u32[]{:S(2)}) %collective-permute-start.2) | collective-permute-done | bytes 131104 | tf_op jit(solution)/shard_map/ppermute | solution.py:19
  45.9 4.4 %collective-permute-done.4 = bf16[32,6144]{1,0:T(8,128)(2,1)} collective-permute-done((bf16[32,6144]{1,0:T(8,128)(2,1)}, bf16[32,6144]{1,0:T(8,128)(2,1)}, u32[]{:S(2)}, u32[]{:S(2)}) %collective-permute-start.4) | collective-permute-done | bytes 393248 | tf_op jit(solution)/shard_map/ppermute | solution.py:19
  50.3 3.3 %collective-permute-done.6 = bf16[128,1536]{1,0:T(8,128)(2,1)S(1)} collective-permute-done((bf16[128,1536]{1,0:T(8,128)(2,1)S(1)}, bf16[128,1536]{1,0:T(8,128)(2,1)S(1)}, u32[]{:S(2)}, u32[]{:S(2)}) %collective-permute-start.6) | collective-permute-done | bytes 393248 | tf_op jit(solution)/shard_map/ppermute | solution.py:19
  58.3 2.6 %collective-permute-start.9 = (bf16[64,1536]{1,0:T(8,128)(2,1)}, bf16[64,1536]{1,0:T(8,128)(2,1)S(1)}, u32[]{:S(2)}, u32[]{:S(2)}) collective-permute-start(bf16[64,1536]{1,0:T(8,128)(2,1)} %slice.191), channel_id=1, source_target_pairs={{0,4},{1,5},{2,6},{3,7},{4,0},{5,1},{6,2},{7,3},{8,12},{9,13},{10,... | collective-permute-start | bytes 589832 | tf_op jit(solution)/shard_map/ppermute | solution.py:19
  65.5 3.5 %collective-permute-done.9 = bf16[64,1536]{1,0:T(8,128)(2,1)S(1)} collective-permute-done((bf16[64,1536]{1,0:T(8,128)(2,1)}, bf16[64,1536]{1,0:T(8,128)(2,1)S(1)}, u32[]{:S(2)}, u32[]{:S(2)}) %collective-permute-start.9) | collective-permute-done | bytes 196640 | tf_op jit(solution)/shard_map/ppermute | solution.py:19
  72.2 5.9 %collective-permute-done.10 = bf16[64,1536]{1,0:T(8,128)(2,1)S(1)} collective-permute-done((bf16[64,1536]{1,0:T(8,128)(2,1)S(1)}, bf16[64,1536]{1,0:T(8,128)(2,1)S(1)}, u32[]{:S(2)}, u32[]{:S(2)}) %collective-permute-start.10) | collective-permute-done | bytes 196640 | tf_op jit(solution)/shard_map/ppermute | solution.py:19
  78.1 2.8 %collective-permute-start.11 = (bf16[64,1536]{1,0:T(8,128)(2,1)S(1)}, bf16[64,1536]{1,0:T(8,128)(2,1)S(1)}, u32[]{:S(2)}, u32[]{:S(2)}) collective-permute-start(bf16[64,1536]{1,0:T(8,128)(2,1)S(1)} %fusion.75), channel_id=1, source_target_pairs={{0,1},{1,0},{2,3},{3,2},{4,5},{5,4},{6,7},{7,6},{8,9},{9,8},{10,11... | collective-permute-start | bytes 589832 | tf_op jit(solution)/shard_map/ppermute | solution.py:19
  81.0 3.5 %collective-permute-done.11 = bf16[64,1536]{1,0:T(8,128)(2,1)S(1)} collective-permute-done((bf16[64,1536]{1,0:T(8,128)(2,1)S(1)}, bf16[64,1536]{1,0:T(8,128)(2,1)S(1)}, u32[]{:S(2)}, u32[]{:S(2)}) %collective-permute-start.11) | collective-permute-done | bytes 196640 | tf_op jit(solution)/shard_map/ppermute | solution.py:19
  86.7 2.5 %collective-permute-start.14 = (bf16[24,6144]{1,0:T(8,128)(2,1)S(1)}, bf16[24,6144]{1,0:T(8,128)(2,1)S(1)}, u32[]{:S(2)}, u32[]{:S(2)}) collective-permute-start(bf16[24,6144]{1,0:T(8,128)(2,1)S(1)} %get-tuple-element.70), channel_id=1, source_target_pairs={{0,2},{1,3},{2,0},{3,1},{4,6},{5,7},{6,4},{7,5},{8,10},{9,11},{10,... | collective-permute-start | bytes 884744 | tf_op jit(solution)/shard_map/ppermute | solution.py:19
  90.7 4.8 %collective-permute-done.14 = bf16[24,6144]{1,0:T(8,128)(2,1)S(1)} collective-permute-done((bf16[24,6144]{1,0:T(8,128)(2,1)S(1)}, bf16[24,6144]{1,0:T(8,128)(2,1)S(1)}, u32[]{:S(2)}, u32[]{:S(2)}) %collective-permute-start.14) | collective-permute-done | bytes 294944 | tf_op jit(solution)/shard_map/ppermute | solution.py:19
  96.7 3.9 %collective-permute-start.15 = (bf16[24,6144]{1,0:T(8,128)(2,1)S(1)}, bf16[24,6144]{1,0:T(8,128)(2,1)S(1)}, u32[]{:S(2)}, u32[]{:S(2)}) collective-permute-start(bf16[24,6144]{1,0:T(8,128)(2,1)S(1)} %get-tuple-element.50), channel_id=1, source_target_pairs={{0,6},{1,7},{2,4},{3,5},{4,2},{5,3},{6,0},{7,1},{8,14},{9,15},{10,... | collective-permute-start | bytes 884744 | tf_op jit(solution)/shard_map/ppermute | solution.py:19
  100.5 5.9 %collective-permute-done.13 = bf16[24,6144]{1,0:T(8,128)(2,1)S(1)} collective-permute-done((bf16[24,6144]{1,0:T(8,128)(2,1)}, bf16[24,6144]{1,0:T(8,128)(2,1)S(1)}, u32[]{:S(2)}, u32[]{:S(2)}) %collective-permute-start.13) | collective-permute-done | bytes 294944 | tf_op jit(solution)/shard_map/ppermute | solution.py:19
  109.6 7.0 %fusion.6 = f32[192,1152]{1,0:T(8,128)S(1)} fusion(bf16[192,6144]{1,0:T(8,128)(2,1)S(1)} %constant_dynamic-update-slice_fusion.2, bf16[1,6144,1152]{2,1,0:T(8,128)(2,1)} %param.23), kind=kOutput, calls=%fused_computation.6 | convolution fusion | flops 2717908992 | bytes 17399808 | tf_op jit(solution)/shard_map/dot_general | solution.py:115
  116.6 6.9 %fusion.10 = f32[192,1152]{1,0:T(8,128)S(1)} fusion(bf16[192,6144]{1,0:T(8,128)(2,1)S(1)} %constant_dynamic-update-slice_fusion.2, bf16[1,6144,1152]{2,1,0:T(8,128)(2,1)} %param.22), kind=kOutput, calls=%fused_computation.10 | convolution fusion | flops 2717908992 | bytes 17399808 | tf_op jit(solution)/shard_map/dot_general | solution.py:114
  123.6 8.5 %fusion.12 = bf16[192,6144]{1,0:T(8,128)(2,1)S(1)} fusion(bf16[1,1152,6144]{2,1,0:T(8,128)(2,1)} %param.24, f32[192,1152]{1,0:T(8,128)S(1)} %fusion.6, f32[192,1152]{1,0:T(8,128)S(1)} %fusion.10), kind=kOutput, calls=%fused_computation.12 | convolution fusion | flops 2720415744 | bytes 18284544 | tf_op jit(solution)/shard_map/dot_general | solution.py:117
  133.0 2.3 %collective-permute-done.21 = bf16[96,6144]{1,0:T(8,128)(2,1)S(1)} collective-permute-done((bf16[96,6144]{1,0:T(8,128)(2,1)S(1)}, bf16[96,6144]{1,0:T(8,128)(2,1)S(1)}, u32[]{:S(2)}, u32[]{:S(2)}) %collective-permute-start.21) | collective-permute-done | bytes 1179680 | tf_op jit(solution)/shard_map/ppermute | solution.py:19
  135.4 3.3 %fusion.4 = f32[192,1152]{1,0:T(8,128)S(1)} fusion(bf16[192,6144]{1,0:T(8,128)(2,1)S(1)} %constant_dynamic-update-slice_fusion.7, bf16[1,6144,1152]{2,1,0:T(8,128)(2,1)S(1)} %bitcast.119), kind=kOutput, calls=%fused_computation.4 | convolution fusion | flops 2717908992 | bytes 17399808 | tf_op jit(solution)/shard_map/dot_general | solution.py:115
  138.7 6.9 %fusion.8 = f32[192,1152]{1,0:T(8,128)S(1)} fusion(bf16[192,6144]{1,0:T(8,128)(2,1)S(1)} %constant_dynamic-update-slice_fusion.7, bf16[1,6144,1152]{2,1,0:T(8,128)(2,1)} %param.22), kind=kOutput, calls=%fused_computation.8 | convolution fusion | flops 2717908992 | bytes 17399808 | tf_op jit(solution)/shard_map/dot_general | solution.py:114
  148.1 3.9 %fusion.15 = bf16[192,6144]{1,0:T(8,128)(2,1)S(1)} fusion(bf16[1,1152,6144]{2,1,0:T(8,128)(2,1)S(1)} %bitcast.121, f32[192,1152]{1,0:T(8,128)S(1)} %fusion.4, f32[192,1152]{1,0:T(8,128)S(1)} %fusion.8), kind=kOutput, calls=%fused_computation.13 | convolution fusion | flops 2720415744 | bytes 18284544 | tf_op jit(solution)/shard_map/dot_general | solution.py:117
  152.1 3.3 %collective-permute-done.24 = bf16[24,6144]{1,0:T(8,128)(2,1)S(1)} collective-permute-done((bf16[24,6144]{1,0:T(8,128)(2,1)S(1)}, bf16[24,6144]{1,0:T(8,128)(2,1)S(1)}, u32[]{:S(2)}, u32[]{:S(2)}) %collective-permute-start.24) | collective-permute-done | bytes 294944 | tf_op jit(solution)/shard_map/ppermute | solution.py:19
  157.8 6.6 %collective-permute-done.25 = bf16[24,6144]{1,0:T(8,128)(2,1)S(1)} collective-permute-done((bf16[24,6144]{1,0:T(8,128)(2,1)S(1)}, bf16[24,6144]{1,0:T(8,128)(2,1)S(1)}, u32[]{:S(2)}, u32[]{:S(2)}) %collective-permute-start.25) | collective-permute-done | bytes 294944 | tf_op jit(solution)/shard_map/ppermute | solution.py:19
  167.2 2.8 %collective-permute-start.28 = (bf16[24,6144]{1,0:T(8,128)(2,1)S(1)}, bf16[24,6144]{1,0:T(8,128)(2,1)S(1)}, u32[]{:S(2)}, u32[]{:S(2)}) collective-permute-start(bf16[24,6144]{1,0:T(8,128)(2,1)S(1)} %add_convert_fusion.2), channel_id=1, source_target_pairs={{0,6},{1,7},{2,4},{3,5},{4,2},{5,3},{6,0},{7,1},{8,14},{9,15},{10,... | collective-permute-start | bytes 884744 | tf_op jit(solution)/shard_map/ppermute | solution.py:19
  171.6 2.2 %collective-permute-done.30 = bf16[24,6144]{1,0:T(8,128)(2,1)S(1)} collective-permute-done((bf16[24,6144]{1,0:T(8,128)(2,1)S(1)}, bf16[24,6144]{1,0:T(8,128)(2,1)S(1)}, u32[]{:S(2)}, u32[]{:S(2)}) %collective-permute-start.30) | collective-permute-done | bytes 294944 | tf_op jit(solution)/shard_map/ppermute | solution.py:19
  173.8 4.0 %collective-permute-start.31 = (bf16[24,6144]{1,0:T(8,128)(2,1)S(1)}, bf16[24,6144]{1,0:T(8,128)(2,1)S(1)}, u32[]{:S(2)}, u32[]{:S(2)}) collective-permute-start(bf16[24,6144]{1,0:T(8,128)(2,1)S(1)} %add_convert_fusion), channel_id=1, source_target_pairs={{0,4},{1,5},{2,6},{3,7},{4,0},{5,1},{6,2},{7,3},{8,12},{9,13},{10,... | collective-permute-start | bytes 884744 | tf_op jit(solution)/shard_map/ppermute | solution.py:19
  178.6 5.8 %collective-permute-done.28 = bf16[24,6144]{1,0:T(8,128)(2,1)S(1)} collective-permute-done((bf16[24,6144]{1,0:T(8,128)(2,1)S(1)}, bf16[24,6144]{1,0:T(8,128)(2,1)S(1)}, u32[]{:S(2)}, u32[]{:S(2)}) %collective-permute-start.28) | collective-permute-done | bytes 294944 | tf_op jit(solution)/shard_map/ppermute | solution.py:19
  186.7 6.7 %collective-permute-done.31 = bf16[24,6144]{1,0:T(8,128)(2,1)S(1)} collective-permute-done((bf16[24,6144]{1,0:T(8,128)(2,1)S(1)}, bf16[24,6144]{1,0:T(8,128)(2,1)S(1)}, u32[]{:S(2)}, u32[]{:S(2)}) %collective-permute-start.31) | collective-permute-done | bytes 294944 | tf_op jit(solution)/shard_map/ppermute | solution.py:19
  195.4 3.9 %collective-permute-done.32 = bf16[12,6144]{1,0:T(8,128)(2,1)S(1)} collective-permute-done((bf16[12,6144]{1,0:T(8,128)(2,1)S(1)}, bf16[12,6144]{1,0:T(8,128)(2,1)S(1)}, u32[]{:S(2)}, u32[]{:S(2)}) %collective-permute-start.32) | collective-permute-done | bytes 147488 | tf_op jit(solution)/shard_map/ppermute | solution.py:19
  (181 shorter events, 50.7 us)
Async XLA Ops:
  0.0 23.1 %collective-permute-start = (bf16[256,1536]{1,0:T(8,128)(2,1)}, bf16[256,1536]{1,0:T(8,128)(2,1)S(1)}, u32[]{:S(2)}, u32[]{:S(2)}) collective-permute-start(bf16[256,1536]{1,0:T(8,128)(2,1)} %param.18), channel_id=1, source_target_pairs={{1,8},{3,10},{5,12},{7,14},{8,1},{10,3},{12,5},{14,7},{17,24},{19,... | collective-permute-start | bytes 2359304 | tf_op jit(solution)/shard_map/ppermute | solution.py:155
  0.8 22.2 %collective-permute-start.1 = (bf16[256,1536]{1,0:T(8,128)(2,1)}, bf16[256,1536]{1,0:T(8,128)(2,1)S(1)}, u32[]{:S(2)}, u32[]{:S(2)}) collective-permute-start(bf16[256,1536]{1,0:T(8,128)(2,1)} %param.18), channel_id=1, source_target_pairs={{0,16},{1,24},{2,18},{3,26},{4,20},{5,28},{6,22},{7,30},{8,17},{9,... | collective-permute-start | bytes 2359304 | tf_op jit(solution)/shard_map/ppermute | solution.py:155
  24.3 15.6 %collective-permute-start.5 = (bf16[256,1536]{1,0:T(8,128)(2,1)S(1)}, bf16[256,1536]{1,0:T(8,128)(2,1)}, u32[]{:S(2)}, u32[]{:S(2)}) collective-permute-start(bf16[256,1536]{1,0:T(8,128)(2,1)S(1)} %broadcast_select_fusion), channel_id=1, source_target_pairs={{0,8},{8,0},{16,24},{24,16},{1,9},{9,1},{17,25},{25,17},{2,10},{10... | collective-permute-start | bytes 2359304 | tf_op jit(solution)/shard_map/ppermute | solution.py:19
  24.5 18.6 %collective-permute-start.7 = (bf16[256,1536]{1,0:T(8,128)(2,1)S(1)}, bf16[256,1536]{1,0:T(8,128)(2,1)}, u32[]{:S(2)}, u32[]{:S(2)}) collective-permute-start(bf16[256,1536]{1,0:T(8,128)(2,1)S(1)} %collective-permute-done.1), channel_id=1, source_target_pairs={{0,8},{8,0},{16,24},{24,16},{1,9},{9,1},{17,25},{25,17},{2,10},{10... | collective-permute-start | bytes 2359304 | tf_op jit(solution)/shard_map/ppermute | solution.py:19
  28.0 8.9 %collective-permute-start.2 = (bf16[256,256]{1,0:T(8,128)(2,1)}, bf16[256,256]{1,0:T(8,128)(2,1)S(1)}, u32[]{:S(2)}, u32[]{:S(2)}) collective-permute-start(bf16[256,256]{1,0:T(8,128)(2,1)} %across_blocks.1), channel_id=1, source_target_pairs={{0,1},{1,0},{2,3},{3,2},{4,5},{5,4},{6,7},{7,6},{8,9},{9,8},{10,11... | collective-permute-start | bytes 393224 | tf_op jit(solution)/shard_map/ppermute | solution.py:19
  37.8 8.1 %collective-permute-start.3 = (s32[32,2]{0,1:T(2,128)S(1)}, s32[32,2]{0,1:T(2,128)S(1)}, u32[]{:S(2)}, u32[]{:S(2)}) collective-permute-start(s32[32,2]{0,1:T(2,128)S(1)} %bitcast.115), channel_id=1, source_target_pairs={{0,1},{1,0},{2,3},{3,2},{4,5},{5,4},{6,7},{7,6},{8,9},{9,8},{10,11... | collective-permute-start | bytes 776 | tf_op jit(solution)/shard_map/ppermute | solution.py:19
  39.6 10.7 %collective-permute-start.4 = (bf16[32,6144]{1,0:T(8,128)(2,1)}, bf16[32,6144]{1,0:T(8,128)(2,1)}, u32[]{:S(2)}, u32[]{:S(2)}) collective-permute-start(bf16[32,6144]{1,0:T(8,128)(2,1)} %bitcast.102), channel_id=1, source_target_pairs={{0,1},{1,0},{2,3},{3,2},{4,5},{5,4},{6,7},{7,6},{8,9},{9,8},{10,11... | collective-permute-start | bytes 1179656 | tf_op jit(solution)/shard_map/ppermute | solution.py:19
  41.5 12.1 %collective-permute-start.6 = (bf16[128,1536]{1,0:T(8,128)(2,1)S(1)}, bf16[128,1536]{1,0:T(8,128)(2,1)S(1)}, u32[]{:S(2)}, u32[]{:S(2)}) collective-permute-start(bf16[128,1536]{1,0:T(8,128)(2,1)S(1)} %convolution_convert_fusion.2), channel_id=1, source_target_pairs={{0,2},{1,3},{2,0},{3,1},{4,6},{5,7},{6,4},{7,5},{8,10},{9,11},{10,... | collective-permute-start | bytes 1179656 | tf_op jit(solution)/shard_map/ppermute | solution.py:19
  45.4 20.1 %collective-permute-start.8 = (bf16[128,1536]{1,0:T(8,128)(2,1)}, bf16[128,1536]{1,0:T(8,128)(2,1)}, u32[]{:S(2)}, u32[]{:S(2)}) collective-permute-start(bf16[128,1536]{1,0:T(8,128)(2,1)} %convolution_convert_fusion.1), channel_id=1, source_target_pairs={{0,2},{1,3},{2,0},{3,1},{4,6},{5,7},{6,4},{7,5},{8,10},{9,11},{10,... | collective-permute-start | bytes 1179656 | tf_op jit(solution)/shard_map/ppermute | solution.py:19
  58.3 10.7 %collective-permute-start.9 = (bf16[64,1536]{1,0:T(8,128)(2,1)}, bf16[64,1536]{1,0:T(8,128)(2,1)S(1)}, u32[]{:S(2)}, u32[]{:S(2)}) collective-permute-start(bf16[64,1536]{1,0:T(8,128)(2,1)} %slice.191), channel_id=1, source_target_pairs={{0,4},{1,5},{2,6},{3,7},{4,0},{5,1},{6,2},{7,3},{8,12},{9,13},{10,... | collective-permute-start | bytes 589832 | tf_op jit(solution)/shard_map/ppermute | solution.py:19
  70.4 7.6 %collective-permute-start.10 = (bf16[64,1536]{1,0:T(8,128)(2,1)S(1)}, bf16[64,1536]{1,0:T(8,128)(2,1)S(1)}, u32[]{:S(2)}, u32[]{:S(2)}) collective-permute-start(bf16[64,1536]{1,0:T(8,128)(2,1)S(1)} %slice.190), channel_id=1, source_target_pairs={{0,4},{1,5},{2,6},{3,7},{4,0},{5,1},{6,2},{7,3},{8,12},{9,13},{10,... | collective-permute-start | bytes 589832 | tf_op jit(solution)/shard_map/ppermute | solution.py:19
  70.6 10.4 %collective-permute-start.12 = (bf16[64,1536]{1,0:T(8,128)(2,1)S(1)}, bf16[64,1536]{1,0:T(8,128)(2,1)S(1)}, u32[]{:S(2)}, u32[]{:S(2)}) collective-permute-start(bf16[64,1536]{1,0:T(8,128)(2,1)S(1)} %fusion.76), channel_id=1, source_target_pairs={{0,1},{1,0},{2,3},{3,2},{4,5},{5,4},{6,7},{7,6},{8,9},{9,8},{10,11... | collective-permute-start | bytes 589832 | tf_op jit(solution)/shard_map/ppermute | solution.py:19
  78.1 6.4 %collective-permute-start.11 = (bf16[64,1536]{1,0:T(8,128)(2,1)S(1)}, bf16[64,1536]{1,0:T(8,128)(2,1)S(1)}, u32[]{:S(2)}, u32[]{:S(2)}) collective-permute-start(bf16[64,1536]{1,0:T(8,128)(2,1)S(1)} %fusion.75), channel_id=1, source_target_pairs={{0,1},{1,0},{2,3},{3,2},{4,5},{5,4},{6,7},{7,6},{8,9},{9,8},{10,11... | collective-permute-start | bytes 589832 | tf_op jit(solution)/shard_map/ppermute | solution.py:19
  86.7 19.8 %collective-permute-start.13 = (bf16[24,6144]{1,0:T(8,128)(2,1)}, bf16[24,6144]{1,0:T(8,128)(2,1)S(1)}, u32[]{:S(2)}, u32[]{:S(2)}) collective-permute-start(bf16[24,6144]{1,0:T(8,128)(2,1)} %get-tuple-element.72), channel_id=1, source_target_pairs={{0,4},{1,5},{2,6},{3,7},{4,0},{5,1},{6,2},{7,3},{8,12},{9,13},{10,... | collective-permute-start | bytes 884744 | tf_op jit(solution)/shard_map/ppermute | solution.py:19
  86.7 8.9 %collective-permute-start.14 = (bf16[24,6144]{1,0:T(8,128)(2,1)S(1)}, bf16[24,6144]{1,0:T(8,128)(2,1)S(1)}, u32[]{:S(2)}, u32[]{:S(2)}) collective-permute-start(bf16[24,6144]{1,0:T(8,128)(2,1)S(1)} %get-tuple-element.70), channel_id=1, source_target_pairs={{0,2},{1,3},{2,0},{3,1},{4,6},{5,7},{6,4},{7,5},{8,10},{9,11},{10,... | collective-permute-start | bytes 884744 | tf_op jit(solution)/shard_map/ppermute | solution.py:19
  89.2 17.3 %collective-permute-start.18 = (bf16[24,6144]{1,0:T(8,128)(2,1)S(1)}, bf16[24,6144]{1,0:T(8,128)(2,1)S(1)}, u32[]{:S(2)}, u32[]{:S(2)}) collective-permute-start(bf16[24,6144]{1,0:T(8,128)(2,1)S(1)} %get-tuple-element.51), channel_id=1, source_target_pairs={{0,16},{8,24},{16,0},{24,8},{1,17},{9,25},{17,1},{25,9},{2,18},{10... | collective-permute-start | bytes 884744 | tf_op jit(solution)/shard_map/ppermute | solution.py:19
  95.5 11.0 %collective-permute-start.19 = (bf16[24,6144]{1,0:T(8,128)(2,1)S(1)}, bf16[24,6144]{1,0:T(8,128)(2,1)S(1)}, u32[]{:S(2)}, u32[]{:S(2)}) collective-permute-start(bf16[24,6144]{1,0:T(8,128)(2,1)S(1)} %collective-permute-done.14), channel_id=1, source_target_pairs={{0,16},{8,24},{16,0},{24,8},{1,17},{9,25},{17,1},{25,9},{2,18},{10... | collective-permute-start | bytes 884744 | tf_op jit(solution)/shard_map/ppermute | solution.py:19
  96.7 10.1 %collective-permute-start.15 = (bf16[24,6144]{1,0:T(8,128)(2,1)S(1)}, bf16[24,6144]{1,0:T(8,128)(2,1)S(1)}, u32[]{:S(2)}, u32[]{:S(2)}) collective-permute-start(bf16[24,6144]{1,0:T(8,128)(2,1)S(1)} %get-tuple-element.50), channel_id=1, source_target_pairs={{0,6},{1,7},{2,4},{3,5},{4,2},{5,3},{6,0},{7,1},{8,14},{9,15},{10,... | collective-permute-start | bytes 884744 | tf_op jit(solution)/shard_map/ppermute | solution.py:19
  106.5 25.7 %collective-permute-start.16 = (bf16[24,6144]{1,0:T(8,128)(2,1)S(1)}, bf16[24,6144]{1,0:T(8,128)(2,1)S(1)}, u32[]{:S(2)}, u32[]{:S(2)}) collective-permute-start(bf16[24,6144]{1,0:T(8,128)(2,1)S(1)} %collective-permute-done.13), channel_id=1, source_target_pairs={{0,16},{8,24},{16,0},{24,8},{1,17},{9,25},{17,1},{25,9},{2,18},{10... | collective-permute-start | bytes 884744 | tf_op jit(solution)/shard_map/ppermute | solution.py:19
  106.6 2.9 %collective-permute-start.20 = (bf16[96,6144]{1,0:T(8,128)(2,1)S(1)}, bf16[96,6144]{1,0:T(8,128)(2,1)S(1)}, u32[]{:S(2)}, u32[]{:S(2)}) collective-permute-start(bf16[96,6144]{1,0:T(8,128)(2,1)S(1)} %pad_maximum_fusion.1), channel_id=1, source_target_pairs={{0,8},{8,0},{16,24},{24,16},{1,9},{9,1},{17,25},{25,17},{2,10},{10... | collective-permute-start | bytes 3538952 | tf_op jit(solution)/shard_map/ppermute | solution.py:19
  106.7 25.4 %collective-permute-start.17 = (bf16[24,6144]{1,0:T(8,128)(2,1)S(1)}, bf16[24,6144]{1,0:T(8,128)(2,1)S(1)}, u32[]{:S(2)}, u32[]{:S(2)}) collective-permute-start(bf16[24,6144]{1,0:T(8,128)(2,1)S(1)} %collective-permute-done.15), channel_id=1, source_target_pairs={{0,16},{8,24},{16,0},{24,8},{1,17},{9,25},{17,1},{25,9},{2,18},{10... | collective-permute-start | bytes 884744 | tf_op jit(solution)/shard_map/ppermute | solution.py:19
  132.5 13.1 %collective-permute-start.23 = (bf16[96,6144]{1,0:T(8,128)(2,1)S(1)}, bf16[96,6144]{1,0:T(8,128)(2,1)S(1)}, u32[]{:S(2)}, u32[]{:S(2)}) collective-permute-start(bf16[96,6144]{1,0:T(8,128)(2,1)S(1)} %slice.129), channel_id=1, source_target_pairs={{0,8},{8,0},{16,24},{24,16},{1,9},{9,1},{17,25},{25,17},{2,10},{10... | collective-permute-start | bytes 3538952 | tf_op jit(solution)/shard_map/ppermute | solution.py:19
  146.0 9.4 %collective-permute-start.24 = (bf16[24,6144]{1,0:T(8,128)(2,1)S(1)}, bf16[24,6144]{1,0:T(8,128)(2,1)S(1)}, u32[]{:S(2)}, u32[]{:S(2)}) collective-permute-start(bf16[24,6144]{1,0:T(8,128)(2,1)S(1)} %slice.189), channel_id=1, source_target_pairs={{0,16},{8,24},{16,0},{24,8},{1,17},{9,25},{17,1},{25,9},{2,18},{10... | collective-permute-start | bytes 884744 | tf_op jit(solution)/shard_map/ppermute | solution.py:19
  152.1 3.4 %collective-permute-start.22 = (bf16[96,6144]{1,0:T(8,128)(2,1)S(1)}, bf16[96,6144]{1,0:T(8,128)(2,1)S(1)}, u32[]{:S(2)}, u32[]{:S(2)}) collective-permute-start(bf16[96,6144]{1,0:T(8,128)(2,1)S(1)} %slice.127), channel_id=1, source_target_pairs={{0,8},{8,0},{16,24},{24,16},{1,9},{9,1},{17,25},{25,17},{2,10},{10... | collective-permute-start | bytes 3538952 | tf_op jit(solution)/shard_map/ppermute | solution.py:19
  155.8 8.6 %collective-permute-start.25 = (bf16[24,6144]{1,0:T(8,128)(2,1)S(1)}, bf16[24,6144]{1,0:T(8,128)(2,1)S(1)}, u32[]{:S(2)}, u32[]{:S(2)}) collective-permute-start(bf16[24,6144]{1,0:T(8,128)(2,1)S(1)} %slice.188), channel_id=1, source_target_pairs={{0,16},{8,24},{16,0},{24,8},{1,17},{9,25},{17,1},{25,9},{2,18},{10... | collective-permute-start | bytes 884744 | tf_op jit(solution)/shard_map/ppermute | solution.py:19
  164.5 9.2 %collective-permute-start.30 = (bf16[24,6144]{1,0:T(8,128)(2,1)S(1)}, bf16[24,6144]{1,0:T(8,128)(2,1)S(1)}, u32[]{:S(2)}, u32[]{:S(2)}) collective-permute-start(bf16[24,6144]{1,0:T(8,128)(2,1)S(1)} %slice.186), channel_id=1, source_target_pairs={{0,16},{8,24},{16,0},{24,8},{1,17},{9,25},{17,1},{25,9},{2,18},{10... | collective-permute-start | bytes 884744 | tf_op jit(solution)/shard_map/ppermute | solution.py:19
  166.1 12.4 %collective-permute-start.27 = (bf16[24,6144]{1,0:T(8,128)(2,1)S(1)}, bf16[24,6144]{1,0:T(8,128)(2,1)S(1)}, u32[]{:S(2)}, u32[]{:S(2)}) collective-permute-start(bf16[24,6144]{1,0:T(8,128)(2,1)S(1)} %fusion.33), channel_id=1, source_target_pairs={{0,2},{1,3},{2,0},{3,1},{4,6},{5,7},{6,4},{7,5},{8,10},{9,11},{10,... | collective-permute-start | bytes 884744 | tf_op jit(solution)/shard_map/ppermute | solution.py:19
  167.2 17.1 %collective-permute-start.28 = (bf16[24,6144]{1,0:T(8,128)(2,1)S(1)}, bf16[24,6144]{1,0:T(8,128)(2,1)S(1)}, u32[]{:S(2)}, u32[]{:S(2)}) collective-permute-start(bf16[24,6144]{1,0:T(8,128)(2,1)S(1)} %add_convert_fusion.2), channel_id=1, source_target_pairs={{0,6},{1,7},{2,4},{3,5},{4,2},{5,3},{6,0},{7,1},{8,14},{9,15},{10,... | collective-permute-start | bytes 884744 | tf_op jit(solution)/shard_map/ppermute | solution.py:19
  170.1 8.5 %collective-permute-start.26 = (bf16[24,6144]{1,0:T(8,128)(2,1)S(1)}, bf16[24,6144]{1,0:T(8,128)(2,1)S(1)}, u32[]{:S(2)}, u32[]{:S(2)}) collective-permute-start(bf16[24,6144]{1,0:T(8,128)(2,1)S(1)} %slice.187), channel_id=1, source_target_pairs={{0,16},{8,24},{16,0},{24,8},{1,17},{9,25},{17,1},{25,9},{2,18},{10... | collective-permute-start | bytes 884744 | tf_op jit(solution)/shard_map/ppermute | solution.py:19
  173.8 19.6 %collective-permute-start.31 = (bf16[24,6144]{1,0:T(8,128)(2,1)S(1)}, bf16[24,6144]{1,0:T(8,128)(2,1)S(1)}, u32[]{:S(2)}, u32[]{:S(2)}) collective-permute-start(bf16[24,6144]{1,0:T(8,128)(2,1)S(1)} %add_convert_fusion), channel_id=1, source_target_pairs={{0,4},{1,5},{2,6},{3,7},{4,0},{5,1},{6,2},{7,3},{8,12},{9,13},{10,... | collective-permute-start | bytes 884744 | tf_op jit(solution)/shard_map/ppermute | solution.py:19
  185.2 14.5 %collective-permute-start.29 = (bf16[32,6144]{1,0:T(8,128)(2,1)S(1)}, bf16[32,6144]{1,0:T(8,128)(2,1)S(1)}, u32[]{:S(2)}, u32[]{:S(2)}) collective-permute-start(bf16[32,6144]{1,0:T(8,128)(2,1)S(1)} %fusion.40), channel_id=1, source_target_pairs={{0,1},{1,0},{2,3},{3,2},{4,5},{5,4},{6,7},{7,6},{8,9},{9,8},{10,11... | collective-permute-start | bytes 1179656 | tf_op jit(solution)/shard_map/ppermute | solution.py:19
  193.5 5.8 %collective-permute-start.32 = (bf16[12,6144]{1,0:T(8,128)(2,1)S(1)}, bf16[12,6144]{1,0:T(8,128)(2,1)S(1)}, u32[]{:S(2)}, u32[]{:S(2)}) collective-permute-start(bf16[12,6144]{1,0:T(8,128)(2,1)S(1)} %constant_dynamic-slice_fusion), channel_id=1, source_target_pairs={{0,1},{1,0},{2,3},{3,2},{4,5},{5,4},{6,7},{7,6},{8,9},{9,8},{10,11... | collective-permute-start | bytes 442376 | tf_op jit(solution)/shard_map/ppermute | solution.py:19
  (22 other events, 305.9 us)

commit v5 on v4

--- a/solution.py
+++ b/solution.py
@@ -166,9 +166,6 @@
         for mine in soon
     ]
     heads = jnp.stack([normed_heads] + [swap(normed_heads, "ep", k) for k in range(1, fast)])
-    own_residual, own_routes, heads = lax.optimization_barrier((own_residual, own_routes, heads))
-    near_residual = [own_residual] + [swap(own_residual, "ep", k) for k in range(1, fast)]
-    near_routes = [own_routes] + [swap(own_routes, "ep", k) for k in range(1, fast)]
     heads = jnp.concatenate(
         [
             lax.dynamic_index_in_dim(heads, lower ^ j ^ near, 0, False)
@@ -183,6 +180,12 @@
     attn = []
     for a in range(high):
         sent = jnp.dot(given, pieces[a], preferred_element_type=f32).astype(bf16)
+        if a == 0:
+            own_residual, own_routes, sent = lax.optimization_barrier(
+                (own_residual, own_routes, sent)
+            )
+            near_residual = [own_residual] + [swap(own_residual, "ep", k) for k in range(1, fast)]
+            near_routes = [own_routes] + [swap(own_routes, "ep", k) for k in range(1, fast)]
         came = swap(sent, "ep", fast)
         if a == 0:
             near_routes, near_residual, came = lax.optimization_barrier(

time: 201 us -> 204 us (1.015)
  transfers between devices with their start and end apart: 33 -> 33, of which waited for: 17 -> 15; matrix products, arithmetic and copies ran while one was open for 27% -> 27% of each run, Pallas kernels for 3% -> 3%
where the time goes in v5:
time: 204 us
  waiting for transfers between devices  69.8 us (34%)
  starting transfers between devices  49.5 us (24%)
  matrix products  43.9 us (22%)
  blocking collectives  14.2 us (7%)
  local copies, waits for them, and re-layouts  10 us (5%)
  other arithmetic  9.24 us (5%)
  Pallas kernels  6.07 us (3%)
    ppermute x31, waiting for transfers between devices, swap(): return lax.ppermute(array, axis, [(i, i ^ mask) for i in range(size)])  69.8 us
    ppermute x31, starting transfers between devices, swap(): return lax.ppermute(array, axis, [(i, i ^ mask) for i in range(size)])  45.6 us
    all_gather x1, blocking collectives, attention(): lax.all_gather(state, 'ctx')  14.2 us
    dot_general x2, matrix products, experts(): gate_out = jnp.dot(rows, gate_weight, preferred_element_type=f32)  13.9 us
    dot_general x2, matrix products, experts(): return jnp.dot(hidden, down_weight, preferred_element_type=f32).astype(bf16)  12.3 us
    dot_general x2, matrix products, experts(): up_out = jnp.dot(rows, up_weight, preferred_element_type=f32)  10.3 us
  transfers between devices with their start and end apart: 33, of which 15 were waited for; matrix products, arithmetic and copies ran while one was open for 27% of the time, Pallas kernels for 3%

profile of v5, /device:TPU:0, one launch (start us, length us, event | category | flops | bytes accessed | tf_op | source)
XLA Modules:
  0.0 203.5 jit_solution(4748276602308694157)
XLA Ops:
  0.8 3.0 %collective-permute-start.1 = (bf16[256,1536]{1,0:T(8,128)(2,1)}, bf16[256,1536]{1,0:T(8,128)(2,1)S(1)}, u32[]{:S(2)}, u32[]{:S(2)}) collective-permute-start(bf16[256,1536]{1,0:T(8,128)(2,1)} %param.18), channel_id=1, source_target_pairs={{0,16},{1,24},{2,18},{3,26},{4,20},{5,28},{6,22},{7,30},{8,17},{9,... | collective-permute-start | bytes 2359304 | tf_op jit(solution)/shard_map/ppermute | solution.py:155
  5.1 3.7 %within_block.1 = (f32[256,256]{1,0:T(8,128)}, f32[256,256]{1,0:T(8,128)}, bf16[288,128]{1,0:T(8,128)(2,1)}) custom-call(bf16[256,256]{1,0:T(8,128)(2,1)} %bitcast.104, bf16[256,256]{1,0:T(8,128)(2,1)} %bitcast.105, bf16[256,256]{1,0:T(8,128)(2,1)} %bitcast.106, f32[2,256]{1,0:T(2,128)} %bitcast.113), custom_call_target="tpu_custom_call" | custom-call | tf_op jit(solution)/shard_map/within_block/pallas_call | solution.py:92
  8.9 14.2 %all-gather = bf16[1152,128]{1,0:T(8,128)(2,1)} all-gather(bf16[288,128]{1,0:T(8,128)(2,1)} %get-tuple-element.35), channel_id=2, replica_groups=mesh['ctx'=4,'ep'=8] {'ctx'}, dimensions={0}, use_global_device_ids=true | all-gather | bytes 368640 | tf_op jit(solution)/shard_map/all_gather | solution.py:101
  25.6 2.3 %across_blocks.1 = bf16[256,256]{1,0:T(8,128)(2,1)} custom-call(s32[1]{0:T(128)} %bitcast.2.place_ref, bf16[4,288,128]{2,1,0:T(8,128)(2,1)} %bitcast.96, f32[256,256]{1,0:T(8,128)} %get-tuple-element.37.inside_ref, f32[256,256]{1,0:T(8,128)} %get-tuple-element.38.query_ref, f32[1,256]{1,0:T(1,128)} %bitcast.117), custom_call_target="tpu_custom_call" | custom-call | tf_op jit(solution)/shard_map/across_blocks/pallas_call | solution.py:104
  28.0 4.5 %collective-permute-start.2 = (bf16[256,256]{1,0:T(8,128)(2,1)}, bf16[256,256]{1,0:T(8,128)(2,1)S(1)}, u32[]{:S(2)}, u32[]{:S(2)}) collective-permute-start(bf16[256,256]{1,0:T(8,128)(2,1)} %across_blocks.1), channel_id=1, source_target_pairs={{0,1},{1,0},{2,3},{3,2},{4,5},{5,4},{6,7},{7,6},{8,9},{9,8},{10,11... | collective-permute-start | bytes 393224 | tf_op jit(solution)/shard_map/ppermute | solution.py:19
  32.6 4.2 %collective-permute-done.2 = bf16[256,256]{1,0:T(8,128)(2,1)S(1)} collective-permute-done((bf16[256,256]{1,0:T(8,128)(2,1)}, bf16[256,256]{1,0:T(8,128)(2,1)S(1)}, u32[]{:S(2)}, u32[]{:S(2)}) %collective-permute-start.2) | collective-permute-done | bytes 131104 | tf_op jit(solution)/shard_map/ppermute | solution.py:19
  45.8 5.8 %collective-permute-done.5 = bf16[32,6144]{1,0:T(8,128)(2,1)S(1)} collective-permute-done((bf16[32,6144]{1,0:T(8,128)(2,1)S(1)}, bf16[32,6144]{1,0:T(8,128)(2,1)S(1)}, u32[]{:S(2)}, u32[]{:S(2)}) %collective-permute-start.5) | collective-permute-done | bytes 393248 | tf_op jit(solution)/shard_map/ppermute | solution.py:19
  58.4 2.6 %collective-permute-start.9 = (bf16[64,1536]{1,0:T(8,128)(2,1)}, bf16[64,1536]{1,0:T(8,128)(2,1)S(1)}, u32[]{:S(2)}, u32[]{:S(2)}) collective-permute-start(bf16[64,1536]{1,0:T(8,128)(2,1)} %slice.191), channel_id=1, source_target_pairs={{0,4},{1,5},{2,6},{3,7},{4,0},{5,1},{6,2},{7,3},{8,12},{9,13},{10,... | collective-permute-start | bytes 589832 | tf_op jit(solution)/shard_map/ppermute | solution.py:19
  65.4 3.4 %collective-permute-done.9 = bf16[64,1536]{1,0:T(8,128)(2,1)S(1)} collective-permute-done((bf16[64,1536]{1,0:T(8,128)(2,1)}, bf16[64,1536]{1,0:T(8,128)(2,1)S(1)}, u32[]{:S(2)}, u32[]{:S(2)}) %collective-permute-start.9) | collective-permute-done | bytes 196640 | tf_op jit(solution)/shard_map/ppermute | solution.py:19
  70.3 1.9 collective-permute-start.12
  72.3 6.7 %collective-permute-done.10 = bf16[64,1536]{1,0:T(8,128)(2,1)S(1)} collective-permute-done((bf16[64,1536]{1,0:T(8,128)(2,1)S(1)}, bf16[64,1536]{1,0:T(8,128)(2,1)S(1)}, u32[]{:S(2)}, u32[]{:S(2)}) %collective-permute-start.10) | collective-permute-done | bytes 196640 | tf_op jit(solution)/shard_map/ppermute | solution.py:19
  79.0 1.9 collective-permute-start.11
  81.0 3.7 %collective-permute-done.11 = bf16[64,1536]{1,0:T(8,128)(2,1)S(1)} collective-permute-done((bf16[64,1536]{1,0:T(8,128)(2,1)S(1)}, bf16[64,1536]{1,0:T(8,128)(2,1)S(1)}, u32[]{:S(2)}, u32[]{:S(2)}) %collective-permute-start.11) | collective-permute-done | bytes 196640 | tf_op jit(solution)/shard_map/ppermute | solution.py:19
  86.9 3.2 %collective-permute-start.14 = (bf16[24,6144]{1,0:T(8,128)(2,1)S(1)}, bf16[24,6144]{1,0:T(8,128)(2,1)S(1)}, u32[]{:S(2)}, u32[]{:S(2)}) collective-permute-start(bf16[24,6144]{1,0:T(8,128)(2,1)S(1)} %get-tuple-element.70), channel_id=1, source_target_pairs={{0,2},{1,3},{2,0},{3,1},{4,6},{5,7},{6,4},{7,5},{8,10},{9,11},{10,... | collective-permute-start | bytes 884744 | tf_op jit(solution)/shard_map/ppermute | solution.py:19
  91.4 6.5 %collective-permute-done.14 = bf16[24,6144]{1,0:T(8,128)(2,1)S(1)} collective-permute-done((bf16[24,6144]{1,0:T(8,128)(2,1)S(1)}, bf16[24,6144]{1,0:T(8,128)(2,1)S(1)}, u32[]{:S(2)}, u32[]{:S(2)}) %collective-permute-start.14) | collective-permute-done | bytes 294944 | tf_op jit(solution)/shard_map/ppermute | solution.py:19
  99.0 4.1 %collective-permute-start.15 = (bf16[24,6144]{1,0:T(8,128)(2,1)S(1)}, bf16[24,6144]{1,0:T(8,128)(2,1)S(1)}, u32[]{:S(2)}, u32[]{:S(2)}) collective-permute-start(bf16[24,6144]{1,0:T(8,128)(2,1)S(1)} %get-tuple-element.50), channel_id=1, source_target_pairs={{0,6},{1,7},{2,4},{3,5},{4,2},{5,3},{6,0},{7,1},{8,14},{9,15},{10,... | collective-permute-start | bytes 884744 | tf_op jit(solution)/shard_map/ppermute | solution.py:19
  105.2 4.1 %collective-permute-done.15 = bf16[24,6144]{1,0:T(8,128)(2,1)S(1)} collective-permute-done((bf16[24,6144]{1,0:T(8,128)(2,1)S(1)}, bf16[24,6144]{1,0:T(8,128)(2,1)S(1)}, u32[]{:S(2)}, u32[]{:S(2)}) %collective-permute-start.15) | collective-permute-done | bytes 294944 | tf_op jit(solution)/shard_map/ppermute | solution.py:19
  110.5 7.0 %fusion.6 = f32[192,1152]{1,0:T(8,128)S(1)} fusion(bf16[192,6144]{1,0:T(8,128)(2,1)S(1)} %constant_dynamic-update-slice_fusion.2, bf16[1,6144,1152]{2,1,0:T(8,128)(2,1)} %param.23), kind=kOutput, calls=%fused_computation.6 | convolution fusion | flops 2717908992 | bytes 17399808 | tf_op jit(solution)/shard_map/dot_general | solution.py:115
  117.6 6.9 %fusion.10 = f32[192,1152]{1,0:T(8,128)S(1)} fusion(bf16[192,6144]{1,0:T(8,128)(2,1)S(1)} %constant_dynamic-update-slice_fusion.2, bf16[1,6144,1152]{2,1,0:T(8,128)(2,1)} %param.22), kind=kOutput, calls=%fused_computation.10 | convolution fusion | flops 2717908992 | bytes 17399808 | tf_op jit(solution)/shard_map/dot_general | solution.py:114
  124.5 8.5 %fusion.12 = bf16[192,6144]{1,0:T(8,128)(2,1)S(1)} fusion(bf16[1,1152,6144]{2,1,0:T(8,128)(2,1)} %param.24, f32[192,1152]{1,0:T(8,128)S(1)} %fusion.6, f32[192,1152]{1,0:T(8,128)S(1)} %fusion.10), kind=kOutput, calls=%fused_computation.12 | convolution fusion | flops 2720415744 | bytes 18284544 | tf_op jit(solution)/shard_map/dot_general | solution.py:117
  133.9 2.3 %collective-permute-done.21 = bf16[96,6144]{1,0:T(8,128)(2,1)S(1)} collective-permute-done((bf16[96,6144]{1,0:T(8,128)(2,1)S(1)}, bf16[96,6144]{1,0:T(8,128)(2,1)S(1)}, u32[]{:S(2)}, u32[]{:S(2)}) %collective-permute-start.21) | collective-permute-done | bytes 1179680 | tf_op jit(solution)/shard_map/ppermute | solution.py:19
  136.3 3.3 %fusion.4 = f32[192,1152]{1,0:T(8,128)S(1)} fusion(bf16[192,6144]{1,0:T(8,128)(2,1)S(1)} %constant_dynamic-update-slice_fusion.7, bf16[1,6144,1152]{2,1,0:T(8,128)(2,1)S(1)} %bitcast.119), kind=kOutput, calls=%fused_computation.4 | convolution fusion | flops 2717908992 | bytes 17399808 | tf_op jit(solution)/shard_map/dot_general | solution.py:115
  139.7 6.9 %fusion.8 = f32[192,1152]{1,0:T(8,128)S(1)} fusion(bf16[192,6144]{1,0:T(8,128)(2,1)S(1)} %constant_dynamic-update-slice_fusion.7, bf16[1,6144,1152]{2,1,0:T(8,128)(2,1)} %param.22), kind=kOutput, calls=%fused_computation.8 | convolution fusion | flops 2717908992 | bytes 17399808 | tf_op jit(solution)/shard_map/dot_general | solution.py:114
  147.9 3.9 %fusion.15 = bf16[192,6144]{1,0:T(8,128)(2,1)S(1)} fusion(bf16[1,1152,6144]{2,1,0:T(8,128)(2,1)S(1)} %bitcast.121, f32[192,1152]{1,0:T(8,128)S(1)} %fusion.4, f32[192,1152]{1,0:T(8,128)S(1)} %fusion.8), kind=kOutput, calls=%fused_computation.13 | convolution fusion | flops 2720415744 | bytes 18284544 | tf_op jit(solution)/shard_map/dot_general | solution.py:117
  151.9 4.1 %collective-permute-done.24 = bf16[24,6144]{1,0:T(8,128)(2,1)S(1)} collective-permute-done((bf16[24,6144]{1,0:T(8,128)(2,1)S(1)}, bf16[24,6144]{1,0:T(8,128)(2,1)S(1)}, u32[]{:S(2)}, u32[]{:S(2)}) %collective-permute-start.24) | collective-permute-done | bytes 294944 | tf_op jit(solution)/shard_map/ppermute | solution.py:19
  157.5 7.2 %collective-permute-done.25 = bf16[24,6144]{1,0:T(8,128)(2,1)S(1)} collective-permute-done((bf16[24,6144]{1,0:T(8,128)(2,1)S(1)}, bf16[24,6144]{1,0:T(8,128)(2,1)S(1)}, u32[]{:S(2)}, u32[]{:S(2)}) %collective-permute-start.25) | collective-permute-done | bytes 294944 | tf_op jit(solution)/shard_map/ppermute | solution.py:19
  165.9 4.9 %collective-permute-start.27 = (bf16[24,6144]{1,0:T(8,128)(2,1)S(1)}, bf16[24,6144]{1,0:T(8,128)(2,1)S(1)}, u32[]{:S(2)}, u32[]{:S(2)}) collective-permute-start(bf16[24,6144]{1,0:T(8,128)(2,1)S(1)} %fusion.33), channel_id=1, source_target_pairs={{0,2},{1,3},{2,0},{3,1},{4,6},{5,7},{6,4},{7,5},{8,10},{9,11},{10,... | collective-permute-start | bytes 884744 | tf_op jit(solution)/shard_map/ppermute | solution.py:19
  170.8 2.6 %collective-permute-start.28 = (bf16[24,6144]{1,0:T(8,128)(2,1)S(1)}, bf16[24,6144]{1,0:T(8,128)(2,1)S(1)}, u32[]{:S(2)}, u32[]{:S(2)}) collective-permute-start(bf16[24,6144]{1,0:T(8,128)(2,1)S(1)} %add_convert_fusion.2), channel_id=1, source_target_pairs={{0,6},{1,7},{2,4},{3,5},{4,2},{5,3},{6,0},{7,1},{8,14},{9,15},{10,... | collective-permute-start | bytes 884744 | tf_op jit(solution)/shard_map/ppermute | solution.py:19
  174.8 6.2 %collective-permute-start.31 = (bf16[24,6144]{1,0:T(8,128)(2,1)S(1)}, bf16[24,6144]{1,0:T(8,128)(2,1)S(1)}, u32[]{:S(2)}, u32[]{:S(2)}) collective-permute-start(bf16[24,6144]{1,0:T(8,128)(2,1)S(1)} %add_convert_fusion), channel_id=1, source_target_pairs={{0,4},{1,5},{2,6},{3,7},{4,0},{5,1},{6,2},{7,3},{8,12},{9,13},{10,... | collective-permute-start | bytes 884744 | tf_op jit(solution)/shard_map/ppermute | solution.py:19
  181.1 6.7 %collective-permute-done.28 = bf16[24,6144]{1,0:T(8,128)(2,1)S(1)} collective-permute-done((bf16[24,6144]{1,0:T(8,128)(2,1)S(1)}, bf16[24,6144]{1,0:T(8,128)(2,1)S(1)}, u32[]{:S(2)}, u32[]{:S(2)}) %collective-permute-start.28) | collective-permute-done | bytes 294944 | tf_op jit(solution)/shard_map/ppermute | solution.py:19
  188.7 7.7 %collective-permute-done.31 = bf16[24,6144]{1,0:T(8,128)(2,1)S(1)} collective-permute-done((bf16[24,6144]{1,0:T(8,128)(2,1)S(1)}, bf16[24,6144]{1,0:T(8,128)(2,1)S(1)}, u32[]{:S(2)}, u32[]{:S(2)}) %collective-permute-start.31) | collective-permute-done | bytes 294944 | tf_op jit(solution)/shard_map/ppermute | solution.py:19
  196.6 5.5 %collective-permute-done.32 = bf16[12,6144]{1,0:T(8,128)(2,1)S(1)} collective-permute-done((bf16[12,6144]{1,0:T(8,128)(2,1)S(1)}, bf16[12,6144]{1,0:T(8,128)(2,1)S(1)}, u32[]{:S(2)}, u32[]{:S(2)}) %collective-permute-start.32) | collective-permute-done | bytes 147488 | tf_op jit(solution)/shard_map/ppermute | solution.py:19
  (186 shorter events, 43.1 us)
Async XLA Ops:
  0.0 23.1 %collective-permute-start = (bf16[256,1536]{1,0:T(8,128)(2,1)}, bf16[256,1536]{1,0:T(8,128)(2,1)S(1)}, u32[]{:S(2)}, u32[]{:S(2)}) collective-permute-start(bf16[256,1536]{1,0:T(8,128)(2,1)} %param.18), channel_id=1, source_target_pairs={{1,8},{3,10},{5,12},{7,14},{8,1},{10,3},{12,5},{14,7},{17,24},{19,... | collective-permute-start | bytes 2359304 | tf_op jit(solution)/shard_map/ppermute | solution.py:155
  0.8 22.3 %collective-permute-start.1 = (bf16[256,1536]{1,0:T(8,128)(2,1)}, bf16[256,1536]{1,0:T(8,128)(2,1)S(1)}, u32[]{:S(2)}, u32[]{:S(2)}) collective-permute-start(bf16[256,1536]{1,0:T(8,128)(2,1)} %param.18), channel_id=1, source_target_pairs={{0,16},{1,24},{2,18},{3,26},{4,20},{5,28},{6,22},{7,30},{8,17},{9,... | collective-permute-start | bytes 2359304 | tf_op jit(solution)/shard_map/ppermute | solution.py:155
  24.3 13.5 %collective-permute-start.3 = (bf16[256,1536]{1,0:T(8,128)(2,1)S(1)}, bf16[256,1536]{1,0:T(8,128)(2,1)}, u32[]{:S(2)}, u32[]{:S(2)}) collective-permute-start(bf16[256,1536]{1,0:T(8,128)(2,1)S(1)} %broadcast_select_fusion), channel_id=1, source_target_pairs={{0,8},{8,0},{16,24},{24,16},{1,9},{9,1},{17,25},{25,17},{2,10},{10... | collective-permute-start | bytes 2359304 | tf_op jit(solution)/shard_map/ppermute | solution.py:19
  24.5 18.6 %collective-permute-start.7 = (bf16[256,1536]{1,0:T(8,128)(2,1)S(1)}, bf16[256,1536]{1,0:T(8,128)(2,1)}, u32[]{:S(2)}, u32[]{:S(2)}) collective-permute-start(bf16[256,1536]{1,0:T(8,128)(2,1)S(1)} %collective-permute-done.1), channel_id=1, source_target_pairs={{0,8},{8,0},{16,24},{24,16},{1,9},{9,1},{17,25},{25,17},{2,10},{10... | collective-permute-start | bytes 2359304 | tf_op jit(solution)/shard_map/ppermute | solution.py:19
  28.0 8.8 %collective-permute-start.2 = (bf16[256,256]{1,0:T(8,128)(2,1)}, bf16[256,256]{1,0:T(8,128)(2,1)S(1)}, u32[]{:S(2)}, u32[]{:S(2)}) collective-permute-start(bf16[256,256]{1,0:T(8,128)(2,1)} %across_blocks.1), channel_id=1, source_target_pairs={{0,1},{1,0},{2,3},{3,2},{4,5},{5,4},{6,7},{7,6},{8,9},{9,8},{10,11... | collective-permute-start | bytes 393224 | tf_op jit(solution)/shard_map/ppermute | solution.py:19
  39.4 6.4 %collective-permute-start.4 = (s32[32,2]{0,1:T(2,128)S(1)}, s32[32,2]{0,1:T(2,128)S(1)}, u32[]{:S(2)}, u32[]{:S(2)}) collective-permute-start(s32[32,2]{0,1:T(2,128)S(1)} %bitcast.115), channel_id=1, source_target_pairs={{0,1},{1,0},{2,3},{3,2},{4,5},{5,4},{6,7},{7,6},{8,9},{9,8},{10,11... | collective-permute-start | bytes 776 | tf_op jit(solution)/shard_map/ppermute | solution.py:19
  41.2 10.4 %collective-permute-start.5 = (bf16[32,6144]{1,0:T(8,128)(2,1)S(1)}, bf16[32,6144]{1,0:T(8,128)(2,1)S(1)}, u32[]{:S(2)}, u32[]{:S(2)}) collective-permute-start(bf16[32,6144]{1,0:T(8,128)(2,1)S(1)} %bitcast.103), channel_id=1, source_target_pairs={{0,1},{1,0},{2,3},{3,2},{4,5},{5,4},{6,7},{7,6},{8,9},{9,8},{10,11... | collective-permute-start | bytes 1179656 | tf_op jit(solution)/shard_map/ppermute | solution.py:19
  41.5 12.1 %collective-permute-start.6 = (bf16[128,1536]{1,0:T(8,128)(2,1)S(1)}, bf16[128,1536]{1,0:T(8,128)(2,1)S(1)}, u32[]{:S(2)}, u32[]{:S(2)}) collective-permute-start(bf16[128,1536]{1,0:T(8,128)(2,1)S(1)} %convolution_convert_fusion.2), channel_id=1, source_target_pairs={{0,2},{1,3},{2,0},{3,1},{4,6},{5,7},{6,4},{7,5},{8,10},{9,11},{10,... | collective-permute-start | bytes 1179656 | tf_op jit(solution)/shard_map/ppermute | solution.py:19
  45.4 20.0 %collective-permute-start.8 = (bf16[128,1536]{1,0:T(8,128)(2,1)}, bf16[128,1536]{1,0:T(8,128)(2,1)}, u32[]{:S(2)}, u32[]{:S(2)}) collective-permute-start(bf16[128,1536]{1,0:T(8,128)(2,1)} %convolution_convert_fusion.1), channel_id=1, source_target_pairs={{0,2},{1,3},{2,0},{3,1},{4,6},{5,7},{6,4},{7,5},{8,10},{9,11},{10,... | collective-permute-start | bytes 1179656 | tf_op jit(solution)/shard_map/ppermute | solution.py:19
  58.4 10.4 %collective-permute-start.9 = (bf16[64,1536]{1,0:T(8,128)(2,1)}, bf16[64,1536]{1,0:T(8,128)(2,1)S(1)}, u32[]{:S(2)}, u32[]{:S(2)}) collective-permute-start(bf16[64,1536]{1,0:T(8,128)(2,1)} %slice.191), channel_id=1, source_target_pairs={{0,4},{1,5},{2,6},{3,7},{4,0},{5,1},{6,2},{7,3},{8,12},{9,13},{10,... | collective-permute-start | bytes 589832 | tf_op jit(solution)/shard_map/ppermute | solution.py:19
  70.2 8.7 %collective-permute-start.10 = (bf16[64,1536]{1,0:T(8,128)(2,1)S(1)}, bf16[64,1536]{1,0:T(8,128)(2,1)S(1)}, u32[]{:S(2)}, u32[]{:S(2)}) collective-permute-start(bf16[64,1536]{1,0:T(8,128)(2,1)S(1)} %slice.190), channel_id=1, source_target_pairs={{0,4},{1,5},{2,6},{3,7},{4,0},{5,1},{6,2},{7,3},{8,12},{9,13},{10,... | collective-permute-start | bytes 589832 | tf_op jit(solution)/shard_map/ppermute | solution.py:19
  70.3 10.7 %collective-permute-start.12 = (bf16[64,1536]{1,0:T(8,128)(2,1)S(1)}, bf16[64,1536]{1,0:T(8,128)(2,1)S(1)}, u32[]{:S(2)}, u32[]{:S(2)}) collective-permute-start(bf16[64,1536]{1,0:T(8,128)(2,1)S(1)} %fusion.78), channel_id=1, source_target_pairs={{0,1},{1,0},{2,3},{3,2},{4,5},{5,4},{6,7},{7,6},{8,9},{9,8},{10,11... | collective-permute-start | bytes 589832 | tf_op jit(solution)/shard_map/ppermute | solution.py:19
  79.0 5.7 %collective-permute-start.11 = (bf16[64,1536]{1,0:T(8,128)(2,1)S(1)}, bf16[64,1536]{1,0:T(8,128)(2,1)S(1)}, u32[]{:S(2)}, u32[]{:S(2)}) collective-permute-start(bf16[64,1536]{1,0:T(8,128)(2,1)S(1)} %fusion.77), channel_id=1, source_target_pairs={{0,1},{1,0},{2,3},{3,2},{4,5},{5,4},{6,7},{7,6},{8,9},{9,8},{10,11... | collective-permute-start | bytes 589832 | tf_op jit(solution)/shard_map/ppermute | solution.py:19
  86.9 16.2 %collective-permute-start.13 = (bf16[24,6144]{1,0:T(8,128)(2,1)}, bf16[24,6144]{1,0:T(8,128)(2,1)S(1)}, u32[]{:S(2)}, u32[]{:S(2)}) collective-permute-start(bf16[24,6144]{1,0:T(8,128)(2,1)} %get-tuple-element.72), channel_id=1, source_target_pairs={{0,4},{1,5},{2,6},{3,7},{4,0},{5,1},{6,2},{7,3},{8,12},{9,13},{10,... | collective-permute-start | bytes 884744 | tf_op jit(solution)/shard_map/ppermute | solution.py:19
  86.9 11.0 %collective-permute-start.14 = (bf16[24,6144]{1,0:T(8,128)(2,1)S(1)}, bf16[24,6144]{1,0:T(8,128)(2,1)S(1)}, u32[]{:S(2)}, u32[]{:S(2)}) collective-permute-start(bf16[24,6144]{1,0:T(8,128)(2,1)S(1)} %get-tuple-element.70), channel_id=1, source_target_pairs={{0,2},{1,3},{2,0},{3,1},{4,6},{5,7},{6,4},{7,5},{8,10},{9,11},{10,... | collective-permute-start | bytes 884744 | tf_op jit(solution)/shard_map/ppermute | solution.py:19
  90.1 14.2 %collective-permute-start.18 = (bf16[24,6144]{1,0:T(8,128)(2,1)S(1)}, bf16[24,6144]{1,0:T(8,128)(2,1)S(1)}, u32[]{:S(2)}, u32[]{:S(2)}) collective-permute-start(bf16[24,6144]{1,0:T(8,128)(2,1)S(1)} %get-tuple-element.51), channel_id=1, source_target_pairs={{0,16},{8,24},{16,0},{24,8},{1,17},{9,25},{17,1},{25,9},{2,18},{10... | collective-permute-start | bytes 884744 | tf_op jit(solution)/shard_map/ppermute | solution.py:19
  97.9 7.0 %collective-permute-start.19 = (bf16[24,6144]{1,0:T(8,128)(2,1)S(1)}, bf16[24,6144]{1,0:T(8,128)(2,1)S(1)}, u32[]{:S(2)}, u32[]{:S(2)}) collective-permute-start(bf16[24,6144]{1,0:T(8,128)(2,1)S(1)} %collective-permute-done.14), channel_id=1, source_target_pairs={{0,16},{8,24},{16,0},{24,8},{1,17},{9,25},{17,1},{25,9},{2,18},{10... | collective-permute-start | bytes 884744 | tf_op jit(solution)/shard_map/ppermute | solution.py:19
  99.0 10.2 %collective-permute-start.15 = (bf16[24,6144]{1,0:T(8,128)(2,1)S(1)}, bf16[24,6144]{1,0:T(8,128)(2,1)S(1)}, u32[]{:S(2)}, u32[]{:S(2)}) collective-permute-start(bf16[24,6144]{1,0:T(8,128)(2,1)S(1)} %get-tuple-element.50), channel_id=1, source_target_pairs={{0,6},{1,7},{2,4},{3,5},{4,2},{5,3},{6,0},{7,1},{8,14},{9,15},{10,... | collective-permute-start | bytes 884744 | tf_op jit(solution)/shard_map/ppermute | solution.py:19
  103.1 30.0 %collective-permute-start.16 = (bf16[24,6144]{1,0:T(8,128)(2,1)S(1)}, bf16[24,6144]{1,0:T(8,128)(2,1)S(1)}, u32[]{:S(2)}, u32[]{:S(2)}) collective-permute-start(bf16[24,6144]{1,0:T(8,128)(2,1)S(1)} %collective-permute-done.13), channel_id=1, source_target_pairs={{0,16},{8,24},{16,0},{24,8},{1,17},{9,25},{17,1},{25,9},{2,18},{10... | collective-permute-start | bytes 884744 | tf_op jit(solution)/shard_map/ppermute | solution.py:19
  105.1 5.4 %collective-permute-start.20 = (bf16[96,6144]{1,0:T(8,128)(2,1)S(1)}, bf16[96,6144]{1,0:T(8,128)(2,1)S(1)}, u32[]{:S(2)}, u32[]{:S(2)}) collective-permute-start(bf16[96,6144]{1,0:T(8,128)(2,1)S(1)} %pad_maximum_fusion.1), channel_id=1, source_target_pairs={{0,8},{8,0},{16,24},{24,16},{1,9},{9,1},{17,25},{25,17},{2,10},{10... | collective-permute-start | bytes 3538952 | tf_op jit(solution)/shard_map/ppermute | solution.py:19
  109.2 23.9 %collective-permute-start.17 = (bf16[24,6144]{1,0:T(8,128)(2,1)S(1)}, bf16[24,6144]{1,0:T(8,128)(2,1)S(1)}, u32[]{:S(2)}, u32[]{:S(2)}) collective-permute-start(bf16[24,6144]{1,0:T(8,128)(2,1)S(1)} %collective-permute-done.15), channel_id=1, source_target_pairs={{0,16},{8,24},{16,0},{24,8},{1,17},{9,25},{17,1},{25,9},{2,18},{10... | collective-permute-start | bytes 884744 | tf_op jit(solution)/shard_map/ppermute | solution.py:19
  133.3 13.3 %collective-permute-start.23 = (bf16[96,6144]{1,0:T(8,128)(2,1)S(1)}, bf16[96,6144]{1,0:T(8,128)(2,1)S(1)}, u32[]{:S(2)}, u32[]{:S(2)}) collective-permute-start(bf16[96,6144]{1,0:T(8,128)(2,1)S(1)} %slice.129), channel_id=1, source_target_pairs={{0,8},{8,0},{16,24},{24,16},{1,9},{9,1},{17,25},{25,17},{2,10},{10... | collective-permute-start | bytes 3538952 | tf_op jit(solution)/shard_map/ppermute | solution.py:19
  146.9 9.1 %collective-permute-start.24 = (bf16[24,6144]{1,0:T(8,128)(2,1)S(1)}, bf16[24,6144]{1,0:T(8,128)(2,1)S(1)}, u32[]{:S(2)}, u32[]{:S(2)}) collective-permute-start(bf16[24,6144]{1,0:T(8,128)(2,1)S(1)} %slice.189), channel_id=1, source_target_pairs={{0,16},{8,24},{16,0},{24,8},{1,17},{9,25},{17,1},{25,9},{2,18},{10... | collective-permute-start | bytes 884744 | tf_op jit(solution)/shard_map/ppermute | solution.py:19
  151.8 4.3 %collective-permute-start.22 = (bf16[96,6144]{1,0:T(8,128)(2,1)S(1)}, bf16[96,6144]{1,0:T(8,128)(2,1)S(1)}, u32[]{:S(2)}, u32[]{:S(2)}) collective-permute-start(bf16[96,6144]{1,0:T(8,128)(2,1)S(1)} %slice.127), channel_id=1, source_target_pairs={{0,8},{8,0},{16,24},{24,16},{1,9},{9,1},{17,25},{25,17},{2,10},{10... | collective-permute-start | bytes 3538952 | tf_op jit(solution)/shard_map/ppermute | solution.py:19
  156.4 8.3 %collective-permute-start.25 = (bf16[24,6144]{1,0:T(8,128)(2,1)S(1)}, bf16[24,6144]{1,0:T(8,128)(2,1)S(1)}, u32[]{:S(2)}, u32[]{:S(2)}) collective-permute-start(bf16[24,6144]{1,0:T(8,128)(2,1)S(1)} %slice.188), channel_id=1, source_target_pairs={{0,16},{8,24},{16,0},{24,8},{1,17},{9,25},{17,1},{25,9},{2,18},{10... | collective-permute-start | bytes 884744 | tf_op jit(solution)/shard_map/ppermute | solution.py:19
  164.8 9.9 %collective-permute-start.30 = (bf16[24,6144]{1,0:T(8,128)(2,1)S(1)}, bf16[24,6144]{1,0:T(8,128)(2,1)S(1)}, u32[]{:S(2)}, u32[]{:S(2)}) collective-permute-start(bf16[24,6144]{1,0:T(8,128)(2,1)S(1)} %slice.186), channel_id=1, source_target_pairs={{0,16},{8,24},{16,0},{24,8},{1,17},{9,25},{17,1},{25,9},{2,18},{10... | collective-permute-start | bytes 884744 | tf_op jit(solution)/shard_map/ppermute | solution.py:19
  165.9 15.2 %collective-permute-start.27 = (bf16[24,6144]{1,0:T(8,128)(2,1)S(1)}, bf16[24,6144]{1,0:T(8,128)(2,1)S(1)}, u32[]{:S(2)}, u32[]{:S(2)}) collective-permute-start(bf16[24,6144]{1,0:T(8,128)(2,1)S(1)} %fusion.33), channel_id=1, source_target_pairs={{0,2},{1,3},{2,0},{3,1},{4,6},{5,7},{6,4},{7,5},{8,10},{9,11},{10,... | collective-permute-start | bytes 884744 | tf_op jit(solution)/shard_map/ppermute | solution.py:19
  170.8 17.0 %collective-permute-start.28 = (bf16[24,6144]{1,0:T(8,128)(2,1)S(1)}, bf16[24,6144]{1,0:T(8,128)(2,1)S(1)}, u32[]{:S(2)}, u32[]{:S(2)}) collective-permute-start(bf16[24,6144]{1,0:T(8,128)(2,1)S(1)} %add_convert_fusion.2), channel_id=1, source_target_pairs={{0,6},{1,7},{2,4},{3,5},{4,2},{5,3},{6,0},{7,1},{8,14},{9,15},{10,... | collective-permute-start | bytes 884744 | tf_op jit(solution)/shard_map/ppermute | solution.py:19
  173.5 7.5 %collective-permute-start.26 = (bf16[24,6144]{1,0:T(8,128)(2,1)S(1)}, bf16[24,6144]{1,0:T(8,128)(2,1)S(1)}, u32[]{:S(2)}, u32[]{:S(2)}) collective-permute-start(bf16[24,6144]{1,0:T(8,128)(2,1)S(1)} %slice.187), channel_id=1, source_target_pairs={{0,16},{8,24},{16,0},{24,8},{1,17},{9,25},{17,1},{25,9},{2,18},{10... | collective-permute-start | bytes 884744 | tf_op jit(solution)/shard_map/ppermute | solution.py:19
  174.8 21.5 %collective-permute-start.31 = (bf16[24,6144]{1,0:T(8,128)(2,1)S(1)}, bf16[24,6144]{1,0:T(8,128)(2,1)S(1)}, u32[]{:S(2)}, u32[]{:S(2)}) collective-permute-start(bf16[24,6144]{1,0:T(8,128)(2,1)S(1)} %add_convert_fusion), channel_id=1, source_target_pairs={{0,4},{1,5},{2,6},{3,7},{4,0},{5,1},{6,2},{7,3},{8,12},{9,13},{10,... | collective-permute-start | bytes 884744 | tf_op jit(solution)/shard_map/ppermute | solution.py:19
  188.6 13.9 %collective-permute-start.29 = (bf16[32,6144]{1,0:T(8,128)(2,1)S(1)}, bf16[32,6144]{1,0:T(8,128)(2,1)S(1)}, u32[]{:S(2)}, u32[]{:S(2)}) collective-permute-start(bf16[32,6144]{1,0:T(8,128)(2,1)S(1)} %fusion.40), channel_id=1, source_target_pairs={{0,1},{1,0},{2,3},{3,2},{4,5},{5,4},{6,7},{7,6},{8,9},{9,8},{10,11... | collective-permute-start | bytes 1179656 | tf_op jit(solution)/shard_map/ppermute | solution.py:19
  196.4 5.7 %collective-permute-start.32 = (bf16[12,6144]{1,0:T(8,128)(2,1)S(1)}, bf16[12,6144]{1,0:T(8,128)(2,1)S(1)}, u32[]{:S(2)}, u32[]{:S(2)}) collective-permute-start(bf16[12,6144]{1,0:T(8,128)(2,1)S(1)} %constant_dynamic-slice_fusion), channel_id=1, source_target_pairs={{0,1},{1,0},{2,3},{3,2},{4,5},{5,4},{6,7},{7,6},{8,9},{9,8},{10,11... | collective-permute-start | bytes 442376 | tf_op jit(solution)/shard_map/ppermute | solution.py:19
  (25 other events, 310.9 us)
